TPU v7x, 32 devices: a whole 2x2x4 slice. The times are simulated.
32 devices in a mesh: row: 4 (over y, core), col: 8 (over z, x).
Axes of the slice: x: 2, y: 2, z: 4, core: 2. Of those that a mesh axis runs over, the one named last changes fastest.
Arguments:
- start_vecs: bfloat16 [32, 1, 4, 8, 512], P(None, None, 'row', 'col'), may hold values from -6 to 6
- blocks: bfloat16 [4, 8, 6, 512, 512], P('row', 'col'), may hold values from -0.125 to 0.125
- block_rows: int32 [4, 8, 6], P('row', 'col'), may hold values from 0 to 3, as said below
- block_cols: int32 [4, 8, 6], P('row', 'col'), may hold values from 0 to 7, as said below
- block_count: int32 [4, 8], P('row', 'col'), may hold values from 3 to 6, as said below
Outputs:
- filtered_one: bfloat16 [32, 1, 4, 8, 512], P(None, None, 'row', 'col')
- filtered_two: bfloat16 [32, 1, 4, 8, 512], P(None, None, 'row', 'col')
Inputs may be any that keep to these rules, and one draw needn't show every extreme that they name: `block_rows`: on device (a, b) a slot with value i has block row I = (i // 4) * 4 * 8 + (i % 4) * 8 + b, and I <= J for the slot's block column J; a pair (I, J) may repeat. `block_cols`: on device (a, b) a slot with value j has block column J = (j // 8) * 4 * 8 + a * 8 + j % 8. The used slots are the first block_count[a, b] of each device; the others are ignored; some device uses all 6.
All inputs are finite; a program needn't handle non-finite values.
Results may differ from a plain program's by a relative error of at most 0.015.
Values may be sent and summed in bfloat16 or wider, within the bound.
No kernel may reach another device: no remote copies, remote signals or barrier semaphores. Data moves between devices by JAX's collectives and lax.ppermute only.
A program may use at most 64 MiB of HBM per device.

v0:
```python
import jax
import jax.numpy as jnp
from jax import lax
from jax.sharding import PartitionSpec as P

STEPS = 2


shift_center = 0.5
half_width = 2.0


def settle(values):
    return lax.optimization_barrier(values.astype(jnp.bfloat16)).astype(jnp.float32)


def add_block(running, index_at, product):
    before = lax.dynamic_index_in_dim(running, index_at, 1, keepdims=False)
    return lax.dynamic_update_index_in_dim(running, before + product, index_at, 1)


def owner_product(block_tile, mirror_vecs, col_at):
    source = lax.dynamic_index_in_dim(mirror_vecs, col_at, 1, keepdims=False)
    return lax.dot_general(
        source, block_tile, (((1,), (1,)), ((), ())), preferred_element_type=jnp.float32
    )


def mirror_product(block_tile, owner_vecs, row_at):
    source = lax.dynamic_index_in_dim(owner_vecs, row_at, 1, keepdims=False)
    return jnp.dot(source, block_tile, preferred_element_type=jnp.float32)


def joint_loop(tiles_here, row_list, col_list, live_count, owner_vecs, mirror_vecs):

    def slot_step(slot_at, partials):
        direct, mirror = partials
        block_tile = lax.dynamic_index_in_dim(tiles_here, slot_at, 0, keepdims=False)
        row_at = row_list[slot_at]
        col_at = col_list[slot_at]
        direct = add_block(direct, row_at, owner_product(block_tile, mirror_vecs, col_at))
        mirror = add_block(mirror, col_at, mirror_product(block_tile, owner_vecs, row_at))
        return (direct, mirror)

    initial = (jnp.zeros(owner_vecs.shape, jnp.float32), jnp.zeros(mirror_vecs.shape, jnp.float32))
    return lax.fori_loop(0, live_count, slot_step, initial)


def advance(applied, current, previous, section_at):
    shifted = (applied - shift_center * current.astype(jnp.float32)) / half_width
    if section_at > 0:
        shifted = 2.0 * shifted - previous.astype(jnp.float32)
    return shifted.astype(jnp.bfloat16)


def body(start_vecs, blocks, block_rows, block_cols, block_count):
    tiles_here = blocks[0, 0]
    row_list = block_rows[0, 0]
    col_list = block_cols[0, 0]
    live_count = block_count[0, 0]
    vec_count = start_vecs.shape[0]
    local_blocks = start_vecs.shape[1]
    block_width = start_vecs.shape[4]
    row_devices = lax.axis_size("row")
    col_devices = lax.axis_size("col")
    previous = start_vecs
    current = start_vecs
    first_result = start_vecs
    for section_at in range(STEPS):
        owner_panel = lax.all_gather(current, "row", axis=2, tiled=True)
        mirror_panel = lax.all_gather(current, "col", axis=3, tiled=True)
        owner_vecs = owner_panel.reshape(vec_count, local_blocks * row_devices, block_width)
        mirror_vecs = mirror_panel.reshape(vec_count, local_blocks * col_devices, block_width)
        direct, mirror = joint_loop(
            tiles_here, row_list, col_list, live_count, owner_vecs, mirror_vecs
        )
        direct_terms = settle(direct).reshape(vec_count, local_blocks, row_devices, 1, block_width)
        direct_own = lax.psum_scatter(
            direct_terms.astype(jnp.bfloat16), "row", scatter_dimension=2, tiled=True
        ).astype(jnp.float32)
        mirror_terms = settle(mirror).reshape(vec_count, local_blocks, 1, col_devices, block_width)
        mirror_own = lax.psum_scatter(
            mirror_terms.astype(jnp.bfloat16), "col", scatter_dimension=3, tiled=True
        ).astype(jnp.float32)
        updated = advance(direct_own + mirror_own, current, previous, section_at)
        if section_at == 0:
            first_result = updated
        previous = current
        current = updated
    return (first_result, current)


def solution(mesh):
    return jax.shard_map(
        body,
        mesh=mesh,
        in_specs=(
            P(None, None, "row", "col", None),
            P("row", "col", None, None, None),
            P("row", "col", None),
            P("row", "col", None),
            P("row", "col"),
        ),
        out_specs=(P(None, None, "row", "col", None), P(None, None, "row", "col", None)),
        check_vma=False,
    )
```

profile of v0, /device:TPU:0, one launch (start us, length us, event | category | flops | bytes accessed | tf_op | source)
XLA Modules:
  0.0 380.5 jit_solution(1223088602546984760)
XLA Ops:
  7.2 0.0 reduce-scatter.5.cloned.1.call-start
  7.2 32.7 %all_gather.12 = bf16[32,1,1,8,512]{4,0,2,1,3:T(8,128)(2,1)S(1)} all-gather(bf16[32,1,1,1,512]{4,0,2,1,3:T(8,128)(2,1)} %bitcast.120), channel_id=1, replica_groups=mesh['row'=4,'col'=8] {'col'}, dimensions={3}, use_global_device_ids=true | all-gather | bytes 294912 | tf_op jit(solution)/shard_map/all_gather | solution.py:71
  39.9 5.6 %all_gather.13 = bf16[32,1,4,1,512]{4,0,3,1,2:T(8,128)(2,1)S(1)} all-gather(bf16[32,1,1,1,512]{4,0,3,1,2:T(8,128)(2,1)} %bitcast.121), channel_id=1, replica_groups=mesh['row'=4,'col'=8] {'row'}, dimensions={2}, use_global_device_ids=true | all-gather | bytes 163840 | tf_op jit(solution)/shard_map/all_gather | solution.py:70
  45.7 0.0 copy-start
  45.7 39.2 %while.24 = (s32[]{:T(128)}, f32[32,4,512]{2,0,1:T(8,128)S(1)}, f32[32,8,512]{2,0,1:T(8,128)S(1)}, s32[]{:T(128)}, s32[6]{0:T(128)}, /*index=5*/s32[6]{0:T(128)}...) while((s32[]{:T(128)}, f32[32,4,512]{2,0,1:T(8,128)S(1)}, ...), condition=%wide.region_1.2_spmd, body=%wide.region_0.1_spmd.sunk | while | flops 33587208 | bytes 1638691 | solution.py:46
  46.3 1.2 dynamic_slice.103
  49.5 1.2 dynamic_slice.102
  52.7 1.2 fusion.50
  54.0 1.3 fusion.49
  56.0 1.2 dynamic_slice.103
  59.2 1.2 dynamic_slice.102
  62.4 1.2 fusion.50
  63.6 1.3 fusion.49
  65.6 1.2 dynamic_slice.103
  68.8 1.2 dynamic_slice.102
  72.0 1.2 fusion.50
  73.2 1.3 fusion.49
  75.2 1.2 dynamic_slice.103
  78.4 1.2 dynamic_slice.102
  81.6 1.2 fusion.50
  82.9 1.3 fusion.49
  84.8 0.7 convert_element_type.57
  85.5 0.0 reduce-scatter.5.cloned.1.call-update
  85.5 0.0 reduce-scatter.7.cloned.1.call-start
  85.6 0.7 convert_element_type.60
  86.3 0.0 reduce-scatter.7.cloned.1.call-update
  86.3 0.0 reduce-scatter.9.cloned.1.call-start
  86.4 39.1 %reduce-scatter.5.cloned.1.call-done = bf16[32,1,1,1,512]{4,0,2,1,3:T(8,128)(2,1)} async-done(((bf16[32,1,4,1,512]{4,0,2,1,3:T(8,128)(2,1)}), bf16[32,1,1,1,512]{4,0,2,1,3:T(8,128)(2,1)}) %reduce-scatter.5.cloned.1.call-update) | async-done | bytes 32784 | tf_op jit(solution)/shard_map/reduce_scatter | solution.py:78
  125.5 65.0 %reduce-scatter.7.cloned.1.call-done = bf16[32,1,1,1,512]{4,0,2,1,3:T(8,128)(2,1)} async-done(((bf16[32,1,1,8,512]{4,0,2,1,3:T(8,128)(2,1)}), bf16[32,1,1,1,512]{4,0,2,1,3:T(8,128)(2,1)}) %reduce-scatter.7.cloned.1.call-update) | async-done | bytes 32784 | tf_op jit(solution)/shard_map/reduce_scatter | solution.py:82
  190.4 0.0 copy-done
  190.4 0.8 fusion.30
  191.2 0.0 copy-start.1
  191.2 30.9 %all_gather.14 = bf16[32,1,1,8,512]{4,0,2,1,3:T(8,128)(2,1)S(1)} all-gather(bf16[32,1,1,1,512]{4,0,2,1,3:T(8,128)(2,1)S(1)} %fusion.30), channel_id=1, replica_groups=mesh['row'=4,'col'=8] {'col'}, dimensions={3}, use_global_device_ids=true | all-gather | bytes 294912 | tf_op jit(solution)/shard_map/all_gather | solution.py:71
  222.1 5.4 %all_gather.15 = bf16[32,1,4,1,512]{4,0,3,1,2:T(8,128)(2,1)S(1)} all-gather(bf16[32,1,1,1,512]{4,0,3,1,2:T(8,128)(2,1)S(1)} %bitcast.122), channel_id=1, replica_groups=mesh['row'=4,'col'=8] {'row'}, dimensions={2}, use_global_device_ids=true | all-gather | bytes 163840 | tf_op jit(solution)/shard_map/all_gather | solution.py:70
  227.6 40.8 %while.25 = (s32[]{:T(128)}, f32[32,4,512]{2,0,1:T(8,128)S(1)}, f32[32,8,512]{2,0,1:T(8,128)S(1)}, s32[]{:T(128)}, s32[6]{0:T(128)}, /*index=5*/s32[6]{0:T(128)}...) while((s32[]{:T(128)}, f32[32,4,512]{2,0,1:T(8,128)S(1)}, ...), condition=%wide.region_5.6_spmd, body=%wide.region_4.5_spmd.sunk | while | flops 33587208 | bytes 1638691 | solution.py:46
  228.3 1.3 dynamic_slice.110
  231.7 1.3 dynamic_slice.109
  235.1 1.2 fusion.56
  236.4 1.3 fusion.55
  238.3 1.3 dynamic_slice.110
  241.7 1.3 dynamic_slice.109
  245.2 1.2 fusion.56
  246.4 1.3 fusion.55
  248.4 1.3 dynamic_slice.110
  251.8 1.3 dynamic_slice.109
  255.2 1.2 fusion.56
  256.5 1.3 fusion.55
  258.4 1.3 dynamic_slice.110
  261.8 1.3 dynamic_slice.109
  265.3 1.2 fusion.56
  266.5 1.3 fusion.55
  268.5 0.7 convert_element_type.65
  269.1 0.0 reduce-scatter.9.cloned.1.call-update
  269.2 0.0 reduce-scatter.11.cloned.1.call-start
  269.2 0.7 convert_element_type.68
  270.0 0.0 reduce-scatter.11.cloned.1.call-update
  270.0 38.1 %reduce-scatter.9.cloned.1.call-done = bf16[32,1,1,1,512]{4,0,2,1,3:T(8,128)(2,1)} async-done(((bf16[32,1,4,1,512]{4,0,2,1,3:T(8,128)(2,1)}), bf16[32,1,1,1,512]{4,0,2,1,3:T(8,128)(2,1)}) %reduce-scatter.9.cloned.1.call-update) | async-done | bytes 32784 | tf_op jit(solution)/shard_map/reduce_scatter | solution.py:78
  308.0 64.5 %reduce-scatter.11.cloned.1.call-done = bf16[32,1,1,1,512]{4,0,2,1,3:T(8,128)(2,1)} async-done(((bf16[32,1,1,8,512]{4,0,2,1,3:T(8,128)(2,1)}), bf16[32,1,1,1,512]{4,0,2,1,3:T(8,128)(2,1)}) %reduce-scatter.11.cloned.1.call-update) | async-done | bytes 32784 | tf_op jit(solution)/shard_map/reduce_scatter | solution.py:82
  372.5 0.0 copy-done.1
  372.5 1.4 fusion.32
  (12 shorter events, 0.3 us)
Async XLA Ops:
  7.2 118.3 %reduce-scatter.5.cloned.1.call-start = ((), (), s32[]{:S(2)}) async-start(), calls=%async_computation.4 | async-start | bytes 163840 | tf_op jit(solution)/shard_map/reduce_scatter | solution.py:78
  45.7 144.8 %copy-start = (bf16[32,1,1,1,512]{4,0,3,2,1:T(8,128)(2,1)S(1)}, bf16[32,1,1,1,512]{4,0,3,2,1:T(8,128)(2,1)}, u32[]{:S(2)}) copy-start(bf16[32,1,1,1,512]{4,0,3,2,1:T(8,128)(2,1)} %param.9) | copy-start | bytes 98308
  85.5 104.9 %reduce-scatter.7.cloned.1.call-start = ((), (), s32[]{:S(2)}) async-start(), calls=%async_computation.5 | async-start | bytes 294912 | tf_op jit(solution)/shard_map/reduce_scatter | solution.py:82
  86.3 221.7 %reduce-scatter.9.cloned.1.call-start = ((), (), s32[]{:S(2)}) async-start(), calls=%async_computation.6 | async-start | bytes 163840 | tf_op jit(solution)/shard_map/reduce_scatter | solution.py:78
  191.2 181.3 %copy-start.1 = (bf16[32,1,1,1,512]{4,0,2,1,3:T(8,128)(2,1)}, bf16[32,1,1,1,512]{4,0,2,1,3:T(8,128)(2,1)S(1)}, u32[]{:S(2)}) copy-start(bf16[32,1,1,1,512]{4,0,2,1,3:T(8,128)(2,1)S(1)} %fusion.30) | copy-start | bytes 98308
  269.2 103.3 %reduce-scatter.11.cloned.1.call-start = ((), (), s32[]{:S(2)}) async-start(), calls=%async_computation.7 | async-start | bytes 294912 | tf_op jit(solution)/shard_map/reduce_scatter | solution.py:82
Sparse Core Ops, SparseCore 0:
  85.6 39.7 reduce-scatter.4
  129.1 61.2 reduce-scatter.6
  269.3 38.7 reduce-scatter.8
  311.2 61.2 reduce-scatter.10
where the time goes:
time: 380 us
  waiting for transfers between devices  207 us (54%)
  blocking collectives  74.7 us (20%)
  loops' own time  39 us (10%)
  local copies, waits for them, and re-layouts  20.8 us (5%)
  matrix products  20.3 us (5%)
  between operations  13.8 us (4%)
  other arithmetic  5.01 us (1%)
    reduce_scatter x2, waiting for transfers between devices, body(): lax.psum_scatter(mirror_terms.astype(jnp.bfloat16), 'col', scatter_dimens...  129 us
    reduce_scatter x2, waiting for transfers between devices, body(): lax.psum_scatter(direct_terms.astype(jnp.bfloat16), 'row', scatter_dimens...  77.1 us
    all_gather x2, blocking collectives, body(): mirror_panel = lax.all_gather(current, 'col', axis=3, tiled=True)  63.6 us
    another operation x2, loops' own time, joint_loop(): return lax.fori_loop(0, live_count, slot_step, initial)  39 us
    all_gather x2, blocking collectives, body(): owner_panel = lax.all_gather(current, 'row', axis=2, tiled=True)  11 us
    dot_general x8, matrix products, owner_product(): lax.dot_general(source, block_tile, (((1,), (1,)), ((), ())), preferred_e...  10.4 us
    dynamic_slice x8, local copies, waits for them, and re-layouts, slot_step(): row_at = row_list[slot_at]  10.3 us
    dynamic_slice x8, local copies, waits for them, and re-layouts, slot_step(): col_at = col_list[slot_at]  10.3 us
  transfers between devices with their start and end apart: 4, of which 4 were waited for; matrix products, arithmetic and copies ran while one was open for 0% of the time, Pallas kernels for 0%

commit v1 on v0

v1 whole, which is shorter than its diff:
```python
import jax
import jax.numpy as jnp
from jax import lax
from jax.experimental import pallas as pl
from jax.experimental.pallas import tpu as pltpu
from jax.sharding import PartitionSpec as P

shift_center = 0.5
half_width = 2.0

VMEM = pl.BlockSpec(memory_space=pltpu.VMEM)
SMEM = pl.BlockSpec(memory_space=pltpu.SMEM)
PARAMS = pltpu.CompilerParams(vmem_limit_bytes=16 * 1024 * 1024)
f32 = jnp.float32
bf16 = jnp.bfloat16


def swap(value, axes, pattern):
    if isinstance(axes, str):
        pairs = [(i, i ^ pattern) for i in range(lax.axis_size(axes))]
    else:
        n_first, n_second = (lax.axis_size(a) for a in axes)
        pairs = [
            (i * n_second + j, (i ^ pattern[0]) * n_second + (j ^ pattern[1]))
            for i in range(n_first)
            for j in range(n_second)
        ]
    return lax.ppermute(value, axes, pairs)


def spread(values, axis):
    pair = jnp.concatenate(values, axis=0)
    return [pair] + [swap(pair, axis, s << 1) for s in range(1, lax.axis_size(axis) // 2)]


def slot_products(meta, tiles, row_pairs, col_pairs):
    slots, width = tiles.shape[0], tiles.shape[1]
    n_vec = row_pairs[0].shape[0] // 2
    n_row, n_col = len(row_pairs), len(col_pairs)

    def kernel(meta_ref, tiles_ref, *refs):
        row_in, refs = refs[:n_row], refs[n_row:]
        col_in, refs = refs[:n_col], refs[n_col:]
        row_out, refs = refs[:n_row], refs[n_row:]
        col_out, refs = refs[:n_col], refs[n_col:]
        row_vecs, col_vecs, direct, mirror = refs
        for source, panel in ((row_in, row_vecs), (col_in, col_vecs)):
            for k, ref in enumerate(source):
                for half in range(2):
                    panel[2 * k + half] = ref[half * n_vec : (half + 1) * n_vec, :]
        direct[...] = jnp.zeros(direct.shape, f32)
        mirror[...] = jnp.zeros(mirror.shape, f32)
        count = meta_ref[2 * slots]
        for s in range(slots):
            used = s < count
            r = meta_ref[s]
            c = meta_ref[slots + s]
            tile = tiles_ref[s]
            source = jnp.where(used, col_vecs[c], jnp.zeros((), bf16))
            owner = lax.dot_general(source, tile, (((1,), (1,)), ((), ())), preferred_element_type=f32)
            source = jnp.where(used, row_vecs[r], jnp.zeros((), bf16))
            other = jnp.dot(source, tile, preferred_element_type=f32)
            direct[r] += owner
            mirror[c] += other
        for total, outs in ((direct, row_out), (mirror, col_out)):
            for k, ref in enumerate(outs):
                for half in range(2):
                    ref[half * n_vec : (half + 1) * n_vec, :] = total[2 * k + half].astype(ref.dtype)

    def outs(n):
        return [jax.ShapeDtypeStruct((2 * n_vec, width), f32 if k == 0 else bf16) for k in range(n)]

    done = pl.pallas_call(
        kernel,
        out_shape=outs(n_row) + outs(n_col),
        in_specs=[SMEM, VMEM] + [VMEM] * (n_row + n_col),
        out_specs=[VMEM] * (n_row + n_col),
        scratch_shapes=[
            pltpu.VMEM((2 * n_row, n_vec, width), bf16),
            pltpu.VMEM((2 * n_col, n_vec, width), bf16),
            pltpu.VMEM((2 * n_row, n_vec, width), f32),
            pltpu.VMEM((2 * n_col, n_vec, width), f32),
        ],
        compiler_params=PARAMS,
        cost_estimate=pl.CostEstimate(
            flops=slots * 4 * n_vec * width * width, bytes_accessed=slots * width * width * 2, transcendentals=0
        ),
    )(meta, tiles, *row_pairs, *col_pairs)
    return done[:n_row], done[n_row:]


def local_call(kernel, shapes, *operands):
    return pl.pallas_call(
        kernel,
        out_shape=[jax.ShapeDtypeStruct(s, d) for s, d in shapes],
        in_specs=[VMEM] * len(operands),
        out_specs=[VMEM] * len(shapes),
        compiler_params=PARAMS,
    )(*operands)


def scatter_high(terms, axis):
    return [swap(t, axis, s << 1) for s, t in enumerate(terms) if s > 0]


def total_of(kept, received, half, n_vec):
    rows = slice(half * n_vec, (half + 1) * n_vec)
    total = kept[rows, :]
    for ref in received:
        total = total + ref[rows, :].astype(f32)
    return total


def body(start_vecs, blocks, block_rows, block_cols, block_count):
    n_vec, width = start_vecs.shape[0], start_vecs.shape[4]
    tiles = blocks[0, 0]
    slots = tiles.shape[0]
    row_at, col_at = lax.axis_index("row"), lax.axis_index("col")
    count = block_count[0, 0]
    live = jnp.arange(slots, dtype=jnp.int32) < count
    meta = jnp.concatenate(
        [
            jnp.where(live, block_rows[0, 0] ^ row_at, 0),
            jnp.where(live, block_cols[0, 0] ^ col_at, 0),
            count[None],
        ]
    )
    current = start_vecs.reshape(n_vec, width)
    one, two = (n_vec, width), (2 * n_vec, width)

    by_x = swap(current, "col", 1)
    by_core = swap(current, "row", 1)
    row_pairs = spread([current, by_core], "row")
    col_pairs = spread([current, by_x], "col")

    direct, mirror = slot_products(meta, tiles, row_pairs, col_pairs)
    direct_in = scatter_high(direct, "row")
    mirror_in = scatter_high(mirror, "col")
    n_d, n_m = len(direct_in), len(mirror_in)

    def partial_sums(d_ref, m_ref, *refs):
        d_in, m_in, outs = refs[:n_d], refs[n_d : n_d + n_m], refs[n_d + n_m :]
        d_keep, m_keep, to_core, to_x, to_diag = outs
        d = [total_of(d_ref, d_in, half, n_vec) for half in range(2)]
        m = [total_of(m_ref, m_in, half, n_vec) for half in range(2)]
        both = (d[0] + m[0]).astype(bf16)
        low, high = slice(0, n_vec), slice(n_vec, 2 * n_vec)
        for half, rows in enumerate((low, high)):
            d_keep[rows, :] = d[half]
            m_keep[rows, :] = m[half]
        d_1, m_1 = d[1].astype(bf16), m[1].astype(bf16)
        to_core[low, :] = d_1
        to_core[high, :] = both
        to_x[low, :] = m_1
        to_x[high, :] = both
        to_diag[low, :] = d_1
        to_diag[high, :] = m_1

    d_keep, m_keep, to_core, to_x, to_diag = local_call(
        partial_sums,
        [(two, f32), (two, f32), (two, bf16), (two, bf16), (two, bf16)],
        direct[0], mirror[0], *direct_in, *mirror_in,
    )
    from_x = swap(to_x, "col", 1)
    from_diag = swap(to_diag, ("row", "col"), (1, 1))
    from_core = swap(to_core, "row", 1)

    def first_update(d_ref, m_ref, core_ref, x_ref, diag_ref, cur_ref, cur_core, cur_x, own_out, row_out, col_out):
        low, high = slice(0, n_vec), slice(n_vec, 2 * n_vec)

        def get(ref, rows):
            return ref[rows, :].astype(f32)

        def advance(applied, ref):
            shifted = (applied - shift_center * ref[...].astype(f32)) / half_width
            return shifted.astype(bf16)

        own = d_ref[low, :] + m_ref[low, :] + get(core_ref, low) + get(x_ref, low)
        core = d_ref[high, :] + get(core_ref, high) + get(diag_ref, high)
        across = m_ref[high, :] + get(x_ref, high) + get(diag_ref, low)
        own = advance(own, cur_ref)
        own_out[...] = own
        row_out[low, :] = own
        col_out[low, :] = own
        row_out[high, :] = advance(core, cur_core)
        col_out[high, :] = advance(across, cur_x)

    first, row_pair, col_pair = local_call(
        first_update,
        [(one, bf16), (two, bf16), (two, bf16)],
        d_keep, m_keep, from_core, from_x, from_diag, current, by_core, by_x,
    )
    row_pairs = [row_pair] + [swap(row_pair, "row", s << 1) for s in range(1, lax.axis_size("row") // 2)]
    col_pairs = [col_pair] + [swap(col_pair, "col", s << 1) for s in range(1, lax.axis_size("col") // 2)]

    direct, mirror = slot_products(meta, tiles, row_pairs, col_pairs)
    direct_in = scatter_high(direct, "row")
    mirror_in = scatter_high(mirror, "col")

    def last_sums(d_ref, m_ref, *refs):
        d_in, m_in, outs = refs[:n_d], refs[n_d : n_d + n_m], refs[n_d + n_m :]
        keep, to_core, to_x = outs
        keep[...] = total_of(d_ref, d_in, 0, n_vec) + total_of(m_ref, m_in, 0, n_vec)
        to_core[...] = total_of(d_ref, d_in, 1, n_vec).astype(bf16)
        to_x[...] = total_of(m_ref, m_in, 1, n_vec).astype(bf16)

    keep, to_core, to_x = local_call(
        last_sums,
        [(one, f32), (one, bf16), (one, bf16)],
        direct[0], mirror[0], *direct_in, *mirror_in,
    )
    from_x = swap(to_x, "col", 1)
    from_core = swap(to_core, "row", 1)

    def last_update(keep_ref, core_ref, x_ref, cur_ref, prev_ref, out_ref):
        applied = keep_ref[...] + core_ref[...].astype(f32) + x_ref[...].astype(f32)
        shifted = (applied - shift_center * cur_ref[...].astype(f32)) / half_width
        shifted = 2.0 * shifted - prev_ref[...].astype(f32)
        out_ref[...] = shifted.astype(bf16)

    (second,) = local_call(last_update, [(one, bf16)], keep, from_core, from_x, first, current)
    shape = start_vecs.shape
    return first.reshape(shape), second.reshape(shape)


def solution(mesh):
    return jax.shard_map(
        body,
        mesh=mesh,
        in_specs=(
            P(None, None, "row", "col", None),
            P("row", "col", None, None, None),
            P("row", "col", None),
            P("row", "col", None),
            P("row", "col"),
        ),
        out_specs=(P(None, None, "row", "col", None), P(None, None, "row", "col", None)),
        check_vma=False,
    )
```

time: 380 us -> 63.5 us (0.17)
  waiting for transfers between devices: 207 us -> 23 us
  blocking collectives: 74.7 us -> 0 us
  loops' own time: 39 us -> 0 us
  starting transfers between devices: 0.16 us -> 29.8 us
  matrix products: 20.3 us -> 0 us
  local copies, waits for them, and re-layouts: 20.8 us -> 1.9 us
  between operations: 13.8 us -> 1.36 us
  Pallas kernels: 0 us -> 5.66 us
    reduce_scatter x4 -> x0, waiting for transfers between devices: 207 us -> none  [the longest x2 129 us: body(): lax.psum_scatter(mirror_terms.astype(jnp.bfloat16), 'col', scatter_dimens...]
    all_gather x4 -> x0, blocking collectives: 74.7 us -> none  [the longest x2 63.6 us: body(): mirror_panel = lax.all_gather(current, 'col', axis=3, tiled=True)]
    another operation x2 -> x0, loops' own time: 39 us -> none  [joint_loop(): return lax.fori_loop(0, live_count, slot_step, initial)]
    ppermute x0 -> x23, starting transfers between devices: none -> 29.8 us  [swap(): return lax.ppermute(value, axes, pairs)]
    ppermute x0 -> x23, waiting for transfers between devices: none -> 23 us  [swap(): return lax.ppermute(value, axes, pairs)]
    dynamic_slice x24 -> x0, local copies, waits for them, and re-layouts: 20.7 us -> none  [the longest x8 10.3 us: slot_step(): row_at = row_list[slot_at]]
    dot_general x16 -> x0, matrix products: 20.3 us -> none  [the longest x8 10.4 us: owner_product(): lax.dot_general(source, block_tile, (((1,), (1,)), ((), ())), preferred_e...]
    pallas_call x0 -> x6, Pallas kernels: none -> 5.66 us  [the longest x2 4.27 us: slot_products(): pl.pallas_call(kernel, out_shape=outs(n_row) + outs(n_col), in_specs=[SME...]
  transfers between devices with their start and end apart: 4 -> 23, of which waited for: 4 -> 12; matrix products, arithmetic and copies ran while one was open for 0% -> 1% of each run, Pallas kernels for 0% -> 0%
where the time goes in v1:
time: 63.5 us; the launch traced here: 63.3 us
  starting transfers between devices  29.8 us (47%)
  waiting for transfers between devices  23 us (36%)
  Pallas kernels  5.66 us (9%)
  local copies, waits for them, and re-layouts  1.9 us (3%)
  other arithmetic  1.52 us (2%)
  between operations  1.36 us (2%)
    ppermute x23, starting transfers between devices, swap(): return lax.ppermute(value, axes, pairs)  29.8 us
    ppermute x23, waiting for transfers between devices, swap(): return lax.ppermute(value, axes, pairs)  23 us
    pallas_call x2, Pallas kernels, slot_products(): pl.pallas_call(kernel, out_shape=outs(n_row) + outs(n_col), in_specs=[SME...  4.27 us
    unnamed x8, local copies, waits for them, and re-layouts  1.9 us
    pallas_call x4, Pallas kernels, local_call(): pl.pallas_call(kernel, out_shape=[jax.ShapeDtypeStruct(s, d) for s, d in...  1.39 us
  transfers between devices with their start and end apart: 23, of which 12 were waited for; matrix products, arithmetic and copies ran while one was open for 1% of the time, Pallas kernels for 0%

profile of v1, /device:TPU:0, one launch (start us, length us, event | category | flops | bytes accessed | tf_op | source)
XLA Modules:
  0.0 63.3 jit_solution(6944229695431138977)
XLA Ops:
  0.6 0.0 copy-start.2
  0.6 3.0 %collective-permute-start.2 = (bf16[32,512]{1,0:T(8,128)(2,1)}, bf16[32,512]{1,0:T(8,128)(2,1)S(1)}, u32[]{:S(2)}, u32[]{:S(2)}) collective-permute-start(bf16[32,512]{1,0:T(8,128)(2,1)} %bitcast.14), channel_id=1, source_target_pairs={{0,1},{1,0},{2,3},{3,2},{4,5},{5,4},{6,7},{7,6},{8,9},{9,8},{10,11... | collective-permute-start | bytes 98312 | tf_op jit(solution)/shard_map/ppermute | solution.py:28
  3.6 0.0 collective-permute-start
  4.3 0.7 %compare_select_fusion = (s32[6]{0:T(128)S(1)}, s32[6]{0:T(128)S(1)}) fusion(s32[1,1,6]{2,1,0:T(1,128)} %param.8, s32[]{:T(128)S(6)} %axis_index.25, s32[]{:T(128)} %bitcast.10, s32[1,1,6]{2,1,0:T(1,128)} %param.7, s32[]{:T(128)S(6)} %axis_index.23), kind=kLoop, calls=%fused_computation.2 | loop fusion | flops 30 | bytes 108 | tf_op jit(solution)/shard_map/jit(_where)/select_n | solution.py:124
  5.0 0.8 %collective-permute-done.2.cur_x = bf16[32,512]{1,0:T(8,128)(2,1)S(1)} collective-permute-done((bf16[32,512]{1,0:T(8,128)(2,1)}, bf16[32,512]{1,0:T(8,128)(2,1)S(1)}, u32[]{:S(2)}, u32[]{:S(2)}) %collective-permute-start.2) | collective-permute-done | bytes 32800 | tf_op jit(solution)/shard_map/ppermute | solution.py:28
  5.8 0.0 collective-permute-done.cur_core
  5.8 0.8 %pad_maximum_fusion = (bf16[64,512]{1,0:T(8,128)(2,1)S(1)}, bf16[64,512]{1,0:T(8,128)(2,1)S(1)}) fusion(bf16[32,512]{1,0:T(8,128)(2,1)} %bitcast.16, bf16[32,512]{1,0:T(8,128)(2,1)S(1)} %collective-permute-done.2.cur_x, bf16[32,512]{1,0:T(8,128)(2,1)S(1)} %collective-permute-done.cur_core), kind=kLoop, calls=%fused_computation | loop fusion | flops 229376 | bytes 229376 | tf_op jit(solution)/shard_map/concatenate | solution.py:32
  6.5 4.2 %collective-permute-start.5 = (bf16[64,512]{1,0:T(8,128)(2,1)S(1)}, bf16[64,512]{1,0:T(8,128)(2,1)S(1)}, u32[]{:S(2)}, u32[]{:S(2)}) collective-permute-start(bf16[64,512]{1,0:T(8,128)(2,1)S(1)} %get-tuple-element.48.refs_2_), channel_id=1, source_target_pairs={{0,6},{1,7},{2,4},{3,5},{4,2},{5,3},{6,0},{7,1},{8,14},{9,15},{10,... | collective-permute-start | bytes 196616 | tf_op jit(solution)/shard_map/ppermute | solution.py:28
  10.7 0.0 collective-permute-start.4
  10.7 0.6 %collective-permute-start.3 = (bf16[64,512]{1,0:T(8,128)(2,1)S(1)}, bf16[64,512]{1,0:T(8,128)(2,1)S(1)}, u32[]{:S(2)}, u32[]{:S(2)}) collective-permute-start(bf16[64,512]{1,0:T(8,128)(2,1)S(1)} %get-tuple-element.48.refs_2_), channel_id=1, source_target_pairs={{0,2},{1,3},{2,0},{3,1},{4,6},{5,7},{6,4},{7,5},{8,10},{9,11},{10,... | collective-permute-start | bytes 196616 | tf_op jit(solution)/shard_map/ppermute | solution.py:28
  11.4 1.7 %collective-permute-start.1 = (bf16[64,512]{1,0:T(8,128)(2,1)S(1)}, bf16[64,512]{1,0:T(8,128)(2,1)S(1)}, u32[]{:S(2)}, u32[]{:S(2)}) collective-permute-start(bf16[64,512]{1,0:T(8,128)(2,1)S(1)} %get-tuple-element.49.refs_0_), channel_id=1, source_target_pairs={{0,16},{8,24},{16,0},{24,8},{1,17},{9,25},{17,1},{25,9},{2,18},{10... | collective-permute-start | bytes 196616 | tf_op jit(solution)/shard_map/ppermute | solution.py:28
  13.0 0.1 pad_add_fusion.meta_ref
  13.1 2.5 %collective-permute-done.1.refs_1_ = bf16[64,512]{1,0:T(8,128)(2,1)S(1)} collective-permute-done((bf16[64,512]{1,0:T(8,128)(2,1)S(1)}, bf16[64,512]{1,0:T(8,128)(2,1)S(1)}, u32[]{:S(2)}, u32[]{:S(2)}) %collective-permute-start.1) | collective-permute-done | bytes 65568 | tf_op jit(solution)/shard_map/ppermute | solution.py:28
  15.6 0.0 collective-permute-done.5.refs_5_
  15.6 0.4 collective-permute-done.4.refs_4_
  16.0 0.0 collective-permute-done.3.refs_3_
  16.0 0.0 copy-start
  16.0 1.9 %copy-done = bf16[1,1,6,512,512]{4,3,2,1,0:T(8,128)(2,1)S(1)} copy-done((bf16[1,1,6,512,512]{4,3,2,1,0:T(8,128)(2,1)S(1)}, bf16[1,1,6,512,512]{4,3,2,1,0:T(8,128)(2,1)}, u32[]{:S(2)}) %copy-start) | copy-done | bytes 3145752
  17.9 0.0 copy-start.1
  17.9 2.1 %shard_map.68 = (f32[64,512]{1,0:T(8,128)S(1)}, bf16[64,512]{1,0:T(8,128)(2,1)S(1)}, f32[64,512]{1,0:T(8,128)S(1)}, bf16[64,512]{1,0:T(8,128)(2,1)S(1)}, bf16[64...) custom-call(s32[13]{0:T(128)S(1)} %pad_add_fusion.meta_ref, bf16[6,512,512]{2,1,0:T(8,128)(2,1)S(1)} %bitcast.12, ...), custom_call_target="tpu_custom_call" | custom-call | flops 201326592 | bytes 3145728 | tf_op jit(solution)/shard_map/pallas_call | solution.py:73
  20.0 1.6 %collective-permute-start.6 = (bf16[64,512]{1,0:T(8,128)(2,1)S(1)}, bf16[64,512]{1,0:T(8,128)(2,1)S(1)}, u32[]{:S(2)}, u32[]{:S(2)}) collective-permute-start(bf16[64,512]{1,0:T(8,128)(2,1)S(1)} %get-tuple-element.27), channel_id=1, source_target_pairs={{0,16},{8,24},{16,0},{24,8},{1,17},{9,25},{17,1},{25,9},{2,18},{10... | collective-permute-start | bytes 196616 | tf_op jit(solution)/shard_map/ppermute | solution.py:28
  21.6 1.0 %collective-permute-start.7 = (bf16[64,512]{1,0:T(8,128)(2,1)S(1)}, bf16[64,512]{1,0:T(8,128)(2,1)S(1)}, u32[]{:S(2)}, u32[]{:S(2)}) collective-permute-start(bf16[64,512]{1,0:T(8,128)(2,1)S(1)} %get-tuple-element.28), channel_id=1, source_target_pairs={{0,2},{1,3},{2,0},{3,1},{4,6},{5,7},{6,4},{7,5},{8,10},{9,11},{10,... | collective-permute-start | bytes 196616 | tf_op jit(solution)/shard_map/ppermute | solution.py:28
  22.7 2.9 %collective-permute-start.8 = (bf16[64,512]{1,0:T(8,128)(2,1)S(1)}, bf16[64,512]{1,0:T(8,128)(2,1)S(1)}, u32[]{:S(2)}, u32[]{:S(2)}) collective-permute-start(bf16[64,512]{1,0:T(8,128)(2,1)S(1)} %get-tuple-element.29), channel_id=1, source_target_pairs={{0,4},{1,5},{2,6},{3,7},{4,0},{5,1},{6,2},{7,3},{8,12},{9,13},{10,... | collective-permute-start | bytes 196616 | tf_op jit(solution)/shard_map/ppermute | solution.py:28
  25.6 0.4 collective-permute-start.9
  26.0 0.0 collective-permute-done.6.refs_0_
  26.0 0.0 collective-permute-done.7.refs_1_
  26.0 3.0 %collective-permute-done.8.refs_2_ = bf16[64,512]{1,0:T(8,128)(2,1)S(1)} collective-permute-done((bf16[64,512]{1,0:T(8,128)(2,1)S(1)}, bf16[64,512]{1,0:T(8,128)(2,1)S(1)}, u32[]{:S(2)}, u32[]{:S(2)}) %collective-permute-start.8) | collective-permute-done | bytes 65568 | tf_op jit(solution)/shard_map/ppermute | solution.py:28
  29.0 2.7 %collective-permute-done.9.refs_3_ = bf16[64,512]{1,0:T(8,128)(2,1)S(1)} collective-permute-done((bf16[64,512]{1,0:T(8,128)(2,1)S(1)}, bf16[64,512]{1,0:T(8,128)(2,1)S(1)}, u32[]{:S(2)}, u32[]{:S(2)}) %collective-permute-start.9) | collective-permute-done | bytes 65568 | tf_op jit(solution)/shard_map/ppermute | solution.py:28
  31.6 0.1 shard_map.69
  31.7 0.1 collective-permute-start.10
  31.8 1.6 %collective-permute-start.11 = (bf16[64,512]{1,0:T(8,128)(2,1)S(1)}, bf16[64,512]{1,0:T(8,128)(2,1)S(1)}, u32[]{:S(2)}, u32[]{:S(2)}) collective-permute-start(bf16[64,512]{1,0:T(8,128)(2,1)S(1)} %get-tuple-element.34), channel_id=1, source_target_pairs={{0,1},{1,0},{2,3},{3,2},{4,5},{5,4},{6,7},{7,6},{8,9},{9,8},{10,11... | collective-permute-start | bytes 196616 | tf_op jit(solution)/shard_map/ppermute | solution.py:28
  33.3 0.3 collective-permute-start.12
  33.6 0.0 collective-permute-done.10.core_ref
  33.6 2.6 %collective-permute-done.11.x_ref = bf16[64,512]{1,0:T(8,128)(2,1)S(1)} collective-permute-done((bf16[64,512]{1,0:T(8,128)(2,1)S(1)}, bf16[64,512]{1,0:T(8,128)(2,1)S(1)}, u32[]{:S(2)}, u32[]{:S(2)}) %collective-permute-start.11) | collective-permute-done | bytes 65568 | tf_op jit(solution)/shard_map/ppermute | solution.py:28
  36.3 1.1 %collective-permute-done.12.diag_ref = bf16[64,512]{1,0:T(8,128)(2,1)S(1)} collective-permute-done((bf16[64,512]{1,0:T(8,128)(2,1)S(1)}, bf16[64,512]{1,0:T(8,128)(2,1)S(1)}, u32[]{:S(2)}, u32[]{:S(2)}) %collective-permute-start.12) | collective-permute-done | bytes 65568 | tf_op jit(solution)/shard_map/ppermute | solution.py:28
  37.4 0.0 copy-done.2
  37.4 0.6 %shard_map.70 = (bf16[32,512]{1,0:T(8,128)(2,1)}, bf16[64,512]{1,0:T(8,128)(2,1)S(1)}, bf16[64,512]{1,0:T(8,128)(2,1)S(1)}) custom-call(f32[64,512]{1,0:T(8,128)S(1)} %get-tuple-element.31.d_ref, f32[64,512]{1,0:T(8,128)S(1)} %get-tuple-element.32.m_ref, bf16[64,512]{1,0:T(8,128)(2,1)S(1)} %collective-permute-done.10.core_ref, ...), custom_call_target="tpu_custom_call" | custom-call | tf_op jit(solution)/shard_map/pallas_call | solution.py:93
  38.0 0.0 copy-start.3
  38.0 0.5 collective-permute-start.13
  38.5 0.7 %collective-permute-start.16 = (bf16[64,512]{1,0:T(8,128)(2,1)S(1)}, bf16[64,512]{1,0:T(8,128)(2,1)S(1)}, u32[]{:S(2)}, u32[]{:S(2)}) collective-permute-start(bf16[64,512]{1,0:T(8,128)(2,1)S(1)} %get-tuple-element.38.refs_2_), channel_id=1, source_target_pairs={{0,6},{1,7},{2,4},{3,5},{4,2},{5,3},{6,0},{7,1},{8,14},{9,15},{10,... | collective-permute-start | bytes 196616 | tf_op jit(solution)/shard_map/ppermute | solution.py:28
  39.2 0.0 collective-permute-start.15
  39.2 3.7 %collective-permute-start.14 = (bf16[64,512]{1,0:T(8,128)(2,1)S(1)}, bf16[64,512]{1,0:T(8,128)(2,1)S(1)}, u32[]{:S(2)}, u32[]{:S(2)}) collective-permute-start(bf16[64,512]{1,0:T(8,128)(2,1)S(1)} %get-tuple-element.38.refs_2_), channel_id=1, source_target_pairs={{0,2},{1,3},{2,0},{3,1},{4,6},{5,7},{6,4},{7,5},{8,10},{9,11},{10,... | collective-permute-start | bytes 196616 | tf_op jit(solution)/shard_map/ppermute | solution.py:28
  42.9 0.0 collective-permute-done.13.refs_1_
  42.9 2.4 %collective-permute-done.16.refs_5_ = bf16[64,512]{1,0:T(8,128)(2,1)S(1)} collective-permute-done((bf16[64,512]{1,0:T(8,128)(2,1)S(1)}, bf16[64,512]{1,0:T(8,128)(2,1)S(1)}, u32[]{:S(2)}, u32[]{:S(2)}) %collective-permute-start.16) | collective-permute-done | bytes 65568 | tf_op jit(solution)/shard_map/ppermute | solution.py:28
  45.4 1.2 %collective-permute-done.15.refs_4_ = bf16[64,512]{1,0:T(8,128)(2,1)S(1)} collective-permute-done((bf16[64,512]{1,0:T(8,128)(2,1)S(1)}, bf16[64,512]{1,0:T(8,128)(2,1)S(1)}, u32[]{:S(2)}, u32[]{:S(2)}) %collective-permute-start.15) | collective-permute-done | bytes 65568 | tf_op jit(solution)/shard_map/ppermute | solution.py:28
  46.5 0.0 collective-permute-done.14.refs_3_
  46.5 0.0 copy-done.1
  46.5 2.1 %shard_map.71 = (f32[64,512]{1,0:T(8,128)S(1)}, bf16[64,512]{1,0:T(8,128)(2,1)S(1)}, f32[64,512]{1,0:T(8,128)S(1)}, bf16[64,512]{1,0:T(8,128)(2,1)S(1)}, bf16[64...) custom-call(s32[13]{0:T(128)S(1)} %pad_add_fusion.meta_ref, bf16[6,512,512]{2,1,0:T(8,128)(2,1)S(1)} %bitcast.13, ...), custom_call_target="tpu_custom_call" | custom-call | flops 201326592 | bytes 3145728 | tf_op jit(solution)/shard_map/pallas_call | solution.py:73
  48.7 1.6 %collective-permute-start.17 = (bf16[64,512]{1,0:T(8,128)(2,1)S(1)}, bf16[64,512]{1,0:T(8,128)(2,1)S(1)}, u32[]{:S(2)}, u32[]{:S(2)}) collective-permute-start(bf16[64,512]{1,0:T(8,128)(2,1)S(1)} %get-tuple-element.41), channel_id=1, source_target_pairs={{0,16},{8,24},{16,0},{24,8},{1,17},{9,25},{17,1},{25,9},{2,18},{10... | collective-permute-start | bytes 196616 | tf_op jit(solution)/shard_map/ppermute | solution.py:28
  50.3 0.6 %collective-permute-start.18 = (bf16[64,512]{1,0:T(8,128)(2,1)S(1)}, bf16[64,512]{1,0:T(8,128)(2,1)S(1)}, u32[]{:S(2)}, u32[]{:S(2)}) collective-permute-start(bf16[64,512]{1,0:T(8,128)(2,1)S(1)} %get-tuple-element.42), channel_id=1, source_target_pairs={{0,2},{1,3},{2,0},{3,1},{4,6},{5,7},{6,4},{7,5},{8,10},{9,11},{10,... | collective-permute-start | bytes 196616 | tf_op jit(solution)/shard_map/ppermute | solution.py:28
  50.9 1.5 %collective-permute-start.19 = (bf16[64,512]{1,0:T(8,128)(2,1)S(1)}, bf16[64,512]{1,0:T(8,128)(2,1)S(1)}, u32[]{:S(2)}, u32[]{:S(2)}) collective-permute-start(bf16[64,512]{1,0:T(8,128)(2,1)S(1)} %get-tuple-element.43), channel_id=1, source_target_pairs={{0,4},{1,5},{2,6},{3,7},{4,0},{5,1},{6,2},{7,3},{8,12},{9,13},{10,... | collective-permute-start | bytes 196616 | tf_op jit(solution)/shard_map/ppermute | solution.py:28
  52.4 2.3 %collective-permute-start.20 = (bf16[64,512]{1,0:T(8,128)(2,1)S(1)}, bf16[64,512]{1,0:T(8,128)(2,1)S(1)}, u32[]{:S(2)}, u32[]{:S(2)}) collective-permute-start(bf16[64,512]{1,0:T(8,128)(2,1)S(1)} %get-tuple-element.44), channel_id=1, source_target_pairs={{0,6},{1,7},{2,4},{3,5},{4,2},{5,3},{6,0},{7,1},{8,14},{9,15},{10,... | collective-permute-start | bytes 196616 | tf_op jit(solution)/shard_map/ppermute | solution.py:28
  54.7 0.0 collective-permute-done.17.refs_0_
  54.7 0.0 collective-permute-done.18.refs_1_
  54.7 2.6 %collective-permute-done.19.refs_2_ = bf16[64,512]{1,0:T(8,128)(2,1)S(1)} collective-permute-done((bf16[64,512]{1,0:T(8,128)(2,1)S(1)}, bf16[64,512]{1,0:T(8,128)(2,1)S(1)}, u32[]{:S(2)}, u32[]{:S(2)}) %collective-permute-start.19) | collective-permute-done | bytes 65568 | tf_op jit(solution)/shard_map/ppermute | solution.py:28
  57.2 1.3 %collective-permute-done.20.refs_3_ = bf16[64,512]{1,0:T(8,128)(2,1)S(1)} collective-permute-done((bf16[64,512]{1,0:T(8,128)(2,1)S(1)}, bf16[64,512]{1,0:T(8,128)(2,1)S(1)}, u32[]{:S(2)}, u32[]{:S(2)}) %collective-permute-start.20) | collective-permute-done | bytes 65568 | tf_op jit(solution)/shard_map/ppermute | solution.py:28
  58.5 0.1 shard_map.72
  58.6 0.1 collective-permute-start.21
  58.7 1.5 %collective-permute-start.22 = (bf16[32,512]{1,0:T(8,128)(2,1)S(1)}, bf16[32,512]{1,0:T(8,128)(2,1)S(1)}, u32[]{:S(2)}, u32[]{:S(2)}) collective-permute-start(bf16[32,512]{1,0:T(8,128)(2,1)S(1)} %get-tuple-element.47), channel_id=1, source_target_pairs={{0,1},{1,0},{2,3},{3,2},{4,5},{5,4},{6,7},{7,6},{8,9},{9,8},{10,11... | collective-permute-start | bytes 98312 | tf_op jit(solution)/shard_map/ppermute | solution.py:28
  60.2 0.0 collective-permute-done.21.core_ref
  60.2 2.5 %collective-permute-done.22.x_ref = bf16[32,512]{1,0:T(8,128)(2,1)S(1)} collective-permute-done((bf16[32,512]{1,0:T(8,128)(2,1)S(1)}, bf16[32,512]{1,0:T(8,128)(2,1)S(1)}, u32[]{:S(2)}, u32[]{:S(2)}) %collective-permute-start.22) | collective-permute-done | bytes 32800 | tf_op jit(solution)/shard_map/ppermute | solution.py:28
  62.7 0.0 copy-done.3
  62.7 0.6 %shard_map.73 = bf16[32,512]{1,0:T(8,128)(2,1)} custom-call(f32[32,512]{1,0:T(8,128)S(1)} %get-tuple-element.45.keep_ref, bf16[32,512]{1,0:T(8,128)(2,1)S(1)} %collective-permute-done.21.core_ref, bf16[32,512]{1,0:T(8,128)(2,1)S(1)} %collective-permute-done.22.x_ref, bf16[32,512]{1,0:T(8,128)(2,1)S(1)} %copy-done.3, bf16[32,512]{1,0:T(8,128)(2,1)S(1)} %bitcast.18), custom_call_target="tpu_custom_call" | custom-call | tf_op jit(solution)/shard_map/pallas_call | solution.py:93
Async XLA Ops:
  0.6 36.7 %copy-start.2 = (bf16[32,1,1,1,512]{4,0,3,2,1:T(8,128)(2,1)S(1)}, bf16[32,1,1,1,512]{4,0,3,2,1:T(8,128)(2,1)}, u32[]{:S(2)}) copy-start(bf16[32,1,1,1,512]{4,0,3,2,1:T(8,128)(2,1)} %param.5) | copy-start | bytes 98308
  0.6 5.1 %collective-permute-start.2 = (bf16[32,512]{1,0:T(8,128)(2,1)}, bf16[32,512]{1,0:T(8,128)(2,1)S(1)}, u32[]{:S(2)}, u32[]{:S(2)}) collective-permute-start(bf16[32,512]{1,0:T(8,128)(2,1)} %bitcast.14), channel_id=1, source_target_pairs={{0,1},{1,0},{2,3},{3,2},{4,5},{5,4},{6,7},{7,6},{8,9},{9,8},{10,11... | collective-permute-start | bytes 98312 | tf_op jit(solution)/shard_map/ppermute | solution.py:28
  3.6 2.1 %collective-permute-start = (bf16[32,512]{1,0:T(8,128)(2,1)}, bf16[32,512]{1,0:T(8,128)(2,1)S(1)}, u32[]{:S(2)}, u32[]{:S(2)}) collective-permute-start(bf16[32,512]{1,0:T(8,128)(2,1)} %bitcast.15), channel_id=1, source_target_pairs={{0,8},{8,0},{16,24},{24,16},{1,9},{9,1},{17,25},{25,17},{2,10},{10... | collective-permute-start | bytes 98312 | tf_op jit(solution)/shard_map/ppermute | solution.py:28
  6.5 9.1 %collective-permute-start.5 = (bf16[64,512]{1,0:T(8,128)(2,1)S(1)}, bf16[64,512]{1,0:T(8,128)(2,1)S(1)}, u32[]{:S(2)}, u32[]{:S(2)}) collective-permute-start(bf16[64,512]{1,0:T(8,128)(2,1)S(1)} %get-tuple-element.48.refs_2_), channel_id=1, source_target_pairs={{0,6},{1,7},{2,4},{3,5},{4,2},{5,3},{6,0},{7,1},{8,14},{9,15},{10,... | collective-permute-start | bytes 196616 | tf_op jit(solution)/shard_map/ppermute | solution.py:28
  10.7 5.3 %collective-permute-start.4 = (bf16[64,512]{1,0:T(8,128)(2,1)S(1)}, bf16[64,512]{1,0:T(8,128)(2,1)S(1)}, u32[]{:S(2)}, u32[]{:S(2)}) collective-permute-start(bf16[64,512]{1,0:T(8,128)(2,1)S(1)} %get-tuple-element.48.refs_2_), channel_id=1, source_target_pairs={{0,4},{1,5},{2,6},{3,7},{4,0},{5,1},{6,2},{7,3},{8,12},{9,13},{10,... | collective-permute-start | bytes 196616 | tf_op jit(solution)/shard_map/ppermute | solution.py:28
  10.7 5.3 %collective-permute-start.3 = (bf16[64,512]{1,0:T(8,128)(2,1)S(1)}, bf16[64,512]{1,0:T(8,128)(2,1)S(1)}, u32[]{:S(2)}, u32[]{:S(2)}) collective-permute-start(bf16[64,512]{1,0:T(8,128)(2,1)S(1)} %get-tuple-element.48.refs_2_), channel_id=1, source_target_pairs={{0,2},{1,3},{2,0},{3,1},{4,6},{5,7},{6,4},{7,5},{8,10},{9,11},{10,... | collective-permute-start | bytes 196616 | tf_op jit(solution)/shard_map/ppermute | solution.py:28
  11.4 4.3 %collective-permute-start.1 = (bf16[64,512]{1,0:T(8,128)(2,1)S(1)}, bf16[64,512]{1,0:T(8,128)(2,1)S(1)}, u32[]{:S(2)}, u32[]{:S(2)}) collective-permute-start(bf16[64,512]{1,0:T(8,128)(2,1)S(1)} %get-tuple-element.49.refs_0_), channel_id=1, source_target_pairs={{0,16},{8,24},{16,0},{24,8},{1,17},{9,25},{17,1},{25,9},{2,18},{10... | collective-permute-start | bytes 196616 | tf_op jit(solution)/shard_map/ppermute | solution.py:28
  16.0 1.9 %copy-start = (bf16[1,1,6,512,512]{4,3,2,1,0:T(8,128)(2,1)S(1)}, bf16[1,1,6,512,512]{4,3,2,1,0:T(8,128)(2,1)}, u32[]{:S(2)}) copy-start(bf16[1,1,6,512,512]{4,3,2,1,0:T(8,128)(2,1)} %param.6) | copy-start | bytes 9437188
  17.9 28.6 %copy-start.1 = (bf16[1,1,6,512,512]{4,3,2,1,0:T(8,128)(2,1)S(1)}, bf16[1,1,6,512,512]{4,3,2,1,0:T(8,128)(2,1)}, u32[]{:S(2)}) copy-start(bf16[1,1,6,512,512]{4,3,2,1,0:T(8,128)(2,1)} %param.6) | copy-start | bytes 9437188
  20.0 6.0 %collective-permute-start.6 = (bf16[64,512]{1,0:T(8,128)(2,1)S(1)}, bf16[64,512]{1,0:T(8,128)(2,1)S(1)}, u32[]{:S(2)}, u32[]{:S(2)}) collective-permute-start(bf16[64,512]{1,0:T(8,128)(2,1)S(1)} %get-tuple-element.27), channel_id=1, source_target_pairs={{0,16},{8,24},{16,0},{24,8},{1,17},{9,25},{17,1},{25,9},{2,18},{10... | collective-permute-start | bytes 196616 | tf_op jit(solution)/shard_map/ppermute | solution.py:28
  21.6 4.4 %collective-permute-start.7 = (bf16[64,512]{1,0:T(8,128)(2,1)S(1)}, bf16[64,512]{1,0:T(8,128)(2,1)S(1)}, u32[]{:S(2)}, u32[]{:S(2)}) collective-permute-start(bf16[64,512]{1,0:T(8,128)(2,1)S(1)} %get-tuple-element.28), channel_id=1, source_target_pairs={{0,2},{1,3},{2,0},{3,1},{4,6},{5,7},{6,4},{7,5},{8,10},{9,11},{10,... | collective-permute-start | bytes 196616 | tf_op jit(solution)/shard_map/ppermute | solution.py:28
  22.7 6.3 %collective-permute-start.8 = (bf16[64,512]{1,0:T(8,128)(2,1)S(1)}, bf16[64,512]{1,0:T(8,128)(2,1)S(1)}, u32[]{:S(2)}, u32[]{:S(2)}) collective-permute-start(bf16[64,512]{1,0:T(8,128)(2,1)S(1)} %get-tuple-element.29), channel_id=1, source_target_pairs={{0,4},{1,5},{2,6},{3,7},{4,0},{5,1},{6,2},{7,3},{8,12},{9,13},{10,... | collective-permute-start | bytes 196616 | tf_op jit(solution)/shard_map/ppermute | solution.py:28
  25.6 6.1 %collective-permute-start.9 = (bf16[64,512]{1,0:T(8,128)(2,1)S(1)}, bf16[64,512]{1,0:T(8,128)(2,1)S(1)}, u32[]{:S(2)}, u32[]{:S(2)}) collective-permute-start(bf16[64,512]{1,0:T(8,128)(2,1)S(1)} %get-tuple-element.30), channel_id=1, source_target_pairs={{0,6},{1,7},{2,4},{3,5},{4,2},{5,3},{6,0},{7,1},{8,14},{9,15},{10,... | collective-permute-start | bytes 196616 | tf_op jit(solution)/shard_map/ppermute | solution.py:28
  31.7 1.9 %collective-permute-start.10 = (bf16[64,512]{1,0:T(8,128)(2,1)S(1)}, bf16[64,512]{1,0:T(8,128)(2,1)S(1)}, u32[]{:S(2)}, u32[]{:S(2)}) collective-permute-start(bf16[64,512]{1,0:T(8,128)(2,1)S(1)} %get-tuple-element.33), channel_id=1, source_target_pairs={{0,8},{8,0},{16,24},{24,16},{1,9},{9,1},{17,25},{25,17},{2,10},{10... | collective-permute-start | bytes 196616 | tf_op jit(solution)/shard_map/ppermute | solution.py:28
  31.8 4.5 %collective-permute-start.11 = (bf16[64,512]{1,0:T(8,128)(2,1)S(1)}, bf16[64,512]{1,0:T(8,128)(2,1)S(1)}, u32[]{:S(2)}, u32[]{:S(2)}) collective-permute-start(bf16[64,512]{1,0:T(8,128)(2,1)S(1)} %get-tuple-element.34), channel_id=1, source_target_pairs={{0,1},{1,0},{2,3},{3,2},{4,5},{5,4},{6,7},{7,6},{8,9},{9,8},{10,11... | collective-permute-start | bytes 196616 | tf_op jit(solution)/shard_map/ppermute | solution.py:28
  33.3 4.0 %collective-permute-start.12 = (bf16[64,512]{1,0:T(8,128)(2,1)S(1)}, bf16[64,512]{1,0:T(8,128)(2,1)S(1)}, u32[]{:S(2)}, u32[]{:S(2)}) collective-permute-start(bf16[64,512]{1,0:T(8,128)(2,1)S(1)} %get-tuple-element.35), channel_id=1, source_target_pairs={{0,9},{1,8},{2,11},{3,10},{4,13},{5,12},{6,15},{7,14},{8,1},{9,0},... | collective-permute-start | bytes 196616 | tf_op jit(solution)/shard_map/ppermute | solution.py:28
  38.0 24.6 %copy-start.3 = (bf16[32,512]{1,0:T(8,128)(2,1)S(1)}, bf16[32,512]{1,0:T(8,128)(2,1)}, u32[]{:S(2)}) copy-start(bf16[32,512]{1,0:T(8,128)(2,1)} %get-tuple-element.36.cur_ref) | copy-start | bytes 98308
  38.0 4.9 %collective-permute-start.13 = (bf16[64,512]{1,0:T(8,128)(2,1)S(1)}, bf16[64,512]{1,0:T(8,128)(2,1)S(1)}, u32[]{:S(2)}, u32[]{:S(2)}) collective-permute-start(bf16[64,512]{1,0:T(8,128)(2,1)S(1)} %get-tuple-element.37.refs_0_), channel_id=1, source_target_pairs={{0,16},{8,24},{16,0},{24,8},{1,17},{9,25},{17,1},{25,9},{2,18},{10... | collective-permute-start | bytes 196616 | tf_op jit(solution)/shard_map/ppermute | solution.py:28
  38.5 6.8 %collective-permute-start.16 = (bf16[64,512]{1,0:T(8,128)(2,1)S(1)}, bf16[64,512]{1,0:T(8,128)(2,1)S(1)}, u32[]{:S(2)}, u32[]{:S(2)}) collective-permute-start(bf16[64,512]{1,0:T(8,128)(2,1)S(1)} %get-tuple-element.38.refs_2_), channel_id=1, source_target_pairs={{0,6},{1,7},{2,4},{3,5},{4,2},{5,3},{6,0},{7,1},{8,14},{9,15},{10,... | collective-permute-start | bytes 196616 | tf_op jit(solution)/shard_map/ppermute | solution.py:28
  39.2 7.3 %collective-permute-start.15 = (bf16[64,512]{1,0:T(8,128)(2,1)S(1)}, bf16[64,512]{1,0:T(8,128)(2,1)S(1)}, u32[]{:S(2)}, u32[]{:S(2)}) collective-permute-start(bf16[64,512]{1,0:T(8,128)(2,1)S(1)} %get-tuple-element.38.refs_2_), channel_id=1, source_target_pairs={{0,4},{1,5},{2,6},{3,7},{4,0},{5,1},{6,2},{7,3},{8,12},{9,13},{10,... | collective-permute-start | bytes 196616 | tf_op jit(solution)/shard_map/ppermute | solution.py:28
  39.2 7.3 %collective-permute-start.14 = (bf16[64,512]{1,0:T(8,128)(2,1)S(1)}, bf16[64,512]{1,0:T(8,128)(2,1)S(1)}, u32[]{:S(2)}, u32[]{:S(2)}) collective-permute-start(bf16[64,512]{1,0:T(8,128)(2,1)S(1)} %get-tuple-element.38.refs_2_), channel_id=1, source_target_pairs={{0,2},{1,3},{2,0},{3,1},{4,6},{5,7},{6,4},{7,5},{8,10},{9,11},{10,... | collective-permute-start | bytes 196616 | tf_op jit(solution)/shard_map/ppermute | solution.py:28
  48.7 6.0 %collective-permute-start.17 = (bf16[64,512]{1,0:T(8,128)(2,1)S(1)}, bf16[64,512]{1,0:T(8,128)(2,1)S(1)}, u32[]{:S(2)}, u32[]{:S(2)}) collective-permute-start(bf16[64,512]{1,0:T(8,128)(2,1)S(1)} %get-tuple-element.41), channel_id=1, source_target_pairs={{0,16},{8,24},{16,0},{24,8},{1,17},{9,25},{17,1},{25,9},{2,18},{10... | collective-permute-start | bytes 196616 | tf_op jit(solution)/shard_map/ppermute | solution.py:28
  50.3 4.4 %collective-permute-start.18 = (bf16[64,512]{1,0:T(8,128)(2,1)S(1)}, bf16[64,512]{1,0:T(8,128)(2,1)S(1)}, u32[]{:S(2)}, u32[]{:S(2)}) collective-permute-start(bf16[64,512]{1,0:T(8,128)(2,1)S(1)} %get-tuple-element.42), channel_id=1, source_target_pairs={{0,2},{1,3},{2,0},{3,1},{4,6},{5,7},{6,4},{7,5},{8,10},{9,11},{10,... | collective-permute-start | bytes 196616 | tf_op jit(solution)/shard_map/ppermute | solution.py:28
  50.9 6.3 %collective-permute-start.19 = (bf16[64,512]{1,0:T(8,128)(2,1)S(1)}, bf16[64,512]{1,0:T(8,128)(2,1)S(1)}, u32[]{:S(2)}, u32[]{:S(2)}) collective-permute-start(bf16[64,512]{1,0:T(8,128)(2,1)S(1)} %get-tuple-element.43), channel_id=1, source_target_pairs={{0,4},{1,5},{2,6},{3,7},{4,0},{5,1},{6,2},{7,3},{8,12},{9,13},{10,... | collective-permute-start | bytes 196616 | tf_op jit(solution)/shard_map/ppermute | solution.py:28
  52.4 6.2 %collective-permute-start.20 = (bf16[64,512]{1,0:T(8,128)(2,1)S(1)}, bf16[64,512]{1,0:T(8,128)(2,1)S(1)}, u32[]{:S(2)}, u32[]{:S(2)}) collective-permute-start(bf16[64,512]{1,0:T(8,128)(2,1)S(1)} %get-tuple-element.44), channel_id=1, source_target_pairs={{0,6},{1,7},{2,4},{3,5},{4,2},{5,3},{6,0},{7,1},{8,14},{9,15},{10,... | collective-permute-start | bytes 196616 | tf_op jit(solution)/shard_map/ppermute | solution.py:28
  58.6 1.6 %collective-permute-start.21 = (bf16[32,512]{1,0:T(8,128)(2,1)S(1)}, bf16[32,512]{1,0:T(8,128)(2,1)S(1)}, u32[]{:S(2)}, u32[]{:S(2)}) collective-permute-start(bf16[32,512]{1,0:T(8,128)(2,1)S(1)} %get-tuple-element.46), channel_id=1, source_target_pairs={{0,8},{8,0},{16,24},{24,16},{1,9},{9,1},{17,25},{25,17},{2,10},{10... | collective-permute-start | bytes 98312 | tf_op jit(solution)/shard_map/ppermute | solution.py:28
  58.7 4.0 %collective-permute-start.22 = (bf16[32,512]{1,0:T(8,128)(2,1)S(1)}, bf16[32,512]{1,0:T(8,128)(2,1)S(1)}, u32[]{:S(2)}, u32[]{:S(2)}) collective-permute-start(bf16[32,512]{1,0:T(8,128)(2,1)S(1)} %get-tuple-element.47), channel_id=1, source_target_pairs={{0,1},{1,0},{2,3},{3,2},{4,5},{5,4},{6,7},{7,6},{8,9},{9,8},{10,11... | collective-permute-start | bytes 98312 | tf_op jit(solution)/shard_map/ppermute | solution.py:28

commit v2 on v0

v2 whole, which is shorter than its diff:
```python
import jax
import jax.numpy as jnp
from jax import lax
from jax.experimental import pallas as pl
from jax.experimental.pallas import tpu as pltpu
from jax.sharding import PartitionSpec as P

shift_center = 0.5
half_width = 2.0

VMEM = pl.BlockSpec(memory_space=pltpu.VMEM)
SMEM = pl.BlockSpec(memory_space=pltpu.SMEM)
PARAMS = pltpu.CompilerParams(vmem_limit_bytes=16 * 1024 * 1024)
f32 = jnp.float32
bf16 = jnp.bfloat16


def swap(value, axis, pattern):
    return lax.ppermute(value, axis, [(i, i ^ pattern) for i in range(lax.axis_size(axis))])


def local_call(kernel, shapes, *operands, specs=None, scratch=(), flops=1000, nbytes=100000, params=PARAMS):
    return pl.pallas_call(
        kernel,
        out_shape=[jax.ShapeDtypeStruct(s, d) for s, d in shapes],
        in_specs=specs or [VMEM] * len(operands),
        out_specs=[VMEM] * len(shapes),
        scratch_shapes=scratch,
        compiler_params=params,
        cost_estimate=pl.CostEstimate(flops=flops, bytes_accessed=nbytes, transcendentals=0),
    )(*operands)


def prepare(blocks, start_vecs, block_rows, block_cols, block_count):
    slots = blocks.shape[2]

    def kernel(count_ref, rows_hbm, cols_hbm, blocks_hbm, vecs_hbm, tiles_out, vecs_out, meta_out, rows_ref, cols_ref, sems):
        copies = [
            pltpu.make_async_copy(rows_hbm, rows_ref, sems.at[slots + 1]),
            pltpu.make_async_copy(cols_hbm, cols_ref, sems.at[slots + 2]),
        ]
        copies += [pltpu.make_async_copy(vecs_hbm, vecs_out, sems.at[slots])]
        copies += [pltpu.make_async_copy(blocks_hbm.at[0, 0, s], tiles_out.at[s], sems.at[s]) for s in range(slots)]
        for copy in copies:
            copy.start()
        row_at, col_at = lax.axis_index("row"), lax.axis_index("col")
        for copy in copies[:2]:
            copy.wait()
        count = count_ref[0, 0]
        for s in range(slots):
            meta_out[s] = jnp.where(s < count, rows_ref[0, 0, s] ^ row_at, 0)
            meta_out[slots + s] = jnp.where(s < count, cols_ref[0, 0, s] ^ col_at, 0)
        meta_out[2 * slots] = count
        for copy in copies[2:]:
            copy.wait()

    arrays = (block_rows, block_cols, blocks, start_vecs)
    return pl.pallas_call(
        kernel,
        out_shape=[
            pltpu.VMEM(blocks.shape[2:], blocks.dtype),
            pltpu.VMEM(start_vecs.shape, start_vecs.dtype),
            pltpu.SMEM((2 * slots + 1,), jnp.int32),
        ],
        in_specs=[SMEM] + [pl.BlockSpec(memory_space=pltpu.HBM)] * len(arrays),
        out_specs=[VMEM, VMEM, SMEM],
        scratch_shapes=[pltpu.SMEM(a.shape, a.dtype) for a in arrays[:2]] + [pltpu.SemaphoreType.DMA((slots + 3,))],
        compiler_params=PARAMS,
        cost_estimate=pl.CostEstimate(flops=1000, bytes_accessed=2 * blocks.size * 2, transcendentals=0),
    )(block_count, *[pltpu.with_memory_space_constraint(a, pltpu.HBM) for a in arrays])


class Axis:
    def __init__(self, name, bit):
        self.name, self.bit = name, bit
        self.size = lax.axis_size(name)
        self.inner = [i for i in range(self.size) if not i & bit]

    def swap_pair(self, value):
        return swap(value, self.name, self.bit)

    def spread(self, pair):
        return [pair if i == 0 else swap(pair, self.name, i) for i in self.inner]

    def collect(self, terms):
        return [swap(t, self.name, i) for i, t in zip(self.inner, terms, strict=True) if i][::-1]


def slot_products(meta, tiles, pairs, source, target, after=()):
    slots, width = tiles.shape[0], tiles.shape[1]
    n_vec = pairs[0].shape[0] // 2
    n_in, n_out = len(pairs), len(target.inner)
    mirrored = source.name == "row"

    def kernel(meta_ref, tiles_ref, *refs):
        ins, refs = refs[:n_in], refs[n_in + len(after) :]
        outs, (vecs, totals) = refs[:n_out], refs[n_out:]
        for i, ref in zip(source.inner, ins, strict=True):
            for half in range(2):
                vecs[i + half * source.bit] = ref[half * n_vec : (half + 1) * n_vec, :]
        totals[...] = jnp.zeros(totals.shape, f32)
        count = meta_ref[2 * slots]
        for s in range(slots):
            r, c = meta_ref[s], meta_ref[slots + s]
            at, to = (r, c) if mirrored else (c, r)
            values = jnp.where(s < count, vecs[at], jnp.zeros((), bf16))
            product = lax.dot_general(
                values, tiles_ref[s], (((1,), (0 if mirrored else 1,)), ((), ())), preferred_element_type=f32
            )
            totals[to] += product
        for i, ref in zip(target.inner[::-1], outs, strict=True):
            for half in range(2):
                ref[half * n_vec : (half + 1) * n_vec, :] = totals[i + half * target.bit].astype(ref.dtype)

    return local_call(
        kernel,
        [((2 * n_vec, width), f32 if k == n_out - 1 else bf16) for k in range(n_out)],
        meta, tiles, *pairs, *after,
        specs=[SMEM] + [VMEM] * (1 + n_in + len(after)),
        scratch=[pltpu.VMEM((source.size, n_vec, width), bf16), pltpu.VMEM((target.size, n_vec, width), f32)],
        flops=slots * 2 * n_vec * width * width,
        nbytes=slots * width * width * 2,
    )[::-1]


def body(start_vecs, blocks, block_rows, block_cols, block_count):
    n_vec, width = start_vecs.shape[0], start_vecs.shape[4]
    rows_axis = Axis("row", lax.axis_size("row") // 2)
    cols_axis = Axis("col", 1)
    tiles, start_here, meta = prepare(blocks, start_vecs.reshape(n_vec, width), block_rows, block_cols, block_count)
    start = start_vecs.reshape(n_vec, width)
    one, two = (n_vec, width), (2 * n_vec, width)
    low, high = slice(0, n_vec), slice(n_vec, 2 * n_vec)
    n_d, n_m = len(rows_axis.inner), len(cols_axis.inner)

    def products(row_pair, col_pair):
        mirror = slot_products(meta, tiles, rows_axis.spread(row_pair), rows_axis, cols_axis)
        direct = slot_products(meta, tiles, cols_axis.spread(col_pair), cols_axis, rows_axis, mirror[:1])
        return [direct[0], *rows_axis.collect(direct)], [mirror[0], *cols_axis.collect(mirror)]

    def sum_of(refs, rows):
        total = refs[0][rows, :]
        for ref in refs[1:]:
            total = total + ref[rows, :].astype(f32)
        return total

    def get(ref, rows):
        return ref[rows, :].astype(f32)

    start_y, start_x = rows_axis.swap_pair(start), cols_axis.swap_pair(start)

    def join(own_ref, other_ref, out_ref):
        out_ref[low, :] = own_ref[...]
        out_ref[high, :] = other_ref[...]

    (row_pair,) = local_call(join, [(two, bf16)], start_here, start_y)
    (col_pair,) = local_call(join, [(two, bf16)], start_here, start_x)

    d_terms, m_terms = products(row_pair, col_pair)

    def partial_sums(*refs):
        d_in, m_in = refs[:n_d], refs[n_d : n_d + n_m]
        to_diag, to_x, to_y, d_keep, m_keep = refs[n_d + n_m :]
        d_own, d_other = sum_of(d_in, low), sum_of(d_in, high)
        m_own, m_other = sum_of(m_in, low), sum_of(m_in, high)
        d_keep[low, :] = d_own
        d_keep[high, :] = d_other
        m_keep[low, :] = m_own
        m_keep[high, :] = m_other
        both = (d_own + m_own).astype(bf16)
        d_other, m_other = d_other.astype(bf16), m_other.astype(bf16)
        to_y[low, :] = d_other
        to_y[high, :] = both
        to_x[low, :] = m_other
        to_x[high, :] = both
        to_diag[low, :] = d_other
        to_diag[high, :] = m_other

    to_diag, to_x, to_y, d_keep, m_keep = local_call(
        partial_sums,
        [(two, bf16), (two, bf16), (two, bf16), (two, f32), (two, f32)],
        *d_terms, *m_terms,
    )
    n_row, n_col = rows_axis.size, cols_axis.size
    diagonal = [
        (i * n_col + j, (i ^ rows_axis.bit) * n_col + (j ^ cols_axis.bit)) for i in range(n_row) for j in range(n_col)
    ]
    from_diag = lax.ppermute(to_diag, ("row", "col"), diagonal)
    from_x = cols_axis.swap_pair(to_x)
    from_y = rows_axis.swap_pair(to_y)

    def first_update(diag_ref, x_ref, y_ref, d_ref, m_ref, cur, cur_y, cur_x, row_out, col_out):
        def advance(applied, ref):
            shifted = (applied - shift_center * ref[...].astype(f32)) / half_width
            return shifted.astype(bf16)

        own = d_ref[low, :] + m_ref[low, :] + get(y_ref, low) + get(x_ref, low)
        own = advance(own, cur)
        row_out[low, :] = own
        col_out[low, :] = own
        row_out[high, :] = advance(d_ref[high, :] + get(y_ref, high) + get(diag_ref, high), cur_y)
        col_out[high, :] = advance(m_ref[high, :] + get(x_ref, high) + get(diag_ref, low), cur_x)

    row_pair, col_pair = local_call(
        first_update, [(two, bf16), (two, bf16)],
        from_diag, from_x, from_y, d_keep, m_keep, start_here, start_y, start_x,
    )

    d_terms, m_terms = products(row_pair, col_pair)

    def last_sums(*refs):
        d_in, m_in, (keep, to_y, to_x) = refs[:n_d], refs[n_d : n_d + n_m], refs[n_d + n_m :]
        keep[...] = sum_of(d_in, low) + sum_of(m_in, low)
        to_y[...] = sum_of(d_in, high).astype(bf16)
        to_x[...] = sum_of(m_in, high).astype(bf16)

    keep, to_y, to_x = local_call(last_sums, [(one, f32), (one, bf16), (one, bf16)], *d_terms, *m_terms)
    from_x = cols_axis.swap_pair(to_x)
    from_y = rows_axis.swap_pair(to_y)

    def last_update(keep_ref, y_ref, x_ref, pair_ref, prev_ref, first_out, second_out):
        current = pair_ref[low, :]
        applied = keep_ref[...] + y_ref[...].astype(f32) + x_ref[...].astype(f32)
        shifted = (applied - shift_center * current.astype(f32)) / half_width
        shifted = 2.0 * shifted - prev_ref[...].astype(f32)
        first_out[...] = current
        second_out[...] = shifted.astype(bf16)

    first, second = local_call(
        last_update, [(one, bf16), (one, bf16)], keep, from_y, from_x, row_pair, start_here
    )
    shape = start_vecs.shape
    return first.reshape(shape), second.reshape(shape)


def solution(mesh):
    return jax.shard_map(
        body,
        mesh=mesh,
        in_specs=(
            P(None, None, "row", "col", None),
            P("row", "col", None, None, None),
            P("row", "col", None),
            P("row", "col", None),
            P("row", "col"),
        ),
        out_specs=(P(None, None, "row", "col", None), P(None, None, "row", "col", None)),
        check_vma=False,
    )
```

time: 380 us -> 50.9 us (0.13)
  waiting for transfers between devices: 207 us -> 14.9 us
  blocking collectives: 74.7 us -> 0 us
  loops' own time: 39 us -> 0 us
  starting transfers between devices: 0.16 us -> 28.3 us
  local copies, waits for them, and re-layouts: 20.8 us -> 0 us
  matrix products: 20.3 us -> 0 us
  between operations: 13.8 us -> 1.43 us
  Pallas kernels: 0 us -> 6.18 us
  other arithmetic: 5.01 us -> 0 us
    reduce_scatter x4 -> x0, waiting for transfers between devices: 207 us -> none  [the longest x2 129 us: body(): lax.psum_scatter(mirror_terms.astype(jnp.bfloat16), 'col', scatter_dimens...]
    all_gather x4 -> x0, blocking collectives: 74.7 us -> none  [the longest x2 63.6 us: body(): mirror_panel = lax.all_gather(current, 'col', axis=3, tiled=True)]
    another operation x2 -> x0, loops' own time: 39 us -> none  [joint_loop(): return lax.fori_loop(0, live_count, slot_step, initial)]
    ppermute x0 -> x23, starting transfers between devices: none -> 28.3 us  [the longest x22 27.1 us: swap(): lax.ppermute(value, axis, [(i, i ^ pattern) for i in range(lax.axis_size(...]
    dynamic_slice x24 -> x0, local copies, waits for them, and re-layouts: 20.7 us -> none  [the longest x8 10.3 us: slot_step(): row_at = row_list[slot_at]]
    dot_general x16 -> x0, matrix products: 20.3 us -> none  [the longest x8 10.4 us: owner_product(): lax.dot_general(source, block_tile, (((1,), (1,)), ((), ())), preferred_e...]
    ppermute x0 -> x23, waiting for transfers between devices: none -> 14.9 us  [the longest x22 12.6 us: swap(): lax.ppermute(value, axis, [(i, i ^ pattern) for i in range(lax.axis_size(...]
    pallas_call x0 -> x11, Pallas kernels: none -> 6.18 us  [the longest x10 4.24 us: local_call(): pl.pallas_call(kernel, out_shape=[jax.ShapeDtypeStruct(s, d) for s, d in...]
  transfers between devices with their start and end apart: 4 -> 23, of which waited for: 4 -> 8; matrix products, arithmetic and copies ran while one was open for 0% -> 0% of each run, Pallas kernels for 0% -> 11%
where the time goes in v2:
time: 50.9 us; the launch traced here: 50.7 us
  starting transfers between devices  28.3 us (56%)
  waiting for transfers between devices  14.9 us (29%)
  Pallas kernels  6.18 us (12%)
  between operations  1.43 us (3%)
    ppermute x22, starting transfers between devices, swap(): lax.ppermute(value, axis, [(i, i ^ pattern) for i in range(lax.axis_size(...  27.1 us
    ppermute x22, waiting for transfers between devices, swap(): lax.ppermute(value, axis, [(i, i ^ pattern) for i in range(lax.axis_size(...  12.6 us
    pallas_call x10, Pallas kernels, local_call(): pl.pallas_call(kernel, out_shape=[jax.ShapeDtypeStruct(s, d) for s, d in...  4.24 us
    ppermute x1, waiting for transfers between devices, body(): from_diag = lax.ppermute(to_diag, ('row', 'col'), diagonal)  2.24 us
    pallas_call x1, Pallas kernels, prepare(): pl.pallas_call(kernel, out_shape=[pltpu.VMEM(blocks.shape[2:], blocks.dty...  1.93 us
    ppermute x1, starting transfers between devices, body(): from_diag = lax.ppermute(to_diag, ('row', 'col'), diagonal)  1.11 us
  transfers between devices with their start and end apart: 23, of which 8 were waited for; matrix products, arithmetic and copies ran while one was open for 0% of the time, Pallas kernels for 11%

profile of v2, /device:TPU:0, one launch (start us, length us, event | category | flops | bytes accessed | tf_op | source)
XLA Modules:
  0.0 50.7 jit_solution(4701782828224565292)
XLA Ops:
  0.6 3.0 %collective-permute-start.4 = (bf16[32,512]{1,0:T(8,128)(2,1)}, bf16[32,512]{1,0:T(8,128)(2,1)S(1)}, u32[]{:S(2)}, u32[]{:S(2)}) collective-permute-start(bf16[32,512]{1,0:T(8,128)(2,1)} %bitcast.3), channel_id=1, source_target_pairs={{0,16},{8,24},{16,0},{24,8},{1,17},{9,25},{17,1},{25,9},{2,18},{10... | collective-permute-start | bytes 98312 | tf_op jit(solution)/shard_map/ppermute | solution.py:19
  3.7 1.5 %collective-permute-start = (bf16[32,512]{1,0:T(8,128)(2,1)}, bf16[32,512]{1,0:T(8,128)(2,1)S(1)}, u32[]{:S(2)}, u32[]{:S(2)}) collective-permute-start(bf16[32,512]{1,0:T(8,128)(2,1)} %bitcast.4), channel_id=1, source_target_pairs={{0,1},{1,0},{2,3},{3,2},{4,5},{5,4},{6,7},{7,6},{8,9},{9,8},{10,11... | collective-permute-start | bytes 98312 | tf_op jit(solution)/shard_map/ppermute | solution.py:19
  5.8 1.9 %shard_map.68 = (bf16[6,512,512]{2,1,0:T(8,128)(2,1)S(1)}, bf16[32,512]{1,0:T(8,128)(2,1)S(1)}, s32[13]{0:T(128)S(4)}) custom-call(s32[1,1]{1,0:T(1,128)S(6)} %copy.7.count_ref, s32[1,1,6]{2,1,0:T(1,128)} %rows_hbm.1, s32[1,1,6]{2,1,0:T(1,128)} %cols_hbm.1, bf16[1,1,6,512,512]{4,3,2,1,0:T(8,128)(2,1)} %blocks_hbm.1, bf16[32,512]{1,0:T(8,128)(2,1)} %bitcast.5), custom_call_target="tpu_custom_call" | custom-call | flops 1000 | bytes 6291456 | tf_op jit(solution)/shard_map/pallas_call | solution.py:58
  7.7 0.0 collective-permute-done.4.other_ref.cur_y
  7.8 0.1 collective-permute-start.5
  7.8 0.0 collective-permute-done.other_ref.cur_x
  7.9 3.7 %collective-permute-start.3 = (bf16[64,512]{1,0:T(8,128)(2,1)S(1)}, bf16[64,512]{1,0:T(8,128)(2,1)S(1)}, u32[]{:S(2)}, u32[]{:S(2)}) collective-permute-start(bf16[64,512]{1,0:T(8,128)(2,1)S(1)} %shard_map.69.refs_0_), channel_id=1, source_target_pairs={{0,6},{1,7},{2,4},{3,5},{4,2},{5,3},{6,0},{7,1},{8,14},{9,15},{10,... | collective-permute-start | bytes 196616 | tf_op jit(solution)/shard_map/ppermute | solution.py:19
  11.5 0.0 collective-permute-start.2
  11.5 0.8 %collective-permute-start.1 = (bf16[64,512]{1,0:T(8,128)(2,1)S(1)}, bf16[64,512]{1,0:T(8,128)(2,1)S(1)}, u32[]{:S(2)}, u32[]{:S(2)}) collective-permute-start(bf16[64,512]{1,0:T(8,128)(2,1)S(1)} %shard_map.69.refs_0_), channel_id=1, source_target_pairs={{0,2},{1,3},{2,0},{3,1},{4,6},{5,7},{6,4},{7,5},{8,10},{9,11},{10,... | collective-permute-start | bytes 196616 | tf_op jit(solution)/shard_map/ppermute | solution.py:19
  12.3 0.0 collective-permute-done.5.refs_1_
  12.3 0.7 %shard_map.71 = (bf16[64,512]{1,0:T(8,128)(2,1)S(1)}, bf16[64,512]{1,0:T(8,128)(2,1)S(1)}, bf16[64,512]{1,0:T(8,128)(2,1)S(1)}, f32[64,512]{1,0:T(8,128)S(1)}) custom-call(s32[13]{0:T(128)S(4)} %get-tuple-element.29.meta_ref, bf16[6,512,512]{2,1,0:T(8,128)(2,1)S(1)} %get-tuple-element.30.tiles_ref, bf16[64,512]{1,0:T(8,128)(2,1)S(1)} %shard_map.70.refs_0_, ...), custom_call_target="tpu_custom_call" | custom-call | flops 100663296 | bytes 3145728 | tf_op jit(solution)/shard_map/pallas_call | solution.py:23
  13.0 3.7 %collective-permute-start.7 = (bf16[64,512]{1,0:T(8,128)(2,1)S(1)}, bf16[64,512]{1,0:T(8,128)(2,1)S(1)}, u32[]{:S(2)}, u32[]{:S(2)}) collective-permute-start(bf16[64,512]{1,0:T(8,128)(2,1)S(1)} %get-tuple-element.35), channel_id=1, source_target_pairs={{0,6},{1,7},{2,4},{3,5},{4,2},{5,3},{6,0},{7,1},{8,14},{9,15},{10,... | collective-permute-start | bytes 196616 | tf_op jit(solution)/shard_map/ppermute | solution.py:19
  16.7 0.0 collective-permute-start.8
  16.7 0.0 collective-permute-done.3.refs_3_
  16.7 0.8 %collective-permute-start.9 = (bf16[64,512]{1,0:T(8,128)(2,1)S(1)}, bf16[64,512]{1,0:T(8,128)(2,1)S(1)}, u32[]{:S(2)}, u32[]{:S(2)}) collective-permute-start(bf16[64,512]{1,0:T(8,128)(2,1)S(1)} %get-tuple-element.37), channel_id=1, source_target_pairs={{0,2},{1,3},{2,0},{3,1},{4,6},{5,7},{6,4},{7,5},{8,10},{9,11},{10,... | collective-permute-start | bytes 196616 | tf_op jit(solution)/shard_map/ppermute | solution.py:19
  17.5 3.4 %collective-permute-done.2.refs_2_ = bf16[64,512]{1,0:T(8,128)(2,1)S(1)} collective-permute-done((bf16[64,512]{1,0:T(8,128)(2,1)S(1)}, bf16[64,512]{1,0:T(8,128)(2,1)S(1)}, u32[]{:S(2)}, u32[]{:S(2)}) %collective-permute-start.2) | collective-permute-done | bytes 65568 | tf_op jit(solution)/shard_map/ppermute | solution.py:19
  20.9 0.0 collective-permute-done.1.refs_1_
  20.9 1.0 %shard_map.72 = (bf16[64,512]{1,0:T(8,128)(2,1)S(1)}, f32[64,512]{1,0:T(8,128)S(1)}) custom-call(s32[13]{0:T(128)S(4)} %get-tuple-element.29.meta_ref, bf16[6,512,512]{2,1,0:T(8,128)(2,1)S(1)} %get-tuple-element.30.tiles_ref, bf16[64,512]{1,0:T(8,128)(2,1)S(1)} %shard_map.69.refs_0_, bf16[64,512]{1,0:T(8,128)(2,1)S(1)} %collective-permute-done.1.refs_1_, ...), custom_call_target="tpu_custom_call" | custom-call | flops 100663296 | bytes 3145728 | tf_op jit(solution)/shard_map/pallas_call | solution.py:23
  21.9 0.1 collective-permute-start.6
  22.0 0.0 collective-permute-done.7.refs_3_
  22.0 1.3 %collective-permute-done.8.refs_4_ = bf16[64,512]{1,0:T(8,128)(2,1)S(1)} collective-permute-done((bf16[64,512]{1,0:T(8,128)(2,1)S(1)}, bf16[64,512]{1,0:T(8,128)(2,1)S(1)}, u32[]{:S(2)}, u32[]{:S(2)}) %collective-permute-start.8) | collective-permute-done | bytes 65568 | tf_op jit(solution)/shard_map/ppermute | solution.py:19
  23.3 0.0 collective-permute-done.9.refs_5_
  23.3 0.0 collective-permute-done.6.refs_1_
  23.3 0.1 shard_map.73
  23.3 1.1 %collective-permute-start.10 = (bf16[64,512]{1,0:T(8,128)(2,1)S(1)}, bf16[64,512]{1,0:T(8,128)(2,1)S(1)}, u32[]{:S(2)}, u32[]{:S(2)}) collective-permute-start(bf16[64,512]{1,0:T(8,128)(2,1)S(1)} %get-tuple-element.38), channel_id=1, source_target_pairs={{0,17},{1,16},{2,19},{3,18},{4,21},{5,20},{6,23},{7,22},{8,25},{9,... | collective-permute-start | bytes 196616 | tf_op jit(solution)/shard_map/ppermute | solution.py:188
  24.4 0.9 %collective-permute-start.11 = (bf16[64,512]{1,0:T(8,128)(2,1)S(1)}, bf16[64,512]{1,0:T(8,128)(2,1)S(1)}, u32[]{:S(2)}, u32[]{:S(2)}) collective-permute-start(bf16[64,512]{1,0:T(8,128)(2,1)S(1)} %get-tuple-element.39), channel_id=1, source_target_pairs={{0,1},{1,0},{2,3},{3,2},{4,5},{5,4},{6,7},{7,6},{8,9},{9,8},{10,11... | collective-permute-start | bytes 196616 | tf_op jit(solution)/shard_map/ppermute | solution.py:19
  25.4 1.5 %collective-permute-start.12 = (bf16[64,512]{1,0:T(8,128)(2,1)S(1)}, bf16[64,512]{1,0:T(8,128)(2,1)S(1)}, u32[]{:S(2)}, u32[]{:S(2)}) collective-permute-start(bf16[64,512]{1,0:T(8,128)(2,1)S(1)} %get-tuple-element.40), channel_id=1, source_target_pairs={{0,16},{8,24},{16,0},{24,8},{1,17},{9,25},{17,1},{25,9},{2,18},{10... | collective-permute-start | bytes 196616 | tf_op jit(solution)/shard_map/ppermute | solution.py:19
  26.9 2.2 %collective-permute-done.10.diag_ref = bf16[64,512]{1,0:T(8,128)(2,1)S(1)} collective-permute-done((bf16[64,512]{1,0:T(8,128)(2,1)S(1)}, bf16[64,512]{1,0:T(8,128)(2,1)S(1)}, u32[]{:S(2)}, u32[]{:S(2)}) %collective-permute-start.10) | collective-permute-done | bytes 65568 | tf_op jit(solution)/shard_map/ppermute | solution.py:188
  29.1 0.0 collective-permute-done.11.x_ref
  29.1 0.7 %collective-permute-done.12.y_ref = bf16[64,512]{1,0:T(8,128)(2,1)S(1)} collective-permute-done((bf16[64,512]{1,0:T(8,128)(2,1)S(1)}, bf16[64,512]{1,0:T(8,128)(2,1)S(1)}, u32[]{:S(2)}, u32[]{:S(2)}) %collective-permute-start.12) | collective-permute-done | bytes 65568 | tf_op jit(solution)/shard_map/ppermute | solution.py:19
  29.8 0.1 shard_map.74
  29.9 0.1 collective-permute-start.16
  30.0 2.4 %collective-permute-start.15 = (bf16[64,512]{1,0:T(8,128)(2,1)S(1)}, bf16[64,512]{1,0:T(8,128)(2,1)S(1)}, u32[]{:S(2)}, u32[]{:S(2)}) collective-permute-start(bf16[64,512]{1,0:T(8,128)(2,1)S(1)} %get-tuple-element.43.refs_0_), channel_id=1, source_target_pairs={{0,6},{1,7},{2,4},{3,5},{4,2},{5,3},{6,0},{7,1},{8,14},{9,15},{10,... | collective-permute-start | bytes 196616 | tf_op jit(solution)/shard_map/ppermute | solution.py:19
  32.3 0.0 collective-permute-start.14
  32.3 2.1 %collective-permute-start.13 = (bf16[64,512]{1,0:T(8,128)(2,1)S(1)}, bf16[64,512]{1,0:T(8,128)(2,1)S(1)}, u32[]{:S(2)}, u32[]{:S(2)}) collective-permute-start(bf16[64,512]{1,0:T(8,128)(2,1)S(1)} %get-tuple-element.43.refs_0_), channel_id=1, source_target_pairs={{0,2},{1,3},{2,0},{3,1},{4,6},{5,7},{6,4},{7,5},{8,10},{9,11},{10,... | collective-permute-start | bytes 196616 | tf_op jit(solution)/shard_map/ppermute | solution.py:19
  34.4 0.0 collective-permute-done.16.refs_1_
  34.4 0.7 %shard_map.75 = (bf16[64,512]{1,0:T(8,128)(2,1)S(1)}, bf16[64,512]{1,0:T(8,128)(2,1)S(1)}, bf16[64,512]{1,0:T(8,128)(2,1)S(1)}, f32[64,512]{1,0:T(8,128)S(1)}) custom-call(s32[13]{0:T(128)S(4)} %get-tuple-element.29.meta_ref, bf16[6,512,512]{2,1,0:T(8,128)(2,1)S(1)} %get-tuple-element.30.tiles_ref, bf16[64,512]{1,0:T(8,128)(2,1)S(1)} %get-tuple-element.44.refs_0_.pair_ref, ...), custom_call_target="tpu_custom_call" | custom-call | flops 100663296 | bytes 3145728 | tf_op jit(solution)/shard_map/pallas_call | solution.py:23
  35.1 2.4 %collective-permute-start.18 = (bf16[64,512]{1,0:T(8,128)(2,1)S(1)}, bf16[64,512]{1,0:T(8,128)(2,1)S(1)}, u32[]{:S(2)}, u32[]{:S(2)}) collective-permute-start(bf16[64,512]{1,0:T(8,128)(2,1)S(1)} %get-tuple-element.48), channel_id=1, source_target_pairs={{0,6},{1,7},{2,4},{3,5},{4,2},{5,3},{6,0},{7,1},{8,14},{9,15},{10,... | collective-permute-start | bytes 196616 | tf_op jit(solution)/shard_map/ppermute | solution.py:19
  37.5 0.0 collective-permute-start.19
  37.5 0.0 collective-permute-done.15.refs_3_
  37.5 2.1 %collective-permute-start.20 = (bf16[64,512]{1,0:T(8,128)(2,1)S(1)}, bf16[64,512]{1,0:T(8,128)(2,1)S(1)}, u32[]{:S(2)}, u32[]{:S(2)}) collective-permute-start(bf16[64,512]{1,0:T(8,128)(2,1)S(1)} %get-tuple-element.50), channel_id=1, source_target_pairs={{0,2},{1,3},{2,0},{3,1},{4,6},{5,7},{6,4},{7,5},{8,10},{9,11},{10,... | collective-permute-start | bytes 196616 | tf_op jit(solution)/shard_map/ppermute | solution.py:19
  39.6 0.0 collective-permute-done.14.refs_2_
  39.6 0.0 collective-permute-done.13.refs_1_
  39.6 1.0 %shard_map.76 = (bf16[64,512]{1,0:T(8,128)(2,1)S(1)}, f32[64,512]{1,0:T(8,128)S(1)}) custom-call(s32[13]{0:T(128)S(4)} %get-tuple-element.29.meta_ref, bf16[6,512,512]{2,1,0:T(8,128)(2,1)S(1)} %get-tuple-element.30.tiles_ref, bf16[64,512]{1,0:T(8,128)(2,1)S(1)} %get-tuple-element.43.refs_0_, bf16[64,512]{1,0:T(8,128)(2,1)S(1)} %collective-permute-done.13.refs_1_, ...), custom_call_target="tpu_custom_call" | custom-call | flops 100663296 | bytes 3145728 | tf_op jit(solution)/shard_map/pallas_call | solution.py:23
  40.6 0.1 collective-permute-start.17
  40.7 0.7 %collective-permute-done.18.refs_3_ = bf16[64,512]{1,0:T(8,128)(2,1)S(1)} collective-permute-done((bf16[64,512]{1,0:T(8,128)(2,1)S(1)}, bf16[64,512]{1,0:T(8,128)(2,1)S(1)}, u32[]{:S(2)}, u32[]{:S(2)}) %collective-permute-start.18) | collective-permute-done | bytes 65568 | tf_op jit(solution)/shard_map/ppermute | solution.py:19
  41.4 3.3 %collective-permute-done.19.refs_4_ = bf16[64,512]{1,0:T(8,128)(2,1)S(1)} collective-permute-done((bf16[64,512]{1,0:T(8,128)(2,1)S(1)}, bf16[64,512]{1,0:T(8,128)(2,1)S(1)}, u32[]{:S(2)}, u32[]{:S(2)}) %collective-permute-start.19) | collective-permute-done | bytes 65568 | tf_op jit(solution)/shard_map/ppermute | solution.py:19
  44.7 0.0 collective-permute-done.20.refs_5_
  44.7 0.0 collective-permute-done.17.refs_1_
  44.7 1.4 %collective-permute-start.21 = (bf16[32,512]{1,0:T(8,128)(2,1)S(1)}, bf16[32,512]{1,0:T(8,128)(2,1)S(1)}, u32[]{:S(2)}, u32[]{:S(2)}) collective-permute-start(bf16[32,512]{1,0:T(8,128)(2,1)S(1)} %get-tuple-element.52), channel_id=1, source_target_pairs={{0,16},{8,24},{16,0},{24,8},{1,17},{9,25},{17,1},{25,9},{2,18},{10... | collective-permute-start | bytes 98312 | tf_op jit(solution)/shard_map/ppermute | solution.py:19
  46.1 0.7 %collective-permute-start.22 = (bf16[32,512]{1,0:T(8,128)(2,1)S(1)}, bf16[32,512]{1,0:T(8,128)(2,1)S(1)}, u32[]{:S(2)}, u32[]{:S(2)}) collective-permute-start(bf16[32,512]{1,0:T(8,128)(2,1)S(1)} %get-tuple-element.53), channel_id=1, source_target_pairs={{0,1},{1,0},{2,3},{3,2},{4,5},{5,4},{6,7},{7,6},{8,9},{9,8},{10,11... | collective-permute-start | bytes 98312 | tf_op jit(solution)/shard_map/ppermute | solution.py:19
  46.8 1.9 %collective-permute-done.21.y_ref = bf16[32,512]{1,0:T(8,128)(2,1)S(1)} collective-permute-done((bf16[32,512]{1,0:T(8,128)(2,1)S(1)}, bf16[32,512]{1,0:T(8,128)(2,1)S(1)}, u32[]{:S(2)}, u32[]{:S(2)}) %collective-permute-start.21) | collective-permute-done | bytes 32800 | tf_op jit(solution)/shard_map/ppermute | solution.py:19
  48.7 1.3 %collective-permute-done.22.x_ref = bf16[32,512]{1,0:T(8,128)(2,1)S(1)} collective-permute-done((bf16[32,512]{1,0:T(8,128)(2,1)S(1)}, bf16[32,512]{1,0:T(8,128)(2,1)S(1)}, u32[]{:S(2)}, u32[]{:S(2)}) %collective-permute-start.22) | collective-permute-done | bytes 32800 | tf_op jit(solution)/shard_map/ppermute | solution.py:19
  50.1 0.6 %shard_map.78 = (bf16[32,512]{1,0:T(8,128)(2,1)}, bf16[32,512]{1,0:T(8,128)(2,1)}) custom-call(f32[32,512]{1,0:T(8,128)S(1)} %get-tuple-element.51.keep_ref, bf16[32,512]{1,0:T(8,128)(2,1)S(1)} %collective-permute-done.21.y_ref, bf16[32,512]{1,0:T(8,128)(2,1)S(1)} %collective-permute-done.22.x_ref, bf16[64,512]{1,0:T(8,128)(2,1)S(1)} %get-tuple-element.44.refs_0_.pair_ref, ...), custom_call_target="tpu_custom_call" | custom-call | flops 1000 | bytes 100000 | tf_op jit(solution)/shard_map/pallas_call | solution.py:23
  (3 shorter events, 0.1 us)
Async XLA Ops:
  0.6 7.1 %collective-permute-start.4 = (bf16[32,512]{1,0:T(8,128)(2,1)}, bf16[32,512]{1,0:T(8,128)(2,1)S(1)}, u32[]{:S(2)}, u32[]{:S(2)}) collective-permute-start(bf16[32,512]{1,0:T(8,128)(2,1)} %bitcast.3), channel_id=1, source_target_pairs={{0,16},{8,24},{16,0},{24,8},{1,17},{9,25},{17,1},{25,9},{2,18},{10... | collective-permute-start | bytes 98312 | tf_op jit(solution)/shard_map/ppermute | solution.py:19
  3.7 4.2 %collective-permute-start = (bf16[32,512]{1,0:T(8,128)(2,1)}, bf16[32,512]{1,0:T(8,128)(2,1)S(1)}, u32[]{:S(2)}, u32[]{:S(2)}) collective-permute-start(bf16[32,512]{1,0:T(8,128)(2,1)} %bitcast.4), channel_id=1, source_target_pairs={{0,1},{1,0},{2,3},{3,2},{4,5},{5,4},{6,7},{7,6},{8,9},{9,8},{10,11... | collective-permute-start | bytes 98312 | tf_op jit(solution)/shard_map/ppermute | solution.py:19
  7.8 4.6 %collective-permute-start.5 = (bf16[64,512]{1,0:T(8,128)(2,1)S(1)}, bf16[64,512]{1,0:T(8,128)(2,1)S(1)}, u32[]{:S(2)}, u32[]{:S(2)}) collective-permute-start(bf16[64,512]{1,0:T(8,128)(2,1)S(1)} %shard_map.70.refs_0_), channel_id=1, source_target_pairs={{0,8},{8,0},{16,24},{24,16},{1,9},{9,1},{17,25},{25,17},{2,10},{10... | collective-permute-start | bytes 196616 | tf_op jit(solution)/shard_map/ppermute | solution.py:19
  7.9 8.8 %collective-permute-start.3 = (bf16[64,512]{1,0:T(8,128)(2,1)S(1)}, bf16[64,512]{1,0:T(8,128)(2,1)S(1)}, u32[]{:S(2)}, u32[]{:S(2)}) collective-permute-start(bf16[64,512]{1,0:T(8,128)(2,1)S(1)} %shard_map.69.refs_0_), channel_id=1, source_target_pairs={{0,6},{1,7},{2,4},{3,5},{4,2},{5,3},{6,0},{7,1},{8,14},{9,15},{10,... | collective-permute-start | bytes 196616 | tf_op jit(solution)/shard_map/ppermute | solution.py:19
  11.5 9.3 %collective-permute-start.2 = (bf16[64,512]{1,0:T(8,128)(2,1)S(1)}, bf16[64,512]{1,0:T(8,128)(2,1)S(1)}, u32[]{:S(2)}, u32[]{:S(2)}) collective-permute-start(bf16[64,512]{1,0:T(8,128)(2,1)S(1)} %shard_map.69.refs_0_), channel_id=1, source_target_pairs={{0,4},{1,5},{2,6},{3,7},{4,0},{5,1},{6,2},{7,3},{8,12},{9,13},{10,... | collective-permute-start | bytes 196616 | tf_op jit(solution)/shard_map/ppermute | solution.py:19
  11.5 9.3 %collective-permute-start.1 = (bf16[64,512]{1,0:T(8,128)(2,1)S(1)}, bf16[64,512]{1,0:T(8,128)(2,1)S(1)}, u32[]{:S(2)}, u32[]{:S(2)}) collective-permute-start(bf16[64,512]{1,0:T(8,128)(2,1)S(1)} %shard_map.69.refs_0_), channel_id=1, source_target_pairs={{0,2},{1,3},{2,0},{3,1},{4,6},{5,7},{6,4},{7,5},{8,10},{9,11},{10,... | collective-permute-start | bytes 196616 | tf_op jit(solution)/shard_map/ppermute | solution.py:19
  13.0 9.0 %collective-permute-start.7 = (bf16[64,512]{1,0:T(8,128)(2,1)S(1)}, bf16[64,512]{1,0:T(8,128)(2,1)S(1)}, u32[]{:S(2)}, u32[]{:S(2)}) collective-permute-start(bf16[64,512]{1,0:T(8,128)(2,1)S(1)} %get-tuple-element.35), channel_id=1, source_target_pairs={{0,6},{1,7},{2,4},{3,5},{4,2},{5,3},{6,0},{7,1},{8,14},{9,15},{10,... | collective-permute-start | bytes 196616 | tf_op jit(solution)/shard_map/ppermute | solution.py:19
  16.7 6.6 %collective-permute-start.8 = (bf16[64,512]{1,0:T(8,128)(2,1)S(1)}, bf16[64,512]{1,0:T(8,128)(2,1)S(1)}, u32[]{:S(2)}, u32[]{:S(2)}) collective-permute-start(bf16[64,512]{1,0:T(8,128)(2,1)S(1)} %get-tuple-element.36), channel_id=1, source_target_pairs={{0,4},{1,5},{2,6},{3,7},{4,0},{5,1},{6,2},{7,3},{8,12},{9,13},{10,... | collective-permute-start | bytes 196616 | tf_op jit(solution)/shard_map/ppermute | solution.py:19
  16.7 6.6 %collective-permute-start.9 = (bf16[64,512]{1,0:T(8,128)(2,1)S(1)}, bf16[64,512]{1,0:T(8,128)(2,1)S(1)}, u32[]{:S(2)}, u32[]{:S(2)}) collective-permute-start(bf16[64,512]{1,0:T(8,128)(2,1)S(1)} %get-tuple-element.37), channel_id=1, source_target_pairs={{0,2},{1,3},{2,0},{3,1},{4,6},{5,7},{6,4},{7,5},{8,10},{9,11},{10,... | collective-permute-start | bytes 196616 | tf_op jit(solution)/shard_map/ppermute | solution.py:19
  21.9 1.4 %collective-permute-start.6 = (bf16[64,512]{1,0:T(8,128)(2,1)S(1)}, bf16[64,512]{1,0:T(8,128)(2,1)S(1)}, u32[]{:S(2)}, u32[]{:S(2)}) collective-permute-start(bf16[64,512]{1,0:T(8,128)(2,1)S(1)} %get-tuple-element.34), channel_id=1, source_target_pairs={{0,8},{8,0},{16,24},{24,16},{1,9},{9,1},{17,25},{25,17},{2,10},{10... | collective-permute-start | bytes 196616 | tf_op jit(solution)/shard_map/ppermute | solution.py:19
  23.3 5.8 %collective-permute-start.10 = (bf16[64,512]{1,0:T(8,128)(2,1)S(1)}, bf16[64,512]{1,0:T(8,128)(2,1)S(1)}, u32[]{:S(2)}, u32[]{:S(2)}) collective-permute-start(bf16[64,512]{1,0:T(8,128)(2,1)S(1)} %get-tuple-element.38), channel_id=1, source_target_pairs={{0,17},{1,16},{2,19},{3,18},{4,21},{5,20},{6,23},{7,22},{8,25},{9,... | collective-permute-start | bytes 196616 | tf_op jit(solution)/shard_map/ppermute | solution.py:188
  24.4 4.7 %collective-permute-start.11 = (bf16[64,512]{1,0:T(8,128)(2,1)S(1)}, bf16[64,512]{1,0:T(8,128)(2,1)S(1)}, u32[]{:S(2)}, u32[]{:S(2)}) collective-permute-start(bf16[64,512]{1,0:T(8,128)(2,1)S(1)} %get-tuple-element.39), channel_id=1, source_target_pairs={{0,1},{1,0},{2,3},{3,2},{4,5},{5,4},{6,7},{7,6},{8,9},{9,8},{10,11... | collective-permute-start | bytes 196616 | tf_op jit(solution)/shard_map/ppermute | solution.py:19
  25.4 4.5 %collective-permute-start.12 = (bf16[64,512]{1,0:T(8,128)(2,1)S(1)}, bf16[64,512]{1,0:T(8,128)(2,1)S(1)}, u32[]{:S(2)}, u32[]{:S(2)}) collective-permute-start(bf16[64,512]{1,0:T(8,128)(2,1)S(1)} %get-tuple-element.40), channel_id=1, source_target_pairs={{0,16},{8,24},{16,0},{24,8},{1,17},{9,25},{17,1},{25,9},{2,18},{10... | collective-permute-start | bytes 196616 | tf_op jit(solution)/shard_map/ppermute | solution.py:19
  29.9 4.5 %collective-permute-start.16 = (bf16[64,512]{1,0:T(8,128)(2,1)S(1)}, bf16[64,512]{1,0:T(8,128)(2,1)S(1)}, u32[]{:S(2)}, u32[]{:S(2)}) collective-permute-start(bf16[64,512]{1,0:T(8,128)(2,1)S(1)} %get-tuple-element.44.refs_0_.pair_ref), channel_id=1, source_target_pairs={{0,8},{8,0},{16,24},{24,16},{1,9},{9,1},{17,25},{25,17},{2,10},{10... | collective-permute-start | bytes 196616 | tf_op jit(solution)/shard_map/ppermute | solution.py:19
  30.0 7.5 %collective-permute-start.15 = (bf16[64,512]{1,0:T(8,128)(2,1)S(1)}, bf16[64,512]{1,0:T(8,128)(2,1)S(1)}, u32[]{:S(2)}, u32[]{:S(2)}) collective-permute-start(bf16[64,512]{1,0:T(8,128)(2,1)S(1)} %get-tuple-element.43.refs_0_), channel_id=1, source_target_pairs={{0,6},{1,7},{2,4},{3,5},{4,2},{5,3},{6,0},{7,1},{8,14},{9,15},{10,... | collective-permute-start | bytes 196616 | tf_op jit(solution)/shard_map/ppermute | solution.py:19
  32.3 7.2 %collective-permute-start.14 = (bf16[64,512]{1,0:T(8,128)(2,1)S(1)}, bf16[64,512]{1,0:T(8,128)(2,1)S(1)}, u32[]{:S(2)}, u32[]{:S(2)}) collective-permute-start(bf16[64,512]{1,0:T(8,128)(2,1)S(1)} %get-tuple-element.43.refs_0_), channel_id=1, source_target_pairs={{0,4},{1,5},{2,6},{3,7},{4,0},{5,1},{6,2},{7,3},{8,12},{9,13},{10,... | collective-permute-start | bytes 196616 | tf_op jit(solution)/shard_map/ppermute | solution.py:19
  32.3 7.2 %collective-permute-start.13 = (bf16[64,512]{1,0:T(8,128)(2,1)S(1)}, bf16[64,512]{1,0:T(8,128)(2,1)S(1)}, u32[]{:S(2)}, u32[]{:S(2)}) collective-permute-start(bf16[64,512]{1,0:T(8,128)(2,1)S(1)} %get-tuple-element.43.refs_0_), channel_id=1, source_target_pairs={{0,2},{1,3},{2,0},{3,1},{4,6},{5,7},{6,4},{7,5},{8,10},{9,11},{10,... | collective-permute-start | bytes 196616 | tf_op jit(solution)/shard_map/ppermute | solution.py:19
  35.1 6.3 %collective-permute-start.18 = (bf16[64,512]{1,0:T(8,128)(2,1)S(1)}, bf16[64,512]{1,0:T(8,128)(2,1)S(1)}, u32[]{:S(2)}, u32[]{:S(2)}) collective-permute-start(bf16[64,512]{1,0:T(8,128)(2,1)S(1)} %get-tuple-element.48), channel_id=1, source_target_pairs={{0,6},{1,7},{2,4},{3,5},{4,2},{5,3},{6,0},{7,1},{8,14},{9,15},{10,... | collective-permute-start | bytes 196616 | tf_op jit(solution)/shard_map/ppermute | solution.py:19
  37.5 7.2 %collective-permute-start.19 = (bf16[64,512]{1,0:T(8,128)(2,1)S(1)}, bf16[64,512]{1,0:T(8,128)(2,1)S(1)}, u32[]{:S(2)}, u32[]{:S(2)}) collective-permute-start(bf16[64,512]{1,0:T(8,128)(2,1)S(1)} %get-tuple-element.49), channel_id=1, source_target_pairs={{0,4},{1,5},{2,6},{3,7},{4,0},{5,1},{6,2},{7,3},{8,12},{9,13},{10,... | collective-permute-start | bytes 196616 | tf_op jit(solution)/shard_map/ppermute | solution.py:19
  37.5 7.2 %collective-permute-start.20 = (bf16[64,512]{1,0:T(8,128)(2,1)S(1)}, bf16[64,512]{1,0:T(8,128)(2,1)S(1)}, u32[]{:S(2)}, u32[]{:S(2)}) collective-permute-start(bf16[64,512]{1,0:T(8,128)(2,1)S(1)} %get-tuple-element.50), channel_id=1, source_target_pairs={{0,2},{1,3},{2,0},{3,1},{4,6},{5,7},{6,4},{7,5},{8,10},{9,11},{10,... | collective-permute-start | bytes 196616 | tf_op jit(solution)/shard_map/ppermute | solution.py:19
  40.6 4.1 %collective-permute-start.17 = (bf16[64,512]{1,0:T(8,128)(2,1)S(1)}, bf16[64,512]{1,0:T(8,128)(2,1)S(1)}, u32[]{:S(2)}, u32[]{:S(2)}) collective-permute-start(bf16[64,512]{1,0:T(8,128)(2,1)S(1)} %get-tuple-element.47), channel_id=1, source_target_pairs={{0,8},{8,0},{16,24},{24,16},{1,9},{9,1},{17,25},{25,17},{2,10},{10... | collective-permute-start | bytes 196616 | tf_op jit(solution)/shard_map/ppermute | solution.py:19
  44.7 4.0 %collective-permute-start.21 = (bf16[32,512]{1,0:T(8,128)(2,1)S(1)}, bf16[32,512]{1,0:T(8,128)(2,1)S(1)}, u32[]{:S(2)}, u32[]{:S(2)}) collective-permute-start(bf16[32,512]{1,0:T(8,128)(2,1)S(1)} %get-tuple-element.52), channel_id=1, source_target_pairs={{0,16},{8,24},{16,0},{24,8},{1,17},{9,25},{17,1},{25,9},{2,18},{10... | collective-permute-start | bytes 98312 | tf_op jit(solution)/shard_map/ppermute | solution.py:19
  46.1 3.9 %collective-permute-start.22 = (bf16[32,512]{1,0:T(8,128)(2,1)S(1)}, bf16[32,512]{1,0:T(8,128)(2,1)S(1)}, u32[]{:S(2)}, u32[]{:S(2)}) collective-permute-start(bf16[32,512]{1,0:T(8,128)(2,1)S(1)} %get-tuple-element.53), channel_id=1, source_target_pairs={{0,1},{1,0},{2,3},{3,2},{4,5},{5,4},{6,7},{7,6},{8,9},{9,8},{10,11... | collective-permute-start | bytes 98312 | tf_op jit(solution)/shard_map/ppermute | solution.py:19

commit v3 on v2

v3 whole, which is shorter than its diff:
```python
import jax
import jax.numpy as jnp
from jax import lax
from jax.experimental import pallas as pl
from jax.experimental.pallas import tpu as pltpu
from jax.sharding import PartitionSpec as P

shift_center = 0.5
half_width = 2.0

VMEM = pl.BlockSpec(memory_space=pltpu.VMEM)
SMEM = pl.BlockSpec(memory_space=pltpu.SMEM)
PARAMS = pltpu.CompilerParams(vmem_limit_bytes=16 * 1024 * 1024)
f32 = jnp.float32
bf16 = jnp.bfloat16


def swap(value, axis, pattern):
    return lax.ppermute(value, axis, [(i, i ^ pattern) for i in range(lax.axis_size(axis))])


def local_call(kernel, shapes, *operands, specs=None, scratch=(), flops=1000, nbytes=100000, params=PARAMS):
    return pl.pallas_call(
        kernel,
        out_shape=[jax.ShapeDtypeStruct(s, d) for s, d in shapes],
        in_specs=specs or [VMEM] * len(operands),
        out_specs=[VMEM] * len(shapes),
        scratch_shapes=scratch,
        compiler_params=params,
        cost_estimate=pl.CostEstimate(flops=flops, bytes_accessed=nbytes, transcendentals=0),
    )(*operands)


def prepare(blocks, start_vecs, block_rows, block_cols, block_count):
    slots = blocks.shape[2]

    def kernel(count_ref, rows_hbm, cols_hbm, blocks_hbm, vecs_hbm, tiles_out, vecs_out, meta_out, rows_ref, cols_ref, sems):
        copies = [
            pltpu.make_async_copy(rows_hbm, rows_ref, sems.at[slots + 1]),
            pltpu.make_async_copy(cols_hbm, cols_ref, sems.at[slots + 2]),
        ]
        copies += [pltpu.make_async_copy(vecs_hbm, vecs_out, sems.at[slots])]
        copies += [pltpu.make_async_copy(blocks_hbm.at[0, 0, s], tiles_out.at[s], sems.at[s]) for s in range(slots)]
        for copy in copies:
            copy.start()
        row_at, col_at = lax.axis_index("row"), lax.axis_index("col")
        for copy in copies[:2]:
            copy.wait()
        count = count_ref[0, 0]
        for s in range(slots):
            meta_out[s] = jnp.where(s < count, rows_ref[0, 0, s] ^ row_at, 0)
            meta_out[slots + s] = jnp.where(s < count, cols_ref[0, 0, s] ^ col_at, 0)
        meta_out[2 * slots] = count
        for copy in copies[2:]:
            copy.wait()

    arrays = (block_rows, block_cols, blocks, start_vecs)
    return pl.pallas_call(
        kernel,
        out_shape=[
            pltpu.VMEM(blocks.shape[2:], blocks.dtype),
            pltpu.VMEM(start_vecs.shape, start_vecs.dtype),
            pltpu.SMEM((2 * slots + 1,), jnp.int32),
        ],
        in_specs=[SMEM] + [pl.BlockSpec(memory_space=pltpu.HBM)] * len(arrays),
        out_specs=[VMEM, VMEM, SMEM],
        scratch_shapes=[pltpu.SMEM(a.shape, a.dtype) for a in arrays[:2]] + [pltpu.SemaphoreType.DMA((slots + 3,))],
        compiler_params=PARAMS,
        cost_estimate=pl.CostEstimate(flops=1000, bytes_accessed=2 * blocks.size * 2, transcendentals=0),
    )(block_count, *[pltpu.with_memory_space_constraint(a, pltpu.HBM) for a in arrays])


def stacked(refs, n_vec):
    return [ref[k * n_vec : (k + 1) * n_vec, :] for ref in refs for k in range(ref.shape[0] // n_vec)]


def put(ref, k, value):
    n_vec = value.shape[0]
    ref[k * n_vec : (k + 1) * n_vec, :] = value.astype(ref.dtype)


def join(first, second, *after):
    rows = first.shape[0]

    def kernel(first_ref, second_ref, *refs):
        out_ref = refs[-1]
        out_ref[:rows, :] = first_ref[...]
        out_ref[rows:, :] = second_ref[...]

    return local_call(kernel, [((2 * rows, first.shape[1]), first.dtype)], first, second, *after)[0]


def gather(pair, at, axis, patterns):
    return [pair] + [swap(pair, axis, pattern) for pattern in patterns], at + [i ^ k for k in patterns for i in at]


def combinations(bits):
    found = [0]
    for bit in bits:
        found += [i | bit for i in found]
    return sorted(found, reverse=True)[:-1]


def shares(at, step):
    mask = 0
    for pattern in step:
        mask |= pattern
    mine = [i for i in at if not i & mask]
    return mine, [[i ^ pattern for i in mine] for pattern in step]


def total(refs, rows=slice(None)):
    value = refs[0][rows, :]
    for ref in refs[1:]:
        value = value + ref[rows, :].astype(f32)
    return value


def scatter(kept, sent, at, axis, steps):
    n_vec, width = kept.shape[0] // len(at), kept.shape[1]
    for step, following in zip(steps, steps[1:] + [None]):
        received = [swap(value, axis, pattern) for value, pattern in zip(sent, step, strict=True)]
        if following is None:
            return [kept, *received]
        mine, theirs = shares(at, following)
        order = at

        def kernel(kept_ref, *refs):
            ins, outs = refs[: len(received)], refs[len(received) :]
            totals = dict(zip(order, stacked([kept_ref], n_vec), strict=True))
            for ref in ins:
                for i, block in zip(order, stacked([ref], n_vec), strict=True):
                    totals[i] = totals[i] + block.astype(f32)
            for out, chosen in zip(outs, [*theirs, mine], strict=True):
                for n, i in enumerate(chosen):
                    put(out, n, totals[i])

        part = (len(mine) * n_vec, width)
        *sent, kept = local_call(kernel, [(part, bf16)] * len(theirs) + [(part, f32)], kept, *received)
        at = mine


def slot_products(meta, tiles, parts, at, targets, step, mirrored, after=()):
    slots, width = tiles.shape[0], tiles.shape[1]
    n_vec = sum(p.shape[0] for p in parts) // len(at)
    n_in = len(parts)
    mine, theirs = shares(list(range(targets)), step)

    def kernel(meta_ref, tiles_ref, *refs):
        ins, (*outs, vecs, totals) = refs[:n_in], refs[n_in + len(after) :]
        for i, block in zip(at, stacked(ins, n_vec), strict=True):
            vecs[i] = block
        totals[...] = jnp.zeros(totals.shape, f32)
        count = meta_ref[2 * slots]
        for s in range(slots):
            r, c = meta_ref[s], meta_ref[slots + s]
            source, target = (r, c) if mirrored else (c, r)
            values = jnp.where(s < count, vecs[source], jnp.zeros((), bf16))
            product = lax.dot_general(
                values, tiles_ref[s], (((1,), (0 if mirrored else 1,)), ((), ())), preferred_element_type=f32
            )
            totals[target] += product
        for out, chosen in zip(outs, [*theirs, mine], strict=True):
            for n, i in enumerate(chosen):
                put(out, n, totals[i])

    part = (len(mine) * n_vec, width)
    *sent, kept = local_call(
        kernel, [(part, bf16)] * len(theirs) + [(part, f32)], meta, tiles, *parts, *after,
        specs=[SMEM] + [VMEM] * (1 + n_in + len(after)),
        scratch=[pltpu.VMEM((len(at), n_vec, width), bf16), pltpu.VMEM((targets, n_vec, width), f32)],
        flops=slots * 2 * n_vec * width * width,
        nbytes=slots * width * width * 2,
    )
    return kept, sent, mine


def body(start_vecs, blocks, block_rows, block_cols, block_count):
    n_vec, width = start_vecs.shape[0], start_vecs.shape[4]
    n_row, n_col = lax.axis_size("row"), lax.axis_size("col")
    row_bits = [1 << k for k in range(n_row.bit_length() - 1)]
    col_bits = [1 << k for k in range(n_col.bit_length() - 1)]
    row_pair_bit, row_inner = row_bits[-1], combinations(row_bits[:-1])
    col_pair_bit, col_inner = col_bits[-1], combinations(col_bits[:-1])
    start = start_vecs.reshape(n_vec, width)
    tiles, start_here, meta = prepare(blocks, start, block_rows, block_cols, block_count)
    one, two = (n_vec, width), (2 * n_vec, width)
    low, high = slice(0, n_vec), slice(n_vec, 2 * n_vec)

    def products(row_pair, col_pair, row_steps, col_steps):
        parts, at = gather(row_pair, [0, row_pair_bit], "row", row_inner)
        mirror = slot_products(meta, tiles, parts, at, n_col, col_steps[0], True)
        parts, at = gather(col_pair, [0, col_pair_bit], "col", col_inner[::-1])
        direct = slot_products(meta, tiles, parts, at, n_row, row_steps[0], False, mirror[:1])
        return scatter(*direct, "row", row_steps), scatter(*mirror, "col", col_steps)

    def get(ref, rows):
        return ref[rows, :].astype(f32)

    start_y, start_z = swap(start, "row", row_pair_bit), swap(start, "col", col_pair_bit)
    d_terms, m_terms = products(join(start_here, start_y, start_z), join(start_here, start_z), [row_inner], [col_inner])

    n_d = len(d_terms)

    def partial_sums(*refs):
        *terms, to_diag, to_z, to_y, d_keep, m_keep = refs
        d_own, d_other = (total(terms[:n_d], rows) for rows in (low, high))
        m_own, m_other = (total(terms[n_d:], rows) for rows in (low, high))
        d_keep[low, :] = d_own
        d_keep[high, :] = d_other
        m_keep[low, :] = m_own
        m_keep[high, :] = m_other
        both = (d_own + m_own).astype(bf16)
        d_other, m_other = d_other.astype(bf16), m_other.astype(bf16)
        to_y[low, :] = d_other
        to_y[high, :] = both
        to_z[low, :] = m_other
        to_z[high, :] = both
        to_diag[low, :] = d_other
        to_diag[high, :] = m_other

    to_diag, to_z, to_y, d_sum, m_sum = local_call(
        partial_sums, [(two, bf16)] * 3 + [(two, f32)] * 2, *d_terms, *m_terms
    )
    diagonal = [
        (i * n_col + j, (i ^ row_pair_bit) * n_col + (j ^ col_pair_bit)) for i in range(n_row) for j in range(n_col)
    ]
    from_diag = lax.ppermute(to_diag, ("row", "col"), diagonal)
    from_z = swap(to_z, "col", col_pair_bit)
    from_y = swap(to_y, "row", row_pair_bit)

    def first_update(diag_ref, z_ref, y_ref, d_ref, m_ref, cur, cur_y, cur_z, row_out, col_out):
        def advance(applied, ref):
            shifted = (applied - shift_center * ref[...].astype(f32)) / half_width
            return shifted.astype(bf16)

        own = d_ref[low, :] + m_ref[low, :] + get(y_ref, low) + get(z_ref, low)
        own = advance(own, cur)
        row_out[low, :] = own
        col_out[low, :] = own
        row_out[high, :] = advance(d_ref[high, :] + get(y_ref, high) + get(diag_ref, high), cur_y)
        col_out[high, :] = advance(m_ref[high, :] + get(z_ref, high) + get(diag_ref, low), cur_z)

    row_pair, col_pair = local_call(
        first_update, [(two, bf16), (two, bf16)],
        from_diag, from_z, from_y, d_sum, m_sum, start_here, start_y, start_z,
    )
    d_terms, m_terms = products(row_pair, col_pair, [row_inner, [row_pair_bit]], [col_inner, [col_pair_bit]])
    n_last = len(d_terms)
    terms = [*d_terms, *m_terms]

    def last_update(*refs):
        *terms, pair_ref, prev_ref, first_out, second_out = refs
        current = pair_ref[low, :]
        applied = total(terms[:n_last]) + total(terms[n_last:])
        shifted = (applied - shift_center * current.astype(f32)) / half_width
        shifted = 2.0 * shifted - prev_ref[...].astype(f32)
        first_out[...] = current
        second_out[...] = shifted.astype(bf16)

    first, second = local_call(last_update, [(one, bf16), (one, bf16)], *terms, row_pair, start_here)
    shape = start_vecs.shape
    return first.reshape(shape), second.reshape(shape)


def solution(mesh):
    return jax.shard_map(
        body,
        mesh=mesh,
        in_specs=(
            P(None, None, "row", "col", None),
            P("row", "col", None, None, None),
            P("row", "col", None),
            P("row", "col", None),
            P("row", "col"),
        ),
        out_specs=(P(None, None, "row", "col", None), P(None, None, "row", "col", None)),
        check_vma=False,
    )
```

time: 50.9 us -> 46.9 us (0.921)
  waiting for transfers between devices: 14.9 us -> 11.3 us
    ppermute x22, waiting for transfers between devices: 12.6 us -> 7.65 us  [swap(): lax.ppermute(value, axis, [(i, i ^ pattern) for i in range(lax.axis_size(...]
    ppermute x22, starting transfers between devices: 27.1 us -> 25.4 us  [swap(): lax.ppermute(value, axis, [(i, i ^ pattern) for i in range(lax.axis_size(...]
    ppermute x1, waiting for transfers between devices: 2.24 us -> 3.69 us  [body(): from_diag = lax.ppermute(to_diag, ('row', 'col'), diagonal)]
    ppermute x1, starting transfers between devices: 1.11 us -> 2.37 us  [body(): from_diag = lax.ppermute(to_diag, ('row', 'col'), diagonal)]
    pallas_call x10 -> x11, Pallas kernels: 4.24 us -> 4.25 us  [local_call(): pl.pallas_call(kernel, out_shape=[jax.ShapeDtypeStruct(s, d) for s, d in...]
  transfers between devices with their start and end apart: 23 -> 23, of which waited for: 8 -> 9; matrix products, arithmetic and copies ran while one was open for 0% -> 0% of each run, Pallas kernels for 11% -> 12%
where the time goes in v3:
time: 46.9 us; the launch traced here: 46.7 us
  starting transfers between devices  27.8 us (59%)
  waiting for transfers between devices  11.3 us (24%)
  Pallas kernels  6.18 us (13%)
  between operations  1.42 us (3%)
    ppermute x22, starting transfers between devices, swap(): lax.ppermute(value, axis, [(i, i ^ pattern) for i in range(lax.axis_size(...  25.4 us
    ppermute x22, waiting for transfers between devices, swap(): lax.ppermute(value, axis, [(i, i ^ pattern) for i in range(lax.axis_size(...  7.65 us
    pallas_call x11, Pallas kernels, local_call(): pl.pallas_call(kernel, out_shape=[jax.ShapeDtypeStruct(s, d) for s, d in...  4.25 us
    ppermute x1, waiting for transfers between devices, body(): from_diag = lax.ppermute(to_diag, ('row', 'col'), diagonal)  3.69 us
    ppermute x1, starting transfers between devices, body(): from_diag = lax.ppermute(to_diag, ('row', 'col'), diagonal)  2.37 us
    pallas_call x1, Pallas kernels, prepare(): pl.pallas_call(kernel, out_shape=[pltpu.VMEM(blocks.shape[2:], blocks.dty...  1.93 us
  transfers between devices with their start and end apart: 23, of which 9 were waited for; matrix products, arithmetic and copies ran while one was open for 0% of the time, Pallas kernels for 12%

profile of v3, /device:TPU:0, one launch (start us, length us, event | category | flops | bytes accessed | tf_op | source)
XLA Modules:
  0.0 46.7 jit_solution(8995795516323407119)
XLA Ops:
  0.6 3.0 %collective-permute-start.4 = (bf16[32,512]{1,0:T(8,128)(2,1)}, bf16[32,512]{1,0:T(8,128)(2,1)S(1)}, u32[]{:S(2)}, u32[]{:S(2)}) collective-permute-start(bf16[32,512]{1,0:T(8,128)(2,1)} %bitcast.3), channel_id=1, source_target_pairs={{0,16},{8,24},{16,0},{24,8},{1,17},{9,25},{17,1},{25,9},{2,18},{10... | collective-permute-start | bytes 98312 | tf_op jit(solution)/shard_map/ppermute | solution.py:19
  3.7 2.6 %collective-permute-start = (bf16[32,512]{1,0:T(8,128)(2,1)}, bf16[32,512]{1,0:T(8,128)(2,1)S(1)}, u32[]{:S(2)}, u32[]{:S(2)}) collective-permute-start(bf16[32,512]{1,0:T(8,128)(2,1)} %bitcast.4), channel_id=1, source_target_pairs={{0,4},{1,5},{2,6},{3,7},{4,0},{5,1},{6,2},{7,3},{8,12},{9,13},{10,... | collective-permute-start | bytes 98312 | tf_op jit(solution)/shard_map/ppermute | solution.py:19
  6.9 1.9 %shard_map.68 = (bf16[6,512,512]{2,1,0:T(8,128)(2,1)S(1)}, bf16[32,512]{1,0:T(8,128)(2,1)S(1)}, s32[13]{0:T(128)S(4)}) custom-call(s32[1,1]{1,0:T(1,128)S(6)} %copy.7.count_ref, s32[1,1,6]{2,1,0:T(1,128)} %rows_hbm.1, s32[1,1,6]{2,1,0:T(1,128)} %cols_hbm.1, bf16[1,1,6,512,512]{4,3,2,1,0:T(8,128)(2,1)} %blocks_hbm.1, bf16[32,512]{1,0:T(8,128)(2,1)} %bitcast.5), custom_call_target="tpu_custom_call" | custom-call | flops 1000 | bytes 6291456 | tf_op jit(solution)/shard_map/pallas_call | solution.py:58
  8.8 0.0 collective-permute-done.4.second_ref.cur_y
  8.9 0.0 collective-permute-done.second_ref.refs_0_.cur_z
  8.9 0.1 collective-permute-start.5
  9.0 2.6 %collective-permute-start.3 = (bf16[64,512]{1,0:T(8,128)(2,1)S(1)}, bf16[64,512]{1,0:T(8,128)(2,1)S(1)}, u32[]{:S(2)}, u32[]{:S(2)}) collective-permute-start(bf16[64,512]{1,0:T(8,128)(2,1)S(1)} %shard_map.69.refs_0_), channel_id=1, source_target_pairs={{0,3},{1,2},{2,1},{3,0},{4,7},{5,6},{6,5},{7,4},{8,11},{9,10},{10,... | collective-permute-start | bytes 196616 | tf_op jit(solution)/shard_map/ppermute | solution.py:19
  11.5 0.4 collective-permute-start.2
  12.0 0.5 %collective-permute-start.1 = (bf16[64,512]{1,0:T(8,128)(2,1)S(1)}, bf16[64,512]{1,0:T(8,128)(2,1)S(1)}, u32[]{:S(2)}, u32[]{:S(2)}) collective-permute-start(bf16[64,512]{1,0:T(8,128)(2,1)S(1)} %shard_map.69.refs_0_), channel_id=1, source_target_pairs={{0,1},{1,0},{2,3},{3,2},{4,5},{5,4},{6,7},{7,6},{8,9},{9,8},{10,11... | collective-permute-start | bytes 196616 | tf_op jit(solution)/shard_map/ppermute | solution.py:19
  12.5 0.0 collective-permute-done.5.refs_1_
  12.5 0.7 %shard_map.71 = (bf16[64,512]{1,0:T(8,128)(2,1)S(1)}, bf16[64,512]{1,0:T(8,128)(2,1)S(1)}, bf16[64,512]{1,0:T(8,128)(2,1)S(1)}, f32[64,512]{1,0:T(8,128)S(1)}) custom-call(s32[13]{0:T(128)S(4)} %get-tuple-element.30.meta_ref, bf16[6,512,512]{2,1,0:T(8,128)(2,1)S(1)} %get-tuple-element.31.tiles_ref, bf16[64,512]{1,0:T(8,128)(2,1)S(1)} %shard_map.70.refs_0_, ...), custom_call_target="tpu_custom_call" | custom-call | flops 100663296 | bytes 3145728 | tf_op jit(solution)/shard_map/pallas_call | solution.py:23
  13.2 2.6 %collective-permute-start.7 = (bf16[64,512]{1,0:T(8,128)(2,1)S(1)}, bf16[64,512]{1,0:T(8,128)(2,1)S(1)}, u32[]{:S(2)}, u32[]{:S(2)}) collective-permute-start(bf16[64,512]{1,0:T(8,128)(2,1)S(1)} %get-tuple-element.36), channel_id=1, source_target_pairs={{0,3},{1,2},{2,1},{3,0},{4,7},{5,6},{6,5},{7,4},{8,11},{9,10},{10,... | collective-permute-start | bytes 196616 | tf_op jit(solution)/shard_map/ppermute | solution.py:19
  15.8 0.5 collective-permute-start.8
  16.2 0.0 collective-permute-done.3.refs_3_
  16.2 0.5 %collective-permute-start.9 = (bf16[64,512]{1,0:T(8,128)(2,1)S(1)}, bf16[64,512]{1,0:T(8,128)(2,1)S(1)}, u32[]{:S(2)}, u32[]{:S(2)}) collective-permute-start(bf16[64,512]{1,0:T(8,128)(2,1)S(1)} %get-tuple-element.38), channel_id=1, source_target_pairs={{0,1},{1,0},{2,3},{3,2},{4,5},{5,4},{6,7},{7,6},{8,9},{9,8},{10,11... | collective-permute-start | bytes 196616 | tf_op jit(solution)/shard_map/ppermute | solution.py:19
  16.8 0.0 collective-permute-done.2.refs_2_
  16.8 0.0 collective-permute-done.1.refs_1_
  16.8 1.0 %shard_map.72 = (bf16[64,512]{1,0:T(8,128)(2,1)S(1)}, f32[64,512]{1,0:T(8,128)S(1)}) custom-call(s32[13]{0:T(128)S(4)} %get-tuple-element.30.meta_ref, bf16[6,512,512]{2,1,0:T(8,128)(2,1)S(1)} %get-tuple-element.31.tiles_ref, bf16[64,512]{1,0:T(8,128)(2,1)S(1)} %shard_map.69.refs_0_, bf16[64,512]{1,0:T(8,128)(2,1)S(1)} %collective-permute-done.1.refs_1_, ...), custom_call_target="tpu_custom_call" | custom-call | flops 100663296 | bytes 3145728 | tf_op jit(solution)/shard_map/pallas_call | solution.py:23
  17.8 0.1 collective-permute-start.6
  17.9 1.3 %collective-permute-done.7.refs_3_ = bf16[64,512]{1,0:T(8,128)(2,1)S(1)} collective-permute-done((bf16[64,512]{1,0:T(8,128)(2,1)S(1)}, bf16[64,512]{1,0:T(8,128)(2,1)S(1)}, u32[]{:S(2)}, u32[]{:S(2)}) %collective-permute-start.7) | collective-permute-done | bytes 65568 | tf_op jit(solution)/shard_map/ppermute | solution.py:19
  19.2 0.9 %collective-permute-done.8.refs_4_ = bf16[64,512]{1,0:T(8,128)(2,1)S(1)} collective-permute-done((bf16[64,512]{1,0:T(8,128)(2,1)S(1)}, bf16[64,512]{1,0:T(8,128)(2,1)S(1)}, u32[]{:S(2)}, u32[]{:S(2)}) %collective-permute-start.8) | collective-permute-done | bytes 65568 | tf_op jit(solution)/shard_map/ppermute | solution.py:19
  20.0 0.5 collective-permute-done.9.refs_5_
  20.5 0.0 collective-permute-done.6.refs_1_
  20.5 0.1 shard_map.73
  20.6 2.4 %collective-permute-start.10 = (bf16[64,512]{1,0:T(8,128)(2,1)S(1)}, bf16[64,512]{1,0:T(8,128)(2,1)S(1)}, u32[]{:S(2)}, u32[]{:S(2)}) collective-permute-start(bf16[64,512]{1,0:T(8,128)(2,1)S(1)} %get-tuple-element.39), channel_id=1, source_target_pairs={{0,20},{1,21},{2,22},{3,23},{4,16},{5,17},{6,18},{7,19},{8,28},{9,... | collective-permute-start | bytes 196616 | tf_op jit(solution)/shard_map/ppermute | solution.py:228
  22.9 0.6 %collective-permute-start.11 = (bf16[64,512]{1,0:T(8,128)(2,1)S(1)}, bf16[64,512]{1,0:T(8,128)(2,1)S(1)}, u32[]{:S(2)}, u32[]{:S(2)}) collective-permute-start(bf16[64,512]{1,0:T(8,128)(2,1)S(1)} %get-tuple-element.40), channel_id=1, source_target_pairs={{0,4},{1,5},{2,6},{3,7},{4,0},{5,1},{6,2},{7,3},{8,12},{9,13},{10,... | collective-permute-start | bytes 196616 | tf_op jit(solution)/shard_map/ppermute | solution.py:19
  23.5 1.5 %collective-permute-start.12 = (bf16[64,512]{1,0:T(8,128)(2,1)S(1)}, bf16[64,512]{1,0:T(8,128)(2,1)S(1)}, u32[]{:S(2)}, u32[]{:S(2)}) collective-permute-start(bf16[64,512]{1,0:T(8,128)(2,1)S(1)} %get-tuple-element.41), channel_id=1, source_target_pairs={{0,16},{8,24},{16,0},{24,8},{1,17},{9,25},{17,1},{25,9},{2,18},{10... | collective-permute-start | bytes 196616 | tf_op jit(solution)/shard_map/ppermute | solution.py:19
  25.0 3.7 %collective-permute-done.10.diag_ref = bf16[64,512]{1,0:T(8,128)(2,1)S(1)} collective-permute-done((bf16[64,512]{1,0:T(8,128)(2,1)S(1)}, bf16[64,512]{1,0:T(8,128)(2,1)S(1)}, u32[]{:S(2)}, u32[]{:S(2)}) %collective-permute-start.10) | collective-permute-done | bytes 65568 | tf_op jit(solution)/shard_map/ppermute | solution.py:228
  28.7 0.0 collective-permute-done.11.z_ref
  28.7 0.0 collective-permute-done.12.y_ref
  28.7 0.1 shard_map.74
  28.8 0.1 collective-permute-start.16
  28.9 1.3 %collective-permute-start.15 = (bf16[64,512]{1,0:T(8,128)(2,1)S(1)}, bf16[64,512]{1,0:T(8,128)(2,1)S(1)}, u32[]{:S(2)}, u32[]{:S(2)}) collective-permute-start(bf16[64,512]{1,0:T(8,128)(2,1)S(1)} %get-tuple-element.44.refs_0_), channel_id=1, source_target_pairs={{0,3},{1,2},{2,1},{3,0},{4,7},{5,6},{6,5},{7,4},{8,11},{9,10},{10,... | collective-permute-start | bytes 196616 | tf_op jit(solution)/shard_map/ppermute | solution.py:19
  30.2 1.8 %collective-permute-start.14 = (bf16[64,512]{1,0:T(8,128)(2,1)S(1)}, bf16[64,512]{1,0:T(8,128)(2,1)S(1)}, u32[]{:S(2)}, u32[]{:S(2)}) collective-permute-start(bf16[64,512]{1,0:T(8,128)(2,1)S(1)} %get-tuple-element.44.refs_0_), channel_id=1, source_target_pairs={{0,2},{1,3},{2,0},{3,1},{4,6},{5,7},{6,4},{7,5},{8,10},{9,11},{10,... | collective-permute-start | bytes 196616 | tf_op jit(solution)/shard_map/ppermute | solution.py:19
  32.0 0.5 collective-permute-start.13
  32.4 0.0 collective-permute-done.16.refs_1_
  32.4 0.7 %shard_map.75 = (bf16[64,512]{1,0:T(8,128)(2,1)S(1)}, bf16[64,512]{1,0:T(8,128)(2,1)S(1)}, bf16[64,512]{1,0:T(8,128)(2,1)S(1)}, f32[64,512]{1,0:T(8,128)S(1)}) custom-call(s32[13]{0:T(128)S(4)} %get-tuple-element.30.meta_ref, bf16[6,512,512]{2,1,0:T(8,128)(2,1)S(1)} %get-tuple-element.31.tiles_ref, bf16[64,512]{1,0:T(8,128)(2,1)S(1)} %get-tuple-element.45.refs_0_.refs_4_, ...), custom_call_target="tpu_custom_call" | custom-call | flops 100663296 | bytes 3145728 | tf_op jit(solution)/shard_map/pallas_call | solution.py:23
  33.1 1.3 %collective-permute-start.19 = (bf16[64,512]{1,0:T(8,128)(2,1)S(1)}, bf16[64,512]{1,0:T(8,128)(2,1)S(1)}, u32[]{:S(2)}, u32[]{:S(2)}) collective-permute-start(bf16[64,512]{1,0:T(8,128)(2,1)S(1)} %get-tuple-element.51), channel_id=1, source_target_pairs={{0,3},{1,2},{2,1},{3,0},{4,7},{5,6},{6,5},{7,4},{8,11},{9,10},{10,... | collective-permute-start | bytes 196616 | tf_op jit(solution)/shard_map/ppermute | solution.py:19
  34.4 1.8 %collective-permute-start.20 = (bf16[64,512]{1,0:T(8,128)(2,1)S(1)}, bf16[64,512]{1,0:T(8,128)(2,1)S(1)}, u32[]{:S(2)}, u32[]{:S(2)}) collective-permute-start(bf16[64,512]{1,0:T(8,128)(2,1)S(1)} %get-tuple-element.52), channel_id=1, source_target_pairs={{0,2},{1,3},{2,0},{3,1},{4,6},{5,7},{6,4},{7,5},{8,10},{9,11},{10,... | collective-permute-start | bytes 196616 | tf_op jit(solution)/shard_map/ppermute | solution.py:19
  36.2 0.0 collective-permute-done.15.refs_3_
  36.2 0.5 collective-permute-start.21
  36.7 0.0 collective-permute-done.14.refs_2_
  36.7 0.0 collective-permute-done.13.refs_1_
  36.7 1.0 %shard_map.76 = (bf16[64,512]{1,0:T(8,128)(2,1)S(1)}, f32[64,512]{1,0:T(8,128)S(1)}) custom-call(s32[13]{0:T(128)S(4)} %get-tuple-element.30.meta_ref, bf16[6,512,512]{2,1,0:T(8,128)(2,1)S(1)} %get-tuple-element.31.tiles_ref, bf16[64,512]{1,0:T(8,128)(2,1)S(1)} %get-tuple-element.44.refs_0_, bf16[64,512]{1,0:T(8,128)(2,1)S(1)} %collective-permute-done.13.refs_1_, ...), custom_call_target="tpu_custom_call" | custom-call | flops 100663296 | bytes 3145728 | tf_op jit(solution)/shard_map/pallas_call | solution.py:23
  37.7 0.1 collective-permute-start.17
  37.8 0.9 %collective-permute-done.19.refs_0_ = bf16[64,512]{1,0:T(8,128)(2,1)S(1)} collective-permute-done((bf16[64,512]{1,0:T(8,128)(2,1)S(1)}, bf16[64,512]{1,0:T(8,128)(2,1)S(1)}, u32[]{:S(2)}, u32[]{:S(2)}) %collective-permute-start.19) | collective-permute-done | bytes 65568 | tf_op jit(solution)/shard_map/ppermute | solution.py:19
  38.7 0.5 %collective-permute-done.20.refs_1_ = bf16[64,512]{1,0:T(8,128)(2,1)S(1)} collective-permute-done((bf16[64,512]{1,0:T(8,128)(2,1)S(1)}, bf16[64,512]{1,0:T(8,128)(2,1)S(1)}, u32[]{:S(2)}, u32[]{:S(2)}) %collective-permute-start.20) | collective-permute-done | bytes 65568 | tf_op jit(solution)/shard_map/ppermute | solution.py:19
  39.2 1.3 %collective-permute-done.21.refs_2_ = bf16[64,512]{1,0:T(8,128)(2,1)S(1)} collective-permute-done((bf16[64,512]{1,0:T(8,128)(2,1)S(1)}, bf16[64,512]{1,0:T(8,128)(2,1)S(1)}, u32[]{:S(2)}, u32[]{:S(2)}) %collective-permute-start.21) | collective-permute-done | bytes 65568 | tf_op jit(solution)/shard_map/ppermute | solution.py:19
  40.5 1.6 %collective-permute-start.22 = (bf16[32,512]{1,0:T(8,128)(2,1)S(1)}, bf16[32,512]{1,0:T(8,128)(2,1)S(1)}, u32[]{:S(2)}, u32[]{:S(2)}) collective-permute-start(bf16[32,512]{1,0:T(8,128)(2,1)S(1)} %get-tuple-element.55), channel_id=1, source_target_pairs={{0,4},{1,5},{2,6},{3,7},{4,0},{5,1},{6,2},{7,3},{8,12},{9,13},{10,... | collective-permute-start | bytes 98312 | tf_op jit(solution)/shard_map/ppermute | solution.py:19
  42.1 0.0 collective-permute-done.17.refs_0_
  42.1 1.6 %collective-permute-start.18 = (bf16[32,512]{1,0:T(8,128)(2,1)S(1)}, bf16[32,512]{1,0:T(8,128)(2,1)S(1)}, u32[]{:S(2)}, u32[]{:S(2)}) collective-permute-start(bf16[32,512]{1,0:T(8,128)(2,1)S(1)} %get-tuple-element.50), channel_id=1, source_target_pairs={{0,16},{8,24},{16,0},{24,8},{1,17},{9,25},{17,1},{25,9},{2,18},{10... | collective-permute-start | bytes 98312 | tf_op jit(solution)/shard_map/ppermute | solution.py:19
  43.7 2.0 %collective-permute-done.22.refs_3_ = bf16[32,512]{1,0:T(8,128)(2,1)S(1)} collective-permute-done((bf16[32,512]{1,0:T(8,128)(2,1)S(1)}, bf16[32,512]{1,0:T(8,128)(2,1)S(1)}, u32[]{:S(2)}, u32[]{:S(2)}) %collective-permute-start.22) | collective-permute-done | bytes 32800 | tf_op jit(solution)/shard_map/ppermute | solution.py:19
  45.7 0.3 collective-permute-done.18.refs_1_
  46.1 0.6 %shard_map.79 = (bf16[32,512]{1,0:T(8,128)(2,1)}, bf16[32,512]{1,0:T(8,128)(2,1)}) custom-call(f32[32,512]{1,0:T(8,128)S(1)} %get-tuple-element.49.refs_0_, bf16[32,512]{1,0:T(8,128)(2,1)S(1)} %collective-permute-done.18.refs_1_, f32[32,512]{1,0:T(8,128)S(1)} %get-tuple-element.54.refs_2_, bf16[32,512]{1,0:T(8,128)(2,1)S(1)} %collective-permute-done.22.refs_3_, ...), custom_call_target="tpu_custom_call" | custom-call | flops 1000 | bytes 100000 | tf_op jit(solution)/shard_map/pallas_call | solution.py:23
  (4 shorter events, 0.1 us)
Async XLA Ops:
  0.6 8.2 %collective-permute-start.4 = (bf16[32,512]{1,0:T(8,128)(2,1)}, bf16[32,512]{1,0:T(8,128)(2,1)S(1)}, u32[]{:S(2)}, u32[]{:S(2)}) collective-permute-start(bf16[32,512]{1,0:T(8,128)(2,1)} %bitcast.3), channel_id=1, source_target_pairs={{0,16},{8,24},{16,0},{24,8},{1,17},{9,25},{17,1},{25,9},{2,18},{10... | collective-permute-start | bytes 98312 | tf_op jit(solution)/shard_map/ppermute | solution.py:19
  3.7 5.2 %collective-permute-start = (bf16[32,512]{1,0:T(8,128)(2,1)}, bf16[32,512]{1,0:T(8,128)(2,1)S(1)}, u32[]{:S(2)}, u32[]{:S(2)}) collective-permute-start(bf16[32,512]{1,0:T(8,128)(2,1)} %bitcast.4), channel_id=1, source_target_pairs={{0,4},{1,5},{2,6},{3,7},{4,0},{5,1},{6,2},{7,3},{8,12},{9,13},{10,... | collective-permute-start | bytes 98312 | tf_op jit(solution)/shard_map/ppermute | solution.py:19
  8.9 3.7 %collective-permute-start.5 = (bf16[64,512]{1,0:T(8,128)(2,1)S(1)}, bf16[64,512]{1,0:T(8,128)(2,1)S(1)}, u32[]{:S(2)}, u32[]{:S(2)}) collective-permute-start(bf16[64,512]{1,0:T(8,128)(2,1)S(1)} %shard_map.70.refs_0_), channel_id=1, source_target_pairs={{0,8},{8,0},{16,24},{24,16},{1,9},{9,1},{17,25},{25,17},{2,10},{10... | collective-permute-start | bytes 196616 | tf_op jit(solution)/shard_map/ppermute | solution.py:19
  9.0 7.3 %collective-permute-start.3 = (bf16[64,512]{1,0:T(8,128)(2,1)S(1)}, bf16[64,512]{1,0:T(8,128)(2,1)S(1)}, u32[]{:S(2)}, u32[]{:S(2)}) collective-permute-start(bf16[64,512]{1,0:T(8,128)(2,1)S(1)} %shard_map.69.refs_0_), channel_id=1, source_target_pairs={{0,3},{1,2},{2,1},{3,0},{4,7},{5,6},{6,5},{7,4},{8,11},{9,10},{10,... | collective-permute-start | bytes 196616 | tf_op jit(solution)/shard_map/ppermute | solution.py:19
  11.5 5.2 %collective-permute-start.2 = (bf16[64,512]{1,0:T(8,128)(2,1)S(1)}, bf16[64,512]{1,0:T(8,128)(2,1)S(1)}, u32[]{:S(2)}, u32[]{:S(2)}) collective-permute-start(bf16[64,512]{1,0:T(8,128)(2,1)S(1)} %shard_map.69.refs_0_), channel_id=1, source_target_pairs={{0,2},{1,3},{2,0},{3,1},{4,6},{5,7},{6,4},{7,5},{8,10},{9,11},{10,... | collective-permute-start | bytes 196616 | tf_op jit(solution)/shard_map/ppermute | solution.py:19
  12.0 4.8 %collective-permute-start.1 = (bf16[64,512]{1,0:T(8,128)(2,1)S(1)}, bf16[64,512]{1,0:T(8,128)(2,1)S(1)}, u32[]{:S(2)}, u32[]{:S(2)}) collective-permute-start(bf16[64,512]{1,0:T(8,128)(2,1)S(1)} %shard_map.69.refs_0_), channel_id=1, source_target_pairs={{0,1},{1,0},{2,3},{3,2},{4,5},{5,4},{6,7},{7,6},{8,9},{9,8},{10,11... | collective-permute-start | bytes 196616 | tf_op jit(solution)/shard_map/ppermute | solution.py:19
  13.2 6.0 %collective-permute-start.7 = (bf16[64,512]{1,0:T(8,128)(2,1)S(1)}, bf16[64,512]{1,0:T(8,128)(2,1)S(1)}, u32[]{:S(2)}, u32[]{:S(2)}) collective-permute-start(bf16[64,512]{1,0:T(8,128)(2,1)S(1)} %get-tuple-element.36), channel_id=1, source_target_pairs={{0,3},{1,2},{2,1},{3,0},{4,7},{5,6},{6,5},{7,4},{8,11},{9,10},{10,... | collective-permute-start | bytes 196616 | tf_op jit(solution)/shard_map/ppermute | solution.py:19
  15.8 4.3 %collective-permute-start.8 = (bf16[64,512]{1,0:T(8,128)(2,1)S(1)}, bf16[64,512]{1,0:T(8,128)(2,1)S(1)}, u32[]{:S(2)}, u32[]{:S(2)}) collective-permute-start(bf16[64,512]{1,0:T(8,128)(2,1)S(1)} %get-tuple-element.37), channel_id=1, source_target_pairs={{0,2},{1,3},{2,0},{3,1},{4,6},{5,7},{6,4},{7,5},{8,10},{9,11},{10,... | collective-permute-start | bytes 196616 | tf_op jit(solution)/shard_map/ppermute | solution.py:19
  16.2 4.3 %collective-permute-start.9 = (bf16[64,512]{1,0:T(8,128)(2,1)S(1)}, bf16[64,512]{1,0:T(8,128)(2,1)S(1)}, u32[]{:S(2)}, u32[]{:S(2)}) collective-permute-start(bf16[64,512]{1,0:T(8,128)(2,1)S(1)} %get-tuple-element.38), channel_id=1, source_target_pairs={{0,1},{1,0},{2,3},{3,2},{4,5},{5,4},{6,7},{7,6},{8,9},{9,8},{10,11... | collective-permute-start | bytes 196616 | tf_op jit(solution)/shard_map/ppermute | solution.py:19
  17.8 2.7 %collective-permute-start.6 = (bf16[64,512]{1,0:T(8,128)(2,1)S(1)}, bf16[64,512]{1,0:T(8,128)(2,1)S(1)}, u32[]{:S(2)}, u32[]{:S(2)}) collective-permute-start(bf16[64,512]{1,0:T(8,128)(2,1)S(1)} %get-tuple-element.35), channel_id=1, source_target_pairs={{0,8},{8,0},{16,24},{24,16},{1,9},{9,1},{17,25},{25,17},{2,10},{10... | collective-permute-start | bytes 196616 | tf_op jit(solution)/shard_map/ppermute | solution.py:19
  20.6 8.1 %collective-permute-start.10 = (bf16[64,512]{1,0:T(8,128)(2,1)S(1)}, bf16[64,512]{1,0:T(8,128)(2,1)S(1)}, u32[]{:S(2)}, u32[]{:S(2)}) collective-permute-start(bf16[64,512]{1,0:T(8,128)(2,1)S(1)} %get-tuple-element.39), channel_id=1, source_target_pairs={{0,20},{1,21},{2,22},{3,23},{4,16},{5,17},{6,18},{7,19},{8,28},{9,... | collective-permute-start | bytes 196616 | tf_op jit(solution)/shard_map/ppermute | solution.py:228
  22.9 5.8 %collective-permute-start.11 = (bf16[64,512]{1,0:T(8,128)(2,1)S(1)}, bf16[64,512]{1,0:T(8,128)(2,1)S(1)}, u32[]{:S(2)}, u32[]{:S(2)}) collective-permute-start(bf16[64,512]{1,0:T(8,128)(2,1)S(1)} %get-tuple-element.40), channel_id=1, source_target_pairs={{0,4},{1,5},{2,6},{3,7},{4,0},{5,1},{6,2},{7,3},{8,12},{9,13},{10,... | collective-permute-start | bytes 196616 | tf_op jit(solution)/shard_map/ppermute | solution.py:19
  23.5 5.2 %collective-permute-start.12 = (bf16[64,512]{1,0:T(8,128)(2,1)S(1)}, bf16[64,512]{1,0:T(8,128)(2,1)S(1)}, u32[]{:S(2)}, u32[]{:S(2)}) collective-permute-start(bf16[64,512]{1,0:T(8,128)(2,1)S(1)} %get-tuple-element.41), channel_id=1, source_target_pairs={{0,16},{8,24},{16,0},{24,8},{1,17},{9,25},{17,1},{25,9},{2,18},{10... | collective-permute-start | bytes 196616 | tf_op jit(solution)/shard_map/ppermute | solution.py:19
  28.8 3.6 %collective-permute-start.16 = (bf16[64,512]{1,0:T(8,128)(2,1)S(1)}, bf16[64,512]{1,0:T(8,128)(2,1)S(1)}, u32[]{:S(2)}, u32[]{:S(2)}) collective-permute-start(bf16[64,512]{1,0:T(8,128)(2,1)S(1)} %get-tuple-element.45.refs_0_.refs_4_), channel_id=1, source_target_pairs={{0,8},{8,0},{16,24},{24,16},{1,9},{9,1},{17,25},{25,17},{2,10},{10... | collective-permute-start | bytes 196616 | tf_op jit(solution)/shard_map/ppermute | solution.py:19
  28.9 7.3 %collective-permute-start.15 = (bf16[64,512]{1,0:T(8,128)(2,1)S(1)}, bf16[64,512]{1,0:T(8,128)(2,1)S(1)}, u32[]{:S(2)}, u32[]{:S(2)}) collective-permute-start(bf16[64,512]{1,0:T(8,128)(2,1)S(1)} %get-tuple-element.44.refs_0_), channel_id=1, source_target_pairs={{0,3},{1,2},{2,1},{3,0},{4,7},{5,6},{6,5},{7,4},{8,11},{9,10},{10,... | collective-permute-start | bytes 196616 | tf_op jit(solution)/shard_map/ppermute | solution.py:19
  30.2 6.5 %collective-permute-start.14 = (bf16[64,512]{1,0:T(8,128)(2,1)S(1)}, bf16[64,512]{1,0:T(8,128)(2,1)S(1)}, u32[]{:S(2)}, u32[]{:S(2)}) collective-permute-start(bf16[64,512]{1,0:T(8,128)(2,1)S(1)} %get-tuple-element.44.refs_0_), channel_id=1, source_target_pairs={{0,2},{1,3},{2,0},{3,1},{4,6},{5,7},{6,4},{7,5},{8,10},{9,11},{10,... | collective-permute-start | bytes 196616 | tf_op jit(solution)/shard_map/ppermute | solution.py:19
  32.0 4.7 %collective-permute-start.13 = (bf16[64,512]{1,0:T(8,128)(2,1)S(1)}, bf16[64,512]{1,0:T(8,128)(2,1)S(1)}, u32[]{:S(2)}, u32[]{:S(2)}) collective-permute-start(bf16[64,512]{1,0:T(8,128)(2,1)S(1)} %get-tuple-element.44.refs_0_), channel_id=1, source_target_pairs={{0,1},{1,0},{2,3},{3,2},{4,5},{5,4},{6,7},{7,6},{8,9},{9,8},{10,11... | collective-permute-start | bytes 196616 | tf_op jit(solution)/shard_map/ppermute | solution.py:19
  33.1 5.6 %collective-permute-start.19 = (bf16[64,512]{1,0:T(8,128)(2,1)S(1)}, bf16[64,512]{1,0:T(8,128)(2,1)S(1)}, u32[]{:S(2)}, u32[]{:S(2)}) collective-permute-start(bf16[64,512]{1,0:T(8,128)(2,1)S(1)} %get-tuple-element.51), channel_id=1, source_target_pairs={{0,3},{1,2},{2,1},{3,0},{4,7},{5,6},{6,5},{7,4},{8,11},{9,10},{10,... | collective-permute-start | bytes 196616 | tf_op jit(solution)/shard_map/ppermute | solution.py:19
  34.4 4.8 %collective-permute-start.20 = (bf16[64,512]{1,0:T(8,128)(2,1)S(1)}, bf16[64,512]{1,0:T(8,128)(2,1)S(1)}, u32[]{:S(2)}, u32[]{:S(2)}) collective-permute-start(bf16[64,512]{1,0:T(8,128)(2,1)S(1)} %get-tuple-element.52), channel_id=1, source_target_pairs={{0,2},{1,3},{2,0},{3,1},{4,6},{5,7},{6,4},{7,5},{8,10},{9,11},{10,... | collective-permute-start | bytes 196616 | tf_op jit(solution)/shard_map/ppermute | solution.py:19
  36.2 4.3 %collective-permute-start.21 = (bf16[64,512]{1,0:T(8,128)(2,1)S(1)}, bf16[64,512]{1,0:T(8,128)(2,1)S(1)}, u32[]{:S(2)}, u32[]{:S(2)}) collective-permute-start(bf16[64,512]{1,0:T(8,128)(2,1)S(1)} %get-tuple-element.53), channel_id=1, source_target_pairs={{0,1},{1,0},{2,3},{3,2},{4,5},{5,4},{6,7},{7,6},{8,9},{9,8},{10,11... | collective-permute-start | bytes 196616 | tf_op jit(solution)/shard_map/ppermute | solution.py:19
  37.7 4.3 %collective-permute-start.17 = (bf16[64,512]{1,0:T(8,128)(2,1)S(1)}, bf16[64,512]{1,0:T(8,128)(2,1)S(1)}, u32[]{:S(2)}, u32[]{:S(2)}) collective-permute-start(bf16[64,512]{1,0:T(8,128)(2,1)S(1)} %get-tuple-element.48), channel_id=1, source_target_pairs={{0,8},{8,0},{16,24},{24,16},{1,9},{9,1},{17,25},{25,17},{2,10},{10... | collective-permute-start | bytes 196616 | tf_op jit(solution)/shard_map/ppermute | solution.py:19
  40.5 5.2 %collective-permute-start.22 = (bf16[32,512]{1,0:T(8,128)(2,1)S(1)}, bf16[32,512]{1,0:T(8,128)(2,1)S(1)}, u32[]{:S(2)}, u32[]{:S(2)}) collective-permute-start(bf16[32,512]{1,0:T(8,128)(2,1)S(1)} %get-tuple-element.55), channel_id=1, source_target_pairs={{0,4},{1,5},{2,6},{3,7},{4,0},{5,1},{6,2},{7,3},{8,12},{9,13},{10,... | collective-permute-start | bytes 98312 | tf_op jit(solution)/shard_map/ppermute | solution.py:19
  42.1 4.0 %collective-permute-start.18 = (bf16[32,512]{1,0:T(8,128)(2,1)S(1)}, bf16[32,512]{1,0:T(8,128)(2,1)S(1)}, u32[]{:S(2)}, u32[]{:S(2)}) collective-permute-start(bf16[32,512]{1,0:T(8,128)(2,1)S(1)} %get-tuple-element.50), channel_id=1, source_target_pairs={{0,16},{8,24},{16,0},{24,8},{1,17},{9,25},{17,1},{25,9},{2,18},{10... | collective-permute-start | bytes 98312 | tf_op jit(solution)/shard_map/ppermute | solution.py:19

commit v4 on v3

--- a/solution.py
+++ b/solution.py
@@ -34,7 +34,7 @@
 def prepare(blocks, start_vecs, block_rows, block_cols, block_count):
     slots = blocks.shape[2]
 
-    def kernel(count_ref, rows_hbm, cols_hbm, blocks_hbm, vecs_hbm, tiles_out, vecs_out, meta_out, rows_ref, cols_ref, sems):
+    def kernel(count_ref, rows_hbm, cols_hbm, blocks_hbm, vecs_hbm, tiles_out, turned_out, vecs_out, meta_out, rows_ref, cols_ref, sems):
         copies = [
             pltpu.make_async_copy(rows_hbm, rows_ref, sems.at[slots + 1]),
             pltpu.make_async_copy(cols_hbm, cols_ref, sems.at[slots + 2]),
@@ -51,19 +51,22 @@
             meta_out[s] = jnp.where(s < count, rows_ref[0, 0, s] ^ row_at, 0)
             meta_out[slots + s] = jnp.where(s < count, cols_ref[0, 0, s] ^ col_at, 0)
         meta_out[2 * slots] = count
-        for copy in copies[2:]:
-            copy.wait()
+        copies[2].wait()
+        for s in range(slots):
+            copies[3 + s].wait()
+            turned_out[s] = tiles_out[s].T
 
     arrays = (block_rows, block_cols, blocks, start_vecs)
     return pl.pallas_call(
         kernel,
         out_shape=[
             pltpu.VMEM(blocks.shape[2:], blocks.dtype),
+            pltpu.VMEM(blocks.shape[2:], blocks.dtype),
             pltpu.VMEM(start_vecs.shape, start_vecs.dtype),
             pltpu.SMEM((2 * slots + 1,), jnp.int32),
         ],
         in_specs=[SMEM] + [pl.BlockSpec(memory_space=pltpu.HBM)] * len(arrays),
-        out_specs=[VMEM, VMEM, SMEM],
+        out_specs=[VMEM, VMEM, VMEM, SMEM],
         scratch_shapes=[pltpu.SMEM(a.shape, a.dtype) for a in arrays[:2]] + [pltpu.SemaphoreType.DMA((slots + 3,))],
         compiler_params=PARAMS,
         cost_estimate=pl.CostEstimate(flops=1000, bytes_accessed=2 * blocks.size * 2, transcendentals=0),
@@ -156,9 +159,7 @@
             r, c = meta_ref[s], meta_ref[slots + s]
             source, target = (r, c) if mirrored else (c, r)
             values = jnp.where(s < count, vecs[source], jnp.zeros((), bf16))
-            product = lax.dot_general(
-                values, tiles_ref[s], (((1,), (0 if mirrored else 1,)), ((), ())), preferred_element_type=f32
-            )
+            product = jnp.dot(values, tiles_ref[s], preferred_element_type=f32)
             totals[target] += product
         for out, chosen in zip(outs, [*theirs, mine], strict=True):
             for n, i in enumerate(chosen):
@@ -183,7 +184,7 @@
     row_pair_bit, row_inner = row_bits[-1], combinations(row_bits[:-1])
     col_pair_bit, col_inner = col_bits[-1], combinations(col_bits[:-1])
     start = start_vecs.reshape(n_vec, width)
-    tiles, start_here, meta = prepare(blocks, start, block_rows, block_cols, block_count)
+    tiles, turned, start_here, meta = prepare(blocks, start, block_rows, block_cols, block_count)
     one, two = (n_vec, width), (2 * n_vec, width)
     low, high = slice(0, n_vec), slice(n_vec, 2 * n_vec)
 
@@ -191,14 +192,14 @@
         parts, at = gather(row_pair, [0, row_pair_bit], "row", row_inner)
         mirror = slot_products(meta, tiles, parts, at, n_col, col_steps[0], True)
         parts, at = gather(col_pair, [0, col_pair_bit], "col", col_inner[::-1])
-        direct = slot_products(meta, tiles, parts, at, n_row, row_steps[0], False, mirror[:1])
+        direct = slot_products(meta, turned, parts, at, n_row, row_steps[0], False, mirror[:1])
         return scatter(*direct, "row", row_steps), scatter(*mirror, "col", col_steps)
 
     def get(ref, rows):
         return ref[rows, :].astype(f32)
 
     start_y, start_z = swap(start, "row", row_pair_bit), swap(start, "col", col_pair_bit)
-    d_terms, m_terms = products(join(start_here, start_y, start_z), join(start_here, start_z), [row_inner], [col_inner])
+    d_terms, m_terms = products(join(start_here, start_y), join(start_here, start_z), [row_inner], [col_inner])
 
     n_d = len(d_terms)
 
@@ -245,7 +246,7 @@
         first_update, [(two, bf16), (two, bf16)],
         from_diag, from_z, from_y, d_sum, m_sum, start_here, start_y, start_z,
     )
-    d_terms, m_terms = products(row_pair, col_pair, [row_inner, [row_pair_bit]], [col_inner, [col_pair_bit]])
+    d_terms, m_terms = products(row_pair, col_pair, [[row_pair_bit], row_inner], [col_inner, [col_pair_bit]])
     n_last = len(d_terms)
     terms = [*d_terms, *m_terms]
 

time: 46.9 us -> 46.2 us (0.985)
    pallas_call x11, Pallas kernels: 4.25 us -> 3.5 us  [local_call(): pl.pallas_call(kernel, out_shape=[jax.ShapeDtypeStruct(s, d) for s, d in...]
  transfers between devices with their start and end apart: 23 -> 23, of which waited for: 9 -> 7; matrix products, arithmetic and copies ran while one was open for 0% -> 0% of each run, Pallas kernels for 12% -> 11%
where the time goes in v4:
time: 46.2 us; the launch traced here: 46 us
  starting transfers between devices  27.5 us (60%)
  waiting for transfers between devices  11.3 us (24%)
  Pallas kernels  5.78 us (13%)
  between operations  1.42 us (3%)
    ppermute x22, starting transfers between devices, swap(): lax.ppermute(value, axis, [(i, i ^ pattern) for i in range(lax.axis_size(...  25.6 us
    ppermute x22, waiting for transfers between devices, swap(): lax.ppermute(value, axis, [(i, i ^ pattern) for i in range(lax.axis_size(...  7.97 us
    pallas_call x11, Pallas kernels, local_call(): pl.pallas_call(kernel, out_shape=[jax.ShapeDtypeStruct(s, d) for s, d in...  3.5 us
    ppermute x1, waiting for transfers between devices, body(): from_diag = lax.ppermute(to_diag, ('row', 'col'), diagonal)  3.36 us
    pallas_call x1, Pallas kernels, prepare(): pl.pallas_call(kernel, out_shape=[pltpu.VMEM(blocks.shape[2:], blocks.dty...  2.29 us
    ppermute x1, starting transfers between devices, body(): from_diag = lax.ppermute(to_diag, ('row', 'col'), diagonal)  1.92 us
  transfers between devices with their start and end apart: 23, of which 7 were waited for; matrix products, arithmetic and copies ran while one was open for 0% of the time, Pallas kernels for 11%

profile of v4, /device:TPU:0, one launch (start us, length us, event | category | flops | bytes accessed | tf_op | source)
XLA Modules:
  0.0 46.0 jit_solution(1795649976083006480)
XLA Ops:
  0.6 3.0 %collective-permute-start.4 = (bf16[32,512]{1,0:T(8,128)(2,1)}, bf16[32,512]{1,0:T(8,128)(2,1)S(1)}, u32[]{:S(2)}, u32[]{:S(2)}) collective-permute-start(bf16[32,512]{1,0:T(8,128)(2,1)} %bitcast.3), channel_id=1, source_target_pairs={{0,16},{8,24},{16,0},{24,8},{1,17},{9,25},{17,1},{25,9},{2,18},{10... | collective-permute-start | bytes 98312 | tf_op jit(solution)/shard_map/ppermute | solution.py:19
  3.7 2.6 %collective-permute-start = (bf16[32,512]{1,0:T(8,128)(2,1)}, bf16[32,512]{1,0:T(8,128)(2,1)S(1)}, u32[]{:S(2)}, u32[]{:S(2)}) collective-permute-start(bf16[32,512]{1,0:T(8,128)(2,1)} %bitcast.4), channel_id=1, source_target_pairs={{0,4},{1,5},{2,6},{3,7},{4,0},{5,1},{6,2},{7,3},{8,12},{9,13},{10,... | collective-permute-start | bytes 98312 | tf_op jit(solution)/shard_map/ppermute | solution.py:19
  6.9 2.3 %shard_map.68 = (bf16[6,512,512]{2,1,0:T(8,128)(2,1)S(1)}, bf16[6,512,512]{2,1,0:T(8,128)(2,1)S(1)}, bf16[32,512]{1,0:T(8,128)(2,1)S(1)}, s32[13]{0:T(128)S(4)}) custom-call(s32[1,1]{1,0:T(1,128)S(6)} %copy.7.count_ref, s32[1,1,6]{2,1,0:T(1,128)} %rows_hbm.1, s32[1,1,6]{2,1,0:T(1,128)} %cols_hbm.1, bf16[1,1,6,512,512]{4,3,2,1,0:T(8,128)(2,1)} %blocks_hbm.1, ...), custom_call_target="tpu_custom_call" | custom-call | flops 1000 | bytes 6291456 | tf_op jit(solution)/shard_map/pallas_call | solution.py:60
  9.2 0.0 collective-permute-done.4.second_ref.cur_y
  9.2 0.1 collective-permute-start.5
  9.3 0.0 collective-permute-done.second_ref.cur_z
  9.3 2.6 %collective-permute-start.3 = (bf16[64,512]{1,0:T(8,128)(2,1)S(1)}, bf16[64,512]{1,0:T(8,128)(2,1)S(1)}, u32[]{:S(2)}, u32[]{:S(2)}) collective-permute-start(bf16[64,512]{1,0:T(8,128)(2,1)S(1)} %shard_map.69.refs_0_), channel_id=1, source_target_pairs={{0,3},{1,2},{2,1},{3,0},{4,7},{5,6},{6,5},{7,4},{8,11},{9,10},{10,... | collective-permute-start | bytes 196616 | tf_op jit(solution)/shard_map/ppermute | solution.py:19
  11.9 0.4 collective-permute-start.2
  12.3 0.5 %collective-permute-start.1 = (bf16[64,512]{1,0:T(8,128)(2,1)S(1)}, bf16[64,512]{1,0:T(8,128)(2,1)S(1)}, u32[]{:S(2)}, u32[]{:S(2)}) collective-permute-start(bf16[64,512]{1,0:T(8,128)(2,1)S(1)} %shard_map.69.refs_0_), channel_id=1, source_target_pairs={{0,1},{1,0},{2,3},{3,2},{4,5},{5,4},{6,7},{7,6},{8,9},{9,8},{10,11... | collective-permute-start | bytes 196616 | tf_op jit(solution)/shard_map/ppermute | solution.py:19
  12.9 0.0 collective-permute-done.5.refs_1_
  12.9 0.7 %shard_map.71 = (bf16[64,512]{1,0:T(8,128)(2,1)S(1)}, bf16[64,512]{1,0:T(8,128)(2,1)S(1)}, bf16[64,512]{1,0:T(8,128)(2,1)S(1)}, f32[64,512]{1,0:T(8,128)S(1)}) custom-call(s32[13]{0:T(128)S(4)} %get-tuple-element.31.meta_ref, bf16[6,512,512]{2,1,0:T(8,128)(2,1)S(1)} %get-tuple-element.34.tiles_ref, bf16[64,512]{1,0:T(8,128)(2,1)S(1)} %shard_map.70.refs_0_, ...), custom_call_target="tpu_custom_call" | custom-call | flops 100663296 | bytes 3145728 | tf_op jit(solution)/shard_map/pallas_call | solution.py:23
  13.6 2.6 %collective-permute-start.7 = (bf16[64,512]{1,0:T(8,128)(2,1)S(1)}, bf16[64,512]{1,0:T(8,128)(2,1)S(1)}, u32[]{:S(2)}, u32[]{:S(2)}) collective-permute-start(bf16[64,512]{1,0:T(8,128)(2,1)S(1)} %get-tuple-element.38), channel_id=1, source_target_pairs={{0,3},{1,2},{2,1},{3,0},{4,7},{5,6},{6,5},{7,4},{8,11},{9,10},{10,... | collective-permute-start | bytes 196616 | tf_op jit(solution)/shard_map/ppermute | solution.py:19
  16.1 0.4 collective-permute-start.8
  16.6 0.0 collective-permute-done.3.refs_3_
  16.6 0.5 %collective-permute-start.9 = (bf16[64,512]{1,0:T(8,128)(2,1)S(1)}, bf16[64,512]{1,0:T(8,128)(2,1)S(1)}, u32[]{:S(2)}, u32[]{:S(2)}) collective-permute-start(bf16[64,512]{1,0:T(8,128)(2,1)S(1)} %get-tuple-element.40), channel_id=1, source_target_pairs={{0,1},{1,0},{2,3},{3,2},{4,5},{5,4},{6,7},{7,6},{8,9},{9,8},{10,11... | collective-permute-start | bytes 196616 | tf_op jit(solution)/shard_map/ppermute | solution.py:19
  17.1 0.0 collective-permute-done.2.refs_2_
  17.1 0.0 collective-permute-done.1.refs_1_
  17.1 0.7 %shard_map.72 = (bf16[64,512]{1,0:T(8,128)(2,1)S(1)}, f32[64,512]{1,0:T(8,128)S(1)}) custom-call(s32[13]{0:T(128)S(4)} %get-tuple-element.31.meta_ref, bf16[6,512,512]{2,1,0:T(8,128)(2,1)S(1)} %get-tuple-element.32.tiles_ref, bf16[64,512]{1,0:T(8,128)(2,1)S(1)} %shard_map.69.refs_0_, bf16[64,512]{1,0:T(8,128)(2,1)S(1)} %collective-permute-done.1.refs_1_, ...), custom_call_target="tpu_custom_call" | custom-call | flops 100663296 | bytes 3145728 | tf_op jit(solution)/shard_map/pallas_call | solution.py:23
  17.8 0.1 collective-permute-start.6
  17.9 1.7 %collective-permute-done.7.refs_3_ = bf16[64,512]{1,0:T(8,128)(2,1)S(1)} collective-permute-done((bf16[64,512]{1,0:T(8,128)(2,1)S(1)}, bf16[64,512]{1,0:T(8,128)(2,1)S(1)}, u32[]{:S(2)}, u32[]{:S(2)}) %collective-permute-start.7) | collective-permute-done | bytes 65568 | tf_op jit(solution)/shard_map/ppermute | solution.py:19
  19.6 0.8 %collective-permute-done.8.refs_4_ = bf16[64,512]{1,0:T(8,128)(2,1)S(1)} collective-permute-done((bf16[64,512]{1,0:T(8,128)(2,1)S(1)}, bf16[64,512]{1,0:T(8,128)(2,1)S(1)}, u32[]{:S(2)}, u32[]{:S(2)}) %collective-permute-start.8) | collective-permute-done | bytes 65568 | tf_op jit(solution)/shard_map/ppermute | solution.py:19
  20.4 0.5 collective-permute-done.9.refs_5_
  20.9 0.0 collective-permute-done.6.refs_1_
  20.9 0.1 shard_map.73
  20.9 1.9 %collective-permute-start.10 = (bf16[64,512]{1,0:T(8,128)(2,1)S(1)}, bf16[64,512]{1,0:T(8,128)(2,1)S(1)}, u32[]{:S(2)}, u32[]{:S(2)}) collective-permute-start(bf16[64,512]{1,0:T(8,128)(2,1)S(1)} %get-tuple-element.41), channel_id=1, source_target_pairs={{0,20},{1,21},{2,22},{3,23},{4,16},{5,17},{6,18},{7,19},{8,28},{9,... | collective-permute-start | bytes 196616 | tf_op jit(solution)/shard_map/ppermute | solution.py:229
  22.8 1.0 %collective-permute-start.11 = (bf16[64,512]{1,0:T(8,128)(2,1)S(1)}, bf16[64,512]{1,0:T(8,128)(2,1)S(1)}, u32[]{:S(2)}, u32[]{:S(2)}) collective-permute-start(bf16[64,512]{1,0:T(8,128)(2,1)S(1)} %get-tuple-element.42), channel_id=1, source_target_pairs={{0,4},{1,5},{2,6},{3,7},{4,0},{5,1},{6,2},{7,3},{8,12},{9,13},{10,... | collective-permute-start | bytes 196616 | tf_op jit(solution)/shard_map/ppermute | solution.py:19
  23.9 1.5 %collective-permute-start.12 = (bf16[64,512]{1,0:T(8,128)(2,1)S(1)}, bf16[64,512]{1,0:T(8,128)(2,1)S(1)}, u32[]{:S(2)}, u32[]{:S(2)}) collective-permute-start(bf16[64,512]{1,0:T(8,128)(2,1)S(1)} %get-tuple-element.43), channel_id=1, source_target_pairs={{0,16},{8,24},{16,0},{24,8},{1,17},{9,25},{17,1},{25,9},{2,18},{10... | collective-permute-start | bytes 196616 | tf_op jit(solution)/shard_map/ppermute | solution.py:19
  25.4 3.4 %collective-permute-done.10.diag_ref = bf16[64,512]{1,0:T(8,128)(2,1)S(1)} collective-permute-done((bf16[64,512]{1,0:T(8,128)(2,1)S(1)}, bf16[64,512]{1,0:T(8,128)(2,1)S(1)}, u32[]{:S(2)}, u32[]{:S(2)}) %collective-permute-start.10) | collective-permute-done | bytes 65568 | tf_op jit(solution)/shard_map/ppermute | solution.py:229
  28.7 0.0 collective-permute-done.11.z_ref
  28.7 0.0 collective-permute-done.12.y_ref
  28.7 0.1 shard_map.74
  28.8 0.1 collective-permute-start.16
  28.9 1.2 %collective-permute-start.15 = (bf16[64,512]{1,0:T(8,128)(2,1)S(1)}, bf16[64,512]{1,0:T(8,128)(2,1)S(1)}, u32[]{:S(2)}, u32[]{:S(2)}) collective-permute-start(bf16[64,512]{1,0:T(8,128)(2,1)S(1)} %get-tuple-element.46.refs_0_), channel_id=1, source_target_pairs={{0,3},{1,2},{2,1},{3,0},{4,7},{5,6},{6,5},{7,4},{8,11},{9,10},{10,... | collective-permute-start | bytes 196616 | tf_op jit(solution)/shard_map/ppermute | solution.py:19
  30.1 1.9 %collective-permute-start.14 = (bf16[64,512]{1,0:T(8,128)(2,1)S(1)}, bf16[64,512]{1,0:T(8,128)(2,1)S(1)}, u32[]{:S(2)}, u32[]{:S(2)}) collective-permute-start(bf16[64,512]{1,0:T(8,128)(2,1)S(1)} %get-tuple-element.46.refs_0_), channel_id=1, source_target_pairs={{0,2},{1,3},{2,0},{3,1},{4,6},{5,7},{6,4},{7,5},{8,10},{9,11},{10,... | collective-permute-start | bytes 196616 | tf_op jit(solution)/shard_map/ppermute | solution.py:19
  31.9 0.5 %collective-permute-start.13 = (bf16[64,512]{1,0:T(8,128)(2,1)S(1)}, bf16[64,512]{1,0:T(8,128)(2,1)S(1)}, u32[]{:S(2)}, u32[]{:S(2)}) collective-permute-start(bf16[64,512]{1,0:T(8,128)(2,1)S(1)} %get-tuple-element.46.refs_0_), channel_id=1, source_target_pairs={{0,1},{1,0},{2,3},{3,2},{4,5},{5,4},{6,7},{7,6},{8,9},{9,8},{10,11... | collective-permute-start | bytes 196616 | tf_op jit(solution)/shard_map/ppermute | solution.py:19
  32.4 0.0 collective-permute-done.16.refs_1_
  32.4 0.7 %shard_map.75 = (bf16[64,512]{1,0:T(8,128)(2,1)S(1)}, bf16[64,512]{1,0:T(8,128)(2,1)S(1)}, bf16[64,512]{1,0:T(8,128)(2,1)S(1)}, f32[64,512]{1,0:T(8,128)S(1)}) custom-call(s32[13]{0:T(128)S(4)} %get-tuple-element.31.meta_ref, bf16[6,512,512]{2,1,0:T(8,128)(2,1)S(1)} %get-tuple-element.34.tiles_ref, bf16[64,512]{1,0:T(8,128)(2,1)S(1)} %get-tuple-element.47.refs_0_.refs_4_, ...), custom_call_target="tpu_custom_call" | custom-call | flops 100663296 | bytes 3145728 | tf_op jit(solution)/shard_map/pallas_call | solution.py:23
  33.1 1.2 %collective-permute-start.19 = (bf16[64,512]{1,0:T(8,128)(2,1)S(1)}, bf16[64,512]{1,0:T(8,128)(2,1)S(1)}, u32[]{:S(2)}, u32[]{:S(2)}) collective-permute-start(bf16[64,512]{1,0:T(8,128)(2,1)S(1)} %get-tuple-element.53), channel_id=1, source_target_pairs={{0,3},{1,2},{2,1},{3,0},{4,7},{5,6},{6,5},{7,4},{8,11},{9,10},{10,... | collective-permute-start | bytes 196616 | tf_op jit(solution)/shard_map/ppermute | solution.py:19
  34.3 1.9 %collective-permute-start.20 = (bf16[64,512]{1,0:T(8,128)(2,1)S(1)}, bf16[64,512]{1,0:T(8,128)(2,1)S(1)}, u32[]{:S(2)}, u32[]{:S(2)}) collective-permute-start(bf16[64,512]{1,0:T(8,128)(2,1)S(1)} %get-tuple-element.54), channel_id=1, source_target_pairs={{0,2},{1,3},{2,0},{3,1},{4,6},{5,7},{6,4},{7,5},{8,10},{9,11},{10,... | collective-permute-start | bytes 196616 | tf_op jit(solution)/shard_map/ppermute | solution.py:19
  36.2 0.0 collective-permute-done.15.refs_3_
  36.2 0.5 %collective-permute-start.21 = (bf16[64,512]{1,0:T(8,128)(2,1)S(1)}, bf16[64,512]{1,0:T(8,128)(2,1)S(1)}, u32[]{:S(2)}, u32[]{:S(2)}) collective-permute-start(bf16[64,512]{1,0:T(8,128)(2,1)S(1)} %get-tuple-element.55), channel_id=1, source_target_pairs={{0,1},{1,0},{2,3},{3,2},{4,5},{5,4},{6,7},{7,6},{8,9},{9,8},{10,11... | collective-permute-start | bytes 196616 | tf_op jit(solution)/shard_map/ppermute | solution.py:19
  36.7 0.0 collective-permute-done.14.refs_2_
  36.7 0.0 collective-permute-done.13.refs_1_
  36.7 0.7 %shard_map.76 = (bf16[64,512]{1,0:T(8,128)(2,1)S(1)}, f32[64,512]{1,0:T(8,128)S(1)}) custom-call(s32[13]{0:T(128)S(4)} %get-tuple-element.31.meta_ref, bf16[6,512,512]{2,1,0:T(8,128)(2,1)S(1)} %get-tuple-element.32.tiles_ref, bf16[64,512]{1,0:T(8,128)(2,1)S(1)} %get-tuple-element.46.refs_0_, bf16[64,512]{1,0:T(8,128)(2,1)S(1)} %collective-permute-done.13.refs_1_, ...), custom_call_target="tpu_custom_call" | custom-call | flops 100663296 | bytes 3145728 | tf_op jit(solution)/shard_map/pallas_call | solution.py:23
  37.4 1.8 %collective-permute-start.17 = (bf16[64,512]{1,0:T(8,128)(2,1)S(1)}, bf16[64,512]{1,0:T(8,128)(2,1)S(1)}, u32[]{:S(2)}, u32[]{:S(2)}) collective-permute-start(bf16[64,512]{1,0:T(8,128)(2,1)S(1)} %get-tuple-element.50), channel_id=1, source_target_pairs={{0,16},{8,24},{16,0},{24,8},{1,17},{9,25},{17,1},{25,9},{2,18},{10... | collective-permute-start | bytes 196616 | tf_op jit(solution)/shard_map/ppermute | solution.py:19
  39.2 0.0 collective-permute-done.19.refs_0_
  39.2 0.0 collective-permute-done.20.refs_1_
  39.2 1.3 %collective-permute-done.21.refs_2_ = bf16[64,512]{1,0:T(8,128)(2,1)S(1)} collective-permute-done((bf16[64,512]{1,0:T(8,128)(2,1)S(1)}, bf16[64,512]{1,0:T(8,128)(2,1)S(1)}, u32[]{:S(2)}, u32[]{:S(2)}) %collective-permute-start.21) | collective-permute-done | bytes 65568 | tf_op jit(solution)/shard_map/ppermute | solution.py:19
  40.5 1.1 %collective-permute-start.22 = (bf16[32,512]{1,0:T(8,128)(2,1)S(1)}, bf16[32,512]{1,0:T(8,128)(2,1)S(1)}, u32[]{:S(2)}, u32[]{:S(2)}) collective-permute-start(bf16[32,512]{1,0:T(8,128)(2,1)S(1)} %get-tuple-element.57), channel_id=1, source_target_pairs={{0,4},{1,5},{2,6},{3,7},{4,0},{5,1},{6,2},{7,3},{8,12},{9,13},{10,... | collective-permute-start | bytes 98312 | tf_op jit(solution)/shard_map/ppermute | solution.py:19
  41.6 0.1 collective-permute-done.17.refs_0_
  41.7 0.1 collective-permute-start.18
  41.8 3.6 %collective-permute-done.22.refs_3_ = bf16[32,512]{1,0:T(8,128)(2,1)S(1)} collective-permute-done((bf16[32,512]{1,0:T(8,128)(2,1)S(1)}, bf16[32,512]{1,0:T(8,128)(2,1)S(1)}, u32[]{:S(2)}, u32[]{:S(2)}) %collective-permute-start.22) | collective-permute-done | bytes 32800 | tf_op jit(solution)/shard_map/ppermute | solution.py:19
  45.4 0.0 collective-permute-done.18.refs_1_
  45.4 0.6 %shard_map.79 = (bf16[32,512]{1,0:T(8,128)(2,1)}, bf16[32,512]{1,0:T(8,128)(2,1)}) custom-call(f32[32,512]{1,0:T(8,128)S(1)} %get-tuple-element.51.refs_0_, bf16[32,512]{1,0:T(8,128)(2,1)S(1)} %collective-permute-done.18.refs_1_, f32[32,512]{1,0:T(8,128)S(1)} %get-tuple-element.56.refs_2_, bf16[32,512]{1,0:T(8,128)(2,1)S(1)} %collective-permute-done.22.refs_3_, ...), custom_call_target="tpu_custom_call" | custom-call | flops 1000 | bytes 100000 | tf_op jit(solution)/shard_map/pallas_call | solution.py:23
  (4 shorter events, 0.1 us)
Async XLA Ops:
  0.6 8.6 %collective-permute-start.4 = (bf16[32,512]{1,0:T(8,128)(2,1)}, bf16[32,512]{1,0:T(8,128)(2,1)S(1)}, u32[]{:S(2)}, u32[]{:S(2)}) collective-permute-start(bf16[32,512]{1,0:T(8,128)(2,1)} %bitcast.3), channel_id=1, source_target_pairs={{0,16},{8,24},{16,0},{24,8},{1,17},{9,25},{17,1},{25,9},{2,18},{10... | collective-permute-start | bytes 98312 | tf_op jit(solution)/shard_map/ppermute | solution.py:19
  3.7 5.6 %collective-permute-start = (bf16[32,512]{1,0:T(8,128)(2,1)}, bf16[32,512]{1,0:T(8,128)(2,1)S(1)}, u32[]{:S(2)}, u32[]{:S(2)}) collective-permute-start(bf16[32,512]{1,0:T(8,128)(2,1)} %bitcast.4), channel_id=1, source_target_pairs={{0,4},{1,5},{2,6},{3,7},{4,0},{5,1},{6,2},{7,3},{8,12},{9,13},{10,... | collective-permute-start | bytes 98312 | tf_op jit(solution)/shard_map/ppermute | solution.py:19
  9.2 3.7 %collective-permute-start.5 = (bf16[64,512]{1,0:T(8,128)(2,1)S(1)}, bf16[64,512]{1,0:T(8,128)(2,1)S(1)}, u32[]{:S(2)}, u32[]{:S(2)}) collective-permute-start(bf16[64,512]{1,0:T(8,128)(2,1)S(1)} %shard_map.70.refs_0_), channel_id=1, source_target_pairs={{0,8},{8,0},{16,24},{24,16},{1,9},{9,1},{17,25},{25,17},{2,10},{10... | collective-permute-start | bytes 196616 | tf_op jit(solution)/shard_map/ppermute | solution.py:19
  9.3 7.3 %collective-permute-start.3 = (bf16[64,512]{1,0:T(8,128)(2,1)S(1)}, bf16[64,512]{1,0:T(8,128)(2,1)S(1)}, u32[]{:S(2)}, u32[]{:S(2)}) collective-permute-start(bf16[64,512]{1,0:T(8,128)(2,1)S(1)} %shard_map.69.refs_0_), channel_id=1, source_target_pairs={{0,3},{1,2},{2,1},{3,0},{4,7},{5,6},{6,5},{7,4},{8,11},{9,10},{10,... | collective-permute-start | bytes 196616 | tf_op jit(solution)/shard_map/ppermute | solution.py:19
  11.9 5.2 %collective-permute-start.2 = (bf16[64,512]{1,0:T(8,128)(2,1)S(1)}, bf16[64,512]{1,0:T(8,128)(2,1)S(1)}, u32[]{:S(2)}, u32[]{:S(2)}) collective-permute-start(bf16[64,512]{1,0:T(8,128)(2,1)S(1)} %shard_map.69.refs_0_), channel_id=1, source_target_pairs={{0,2},{1,3},{2,0},{3,1},{4,6},{5,7},{6,4},{7,5},{8,10},{9,11},{10,... | collective-permute-start | bytes 196616 | tf_op jit(solution)/shard_map/ppermute | solution.py:19
  12.3 4.8 %collective-permute-start.1 = (bf16[64,512]{1,0:T(8,128)(2,1)S(1)}, bf16[64,512]{1,0:T(8,128)(2,1)S(1)}, u32[]{:S(2)}, u32[]{:S(2)}) collective-permute-start(bf16[64,512]{1,0:T(8,128)(2,1)S(1)} %shard_map.69.refs_0_), channel_id=1, source_target_pairs={{0,1},{1,0},{2,3},{3,2},{4,5},{5,4},{6,7},{7,6},{8,9},{9,8},{10,11... | collective-permute-start | bytes 196616 | tf_op jit(solution)/shard_map/ppermute | solution.py:19
  13.6 6.0 %collective-permute-start.7 = (bf16[64,512]{1,0:T(8,128)(2,1)S(1)}, bf16[64,512]{1,0:T(8,128)(2,1)S(1)}, u32[]{:S(2)}, u32[]{:S(2)}) collective-permute-start(bf16[64,512]{1,0:T(8,128)(2,1)S(1)} %get-tuple-element.38), channel_id=1, source_target_pairs={{0,3},{1,2},{2,1},{3,0},{4,7},{5,6},{6,5},{7,4},{8,11},{9,10},{10,... | collective-permute-start | bytes 196616 | tf_op jit(solution)/shard_map/ppermute | solution.py:19
  16.1 4.3 %collective-permute-start.8 = (bf16[64,512]{1,0:T(8,128)(2,1)S(1)}, bf16[64,512]{1,0:T(8,128)(2,1)S(1)}, u32[]{:S(2)}, u32[]{:S(2)}) collective-permute-start(bf16[64,512]{1,0:T(8,128)(2,1)S(1)} %get-tuple-element.39), channel_id=1, source_target_pairs={{0,2},{1,3},{2,0},{3,1},{4,6},{5,7},{6,4},{7,5},{8,10},{9,11},{10,... | collective-permute-start | bytes 196616 | tf_op jit(solution)/shard_map/ppermute | solution.py:19
  16.6 4.3 %collective-permute-start.9 = (bf16[64,512]{1,0:T(8,128)(2,1)S(1)}, bf16[64,512]{1,0:T(8,128)(2,1)S(1)}, u32[]{:S(2)}, u32[]{:S(2)}) collective-permute-start(bf16[64,512]{1,0:T(8,128)(2,1)S(1)} %get-tuple-element.40), channel_id=1, source_target_pairs={{0,1},{1,0},{2,3},{3,2},{4,5},{5,4},{6,7},{7,6},{8,9},{9,8},{10,11... | collective-permute-start | bytes 196616 | tf_op jit(solution)/shard_map/ppermute | solution.py:19
  17.8 3.1 %collective-permute-start.6 = (bf16[64,512]{1,0:T(8,128)(2,1)S(1)}, bf16[64,512]{1,0:T(8,128)(2,1)S(1)}, u32[]{:S(2)}, u32[]{:S(2)}) collective-permute-start(bf16[64,512]{1,0:T(8,128)(2,1)S(1)} %get-tuple-element.37), channel_id=1, source_target_pairs={{0,8},{8,0},{16,24},{24,16},{1,9},{9,1},{17,25},{25,17},{2,10},{10... | collective-permute-start | bytes 196616 | tf_op jit(solution)/shard_map/ppermute | solution.py:19
  20.9 7.8 %collective-permute-start.10 = (bf16[64,512]{1,0:T(8,128)(2,1)S(1)}, bf16[64,512]{1,0:T(8,128)(2,1)S(1)}, u32[]{:S(2)}, u32[]{:S(2)}) collective-permute-start(bf16[64,512]{1,0:T(8,128)(2,1)S(1)} %get-tuple-element.41), channel_id=1, source_target_pairs={{0,20},{1,21},{2,22},{3,23},{4,16},{5,17},{6,18},{7,19},{8,28},{9,... | collective-permute-start | bytes 196616 | tf_op jit(solution)/shard_map/ppermute | solution.py:229
  22.8 5.9 %collective-permute-start.11 = (bf16[64,512]{1,0:T(8,128)(2,1)S(1)}, bf16[64,512]{1,0:T(8,128)(2,1)S(1)}, u32[]{:S(2)}, u32[]{:S(2)}) collective-permute-start(bf16[64,512]{1,0:T(8,128)(2,1)S(1)} %get-tuple-element.42), channel_id=1, source_target_pairs={{0,4},{1,5},{2,6},{3,7},{4,0},{5,1},{6,2},{7,3},{8,12},{9,13},{10,... | collective-permute-start | bytes 196616 | tf_op jit(solution)/shard_map/ppermute | solution.py:19
  23.9 4.9 %collective-permute-start.12 = (bf16[64,512]{1,0:T(8,128)(2,1)S(1)}, bf16[64,512]{1,0:T(8,128)(2,1)S(1)}, u32[]{:S(2)}, u32[]{:S(2)}) collective-permute-start(bf16[64,512]{1,0:T(8,128)(2,1)S(1)} %get-tuple-element.43), channel_id=1, source_target_pairs={{0,16},{8,24},{16,0},{24,8},{1,17},{9,25},{17,1},{25,9},{2,18},{10... | collective-permute-start | bytes 196616 | tf_op jit(solution)/shard_map/ppermute | solution.py:19
  28.8 3.6 %collective-permute-start.16 = (bf16[64,512]{1,0:T(8,128)(2,1)S(1)}, bf16[64,512]{1,0:T(8,128)(2,1)S(1)}, u32[]{:S(2)}, u32[]{:S(2)}) collective-permute-start(bf16[64,512]{1,0:T(8,128)(2,1)S(1)} %get-tuple-element.47.refs_0_.refs_4_), channel_id=1, source_target_pairs={{0,8},{8,0},{16,24},{24,16},{1,9},{9,1},{17,25},{25,17},{2,10},{10... | collective-permute-start | bytes 196616 | tf_op jit(solution)/shard_map/ppermute | solution.py:19
  28.9 7.3 %collective-permute-start.15 = (bf16[64,512]{1,0:T(8,128)(2,1)S(1)}, bf16[64,512]{1,0:T(8,128)(2,1)S(1)}, u32[]{:S(2)}, u32[]{:S(2)}) collective-permute-start(bf16[64,512]{1,0:T(8,128)(2,1)S(1)} %get-tuple-element.46.refs_0_), channel_id=1, source_target_pairs={{0,3},{1,2},{2,1},{3,0},{4,7},{5,6},{6,5},{7,4},{8,11},{9,10},{10,... | collective-permute-start | bytes 196616 | tf_op jit(solution)/shard_map/ppermute | solution.py:19
  30.1 6.6 %collective-permute-start.14 = (bf16[64,512]{1,0:T(8,128)(2,1)S(1)}, bf16[64,512]{1,0:T(8,128)(2,1)S(1)}, u32[]{:S(2)}, u32[]{:S(2)}) collective-permute-start(bf16[64,512]{1,0:T(8,128)(2,1)S(1)} %get-tuple-element.46.refs_0_), channel_id=1, source_target_pairs={{0,2},{1,3},{2,0},{3,1},{4,6},{5,7},{6,4},{7,5},{8,10},{9,11},{10,... | collective-permute-start | bytes 196616 | tf_op jit(solution)/shard_map/ppermute | solution.py:19
  31.9 4.8 %collective-permute-start.13 = (bf16[64,512]{1,0:T(8,128)(2,1)S(1)}, bf16[64,512]{1,0:T(8,128)(2,1)S(1)}, u32[]{:S(2)}, u32[]{:S(2)}) collective-permute-start(bf16[64,512]{1,0:T(8,128)(2,1)S(1)} %get-tuple-element.46.refs_0_), channel_id=1, source_target_pairs={{0,1},{1,0},{2,3},{3,2},{4,5},{5,4},{6,7},{7,6},{8,9},{9,8},{10,11... | collective-permute-start | bytes 196616 | tf_op jit(solution)/shard_map/ppermute | solution.py:19
  33.1 6.0 %collective-permute-start.19 = (bf16[64,512]{1,0:T(8,128)(2,1)S(1)}, bf16[64,512]{1,0:T(8,128)(2,1)S(1)}, u32[]{:S(2)}, u32[]{:S(2)}) collective-permute-start(bf16[64,512]{1,0:T(8,128)(2,1)S(1)} %get-tuple-element.53), channel_id=1, source_target_pairs={{0,3},{1,2},{2,1},{3,0},{4,7},{5,6},{6,5},{7,4},{8,11},{9,10},{10,... | collective-permute-start | bytes 196616 | tf_op jit(solution)/shard_map/ppermute | solution.py:19
  34.3 4.8 %collective-permute-start.20 = (bf16[64,512]{1,0:T(8,128)(2,1)S(1)}, bf16[64,512]{1,0:T(8,128)(2,1)S(1)}, u32[]{:S(2)}, u32[]{:S(2)}) collective-permute-start(bf16[64,512]{1,0:T(8,128)(2,1)S(1)} %get-tuple-element.54), channel_id=1, source_target_pairs={{0,2},{1,3},{2,0},{3,1},{4,6},{5,7},{6,4},{7,5},{8,10},{9,11},{10,... | collective-permute-start | bytes 196616 | tf_op jit(solution)/shard_map/ppermute | solution.py:19
  36.2 4.3 %collective-permute-start.21 = (bf16[64,512]{1,0:T(8,128)(2,1)S(1)}, bf16[64,512]{1,0:T(8,128)(2,1)S(1)}, u32[]{:S(2)}, u32[]{:S(2)}) collective-permute-start(bf16[64,512]{1,0:T(8,128)(2,1)S(1)} %get-tuple-element.55), channel_id=1, source_target_pairs={{0,1},{1,0},{2,3},{3,2},{4,5},{5,4},{6,7},{7,6},{8,9},{9,8},{10,11... | collective-permute-start | bytes 196616 | tf_op jit(solution)/shard_map/ppermute | solution.py:19
  37.4 4.3 %collective-permute-start.17 = (bf16[64,512]{1,0:T(8,128)(2,1)S(1)}, bf16[64,512]{1,0:T(8,128)(2,1)S(1)}, u32[]{:S(2)}, u32[]{:S(2)}) collective-permute-start(bf16[64,512]{1,0:T(8,128)(2,1)S(1)} %get-tuple-element.50), channel_id=1, source_target_pairs={{0,16},{8,24},{16,0},{24,8},{1,17},{9,25},{17,1},{25,9},{2,18},{10... | collective-permute-start | bytes 196616 | tf_op jit(solution)/shard_map/ppermute | solution.py:19
  40.5 4.9 %collective-permute-start.22 = (bf16[32,512]{1,0:T(8,128)(2,1)S(1)}, bf16[32,512]{1,0:T(8,128)(2,1)S(1)}, u32[]{:S(2)}, u32[]{:S(2)}) collective-permute-start(bf16[32,512]{1,0:T(8,128)(2,1)S(1)} %get-tuple-element.57), channel_id=1, source_target_pairs={{0,4},{1,5},{2,6},{3,7},{4,0},{5,1},{6,2},{7,3},{8,12},{9,13},{10,... | collective-permute-start | bytes 98312 | tf_op jit(solution)/shard_map/ppermute | solution.py:19
  41.7 3.6 %collective-permute-start.18 = (bf16[32,512]{1,0:T(8,128)(2,1)S(1)}, bf16[32,512]{1,0:T(8,128)(2,1)S(1)}, u32[]{:S(2)}, u32[]{:S(2)}) collective-permute-start(bf16[32,512]{1,0:T(8,128)(2,1)S(1)} %get-tuple-element.52), channel_id=1, source_target_pairs={{0,8},{8,0},{16,24},{24,16},{1,9},{9,1},{17,25},{25,17},{2,10},{10... | collective-permute-start | bytes 98312 | tf_op jit(solution)/shard_map/ppermute | solution.py:19

commit v5 on v4

--- a/solution.py
+++ b/solution.py
@@ -183,6 +183,7 @@
     col_bits = [1 << k for k in range(n_col.bit_length() - 1)]
     row_pair_bit, row_inner = row_bits[-1], combinations(row_bits[:-1])
     col_pair_bit, col_inner = col_bits[-1], combinations(col_bits[:-1])
+    col_scatter = col_inner[:1] + col_inner[:0:-1]
     start = start_vecs.reshape(n_vec, width)
     tiles, turned, start_here, meta = prepare(blocks, start, block_rows, block_cols, block_count)
     one, two = (n_vec, width), (2 * n_vec, width)
@@ -199,7 +200,7 @@
         return ref[rows, :].astype(f32)
 
     start_y, start_z = swap(start, "row", row_pair_bit), swap(start, "col", col_pair_bit)
-    d_terms, m_terms = products(join(start_here, start_y), join(start_here, start_z), [row_inner], [col_inner])
+    d_terms, m_terms = products(join(start_here, start_y), join(start_here, start_z), [row_inner], [col_scatter])
 
     n_d = len(d_terms)
 
@@ -246,7 +247,7 @@
         first_update, [(two, bf16), (two, bf16)],
         from_diag, from_z, from_y, d_sum, m_sum, start_here, start_y, start_z,
     )
-    d_terms, m_terms = products(row_pair, col_pair, [[row_pair_bit], row_inner], [col_inner, [col_pair_bit]])
+    d_terms, m_terms = products(row_pair, col_pair, [[row_pair_bit], row_inner], [col_scatter, [col_pair_bit]])
     n_last = len(d_terms)
     terms = [*d_terms, *m_terms]
 

time: 46.2 us -> 45.2 us (0.978)
  waiting for transfers between devices: 11.3 us -> 9.33 us
  starting transfers between devices: 27.5 us -> 28.5 us
    ppermute x22, waiting for transfers between devices: 7.97 us -> 5.66 us  [swap(): lax.ppermute(value, axis, [(i, i ^ pattern) for i in range(lax.axis_size(...]
    ppermute x22, starting transfers between devices: 25.6 us -> 26.4 us  [swap(): lax.ppermute(value, axis, [(i, i ^ pattern) for i in range(lax.axis_size(...]
where the time goes in v5:
time: 45.2 us; the launch traced here: 45.1 us
  starting transfers between devices  28.5 us (63%)
  waiting for transfers between devices  9.33 us (21%)
  Pallas kernels  5.78 us (13%)
  between operations  1.42 us (3%)
    ppermute x22, starting transfers between devices, swap(): lax.ppermute(value, axis, [(i, i ^ pattern) for i in range(lax.axis_size(...  26.4 us
    ppermute x22, waiting for transfers between devices, swap(): lax.ppermute(value, axis, [(i, i ^ pattern) for i in range(lax.axis_size(...  5.66 us
    ppermute x1, waiting for transfers between devices, body(): from_diag = lax.ppermute(to_diag, ('row', 'col'), diagonal)  3.67 us
    pallas_call x11, Pallas kernels, local_call(): pl.pallas_call(kernel, out_shape=[jax.ShapeDtypeStruct(s, d) for s, d in...  3.5 us
    pallas_call x1, Pallas kernels, prepare(): pl.pallas_call(kernel, out_shape=[pltpu.VMEM(blocks.shape[2:], blocks.dty...  2.29 us
    ppermute x1, starting transfers between devices, body(): from_diag = lax.ppermute(to_diag, ('row', 'col'), diagonal)  2.14 us
  transfers between devices with their start and end apart: 23, of which 7 were waited for; matrix products, arithmetic and copies ran while one was open for 0% of the time, Pallas kernels for 11%

profile of v5, /device:TPU:0, one launch (start us, length us, event | category | flops | bytes accessed | tf_op | source)
XLA Modules:
  0.0 45.1 jit_solution(12963125535808081924)
XLA Ops:
  0.6 3.0 %collective-permute-start.4 = (bf16[32,512]{1,0:T(8,128)(2,1)}, bf16[32,512]{1,0:T(8,128)(2,1)S(1)}, u32[]{:S(2)}, u32[]{:S(2)}) collective-permute-start(bf16[32,512]{1,0:T(8,128)(2,1)} %bitcast.3), channel_id=1, source_target_pairs={{0,16},{8,24},{16,0},{24,8},{1,17},{9,25},{17,1},{25,9},{2,18},{10... | collective-permute-start | bytes 98312 | tf_op jit(solution)/shard_map/ppermute | solution.py:19
  3.7 2.6 %collective-permute-start = (bf16[32,512]{1,0:T(8,128)(2,1)}, bf16[32,512]{1,0:T(8,128)(2,1)S(1)}, u32[]{:S(2)}, u32[]{:S(2)}) collective-permute-start(bf16[32,512]{1,0:T(8,128)(2,1)} %bitcast.4), channel_id=1, source_target_pairs={{0,4},{1,5},{2,6},{3,7},{4,0},{5,1},{6,2},{7,3},{8,12},{9,13},{10,... | collective-permute-start | bytes 98312 | tf_op jit(solution)/shard_map/ppermute | solution.py:19
  6.9 2.3 %shard_map.68 = (bf16[6,512,512]{2,1,0:T(8,128)(2,1)S(1)}, bf16[6,512,512]{2,1,0:T(8,128)(2,1)S(1)}, bf16[32,512]{1,0:T(8,128)(2,1)S(1)}, s32[13]{0:T(128)S(4)}) custom-call(s32[1,1]{1,0:T(1,128)S(6)} %copy.7.count_ref, s32[1,1,6]{2,1,0:T(1,128)} %rows_hbm.1, s32[1,1,6]{2,1,0:T(1,128)} %cols_hbm.1, bf16[1,1,6,512,512]{4,3,2,1,0:T(8,128)(2,1)} %blocks_hbm.1, ...), custom_call_target="tpu_custom_call" | custom-call | flops 1000 | bytes 6291456 | tf_op jit(solution)/shard_map/pallas_call | solution.py:60
  9.2 0.0 collective-permute-done.4.second_ref.cur_y
  9.2 0.1 collective-permute-start.5
  9.3 0.0 collective-permute-done.second_ref.cur_z
  9.3 2.6 %collective-permute-start.3 = (bf16[64,512]{1,0:T(8,128)(2,1)S(1)}, bf16[64,512]{1,0:T(8,128)(2,1)S(1)}, u32[]{:S(2)}, u32[]{:S(2)}) collective-permute-start(bf16[64,512]{1,0:T(8,128)(2,1)S(1)} %shard_map.69.refs_0_), channel_id=1, source_target_pairs={{0,3},{1,2},{2,1},{3,0},{4,7},{5,6},{6,5},{7,4},{8,11},{9,10},{10,... | collective-permute-start | bytes 196616 | tf_op jit(solution)/shard_map/ppermute | solution.py:19
  11.9 0.4 collective-permute-start.2
  12.3 0.5 %collective-permute-start.1 = (bf16[64,512]{1,0:T(8,128)(2,1)S(1)}, bf16[64,512]{1,0:T(8,128)(2,1)S(1)}, u32[]{:S(2)}, u32[]{:S(2)}) collective-permute-start(bf16[64,512]{1,0:T(8,128)(2,1)S(1)} %shard_map.69.refs_0_), channel_id=1, source_target_pairs={{0,1},{1,0},{2,3},{3,2},{4,5},{5,4},{6,7},{7,6},{8,9},{9,8},{10,11... | collective-permute-start | bytes 196616 | tf_op jit(solution)/shard_map/ppermute | solution.py:19
  12.9 0.0 collective-permute-done.5.refs_1_
  12.9 0.7 %shard_map.71 = (bf16[64,512]{1,0:T(8,128)(2,1)S(1)}, bf16[64,512]{1,0:T(8,128)(2,1)S(1)}, bf16[64,512]{1,0:T(8,128)(2,1)S(1)}, f32[64,512]{1,0:T(8,128)S(1)}) custom-call(s32[13]{0:T(128)S(4)} %get-tuple-element.31.meta_ref, bf16[6,512,512]{2,1,0:T(8,128)(2,1)S(1)} %get-tuple-element.34.tiles_ref, bf16[64,512]{1,0:T(8,128)(2,1)S(1)} %shard_map.70.refs_0_, ...), custom_call_target="tpu_custom_call" | custom-call | flops 100663296 | bytes 3145728 | tf_op jit(solution)/shard_map/pallas_call | solution.py:23
  13.6 2.6 %collective-permute-start.7 = (bf16[64,512]{1,0:T(8,128)(2,1)S(1)}, bf16[64,512]{1,0:T(8,128)(2,1)S(1)}, u32[]{:S(2)}, u32[]{:S(2)}) collective-permute-start(bf16[64,512]{1,0:T(8,128)(2,1)S(1)} %get-tuple-element.38), channel_id=1, source_target_pairs={{0,3},{1,2},{2,1},{3,0},{4,7},{5,6},{6,5},{7,4},{8,11},{9,10},{10,... | collective-permute-start | bytes 196616 | tf_op jit(solution)/shard_map/ppermute | solution.py:19
  16.1 0.5 %collective-permute-start.8 = (bf16[64,512]{1,0:T(8,128)(2,1)S(1)}, bf16[64,512]{1,0:T(8,128)(2,1)S(1)}, u32[]{:S(2)}, u32[]{:S(2)}) collective-permute-start(bf16[64,512]{1,0:T(8,128)(2,1)S(1)} %get-tuple-element.39), channel_id=1, source_target_pairs={{0,1},{1,0},{2,3},{3,2},{4,5},{5,4},{6,7},{7,6},{8,9},{9,8},{10,11... | collective-permute-start | bytes 196616 | tf_op jit(solution)/shard_map/ppermute | solution.py:19
  16.7 0.0 collective-permute-done.3.refs_3_
  16.7 0.4 collective-permute-start.9
  17.1 0.0 collective-permute-done.2.refs_2_
  17.1 0.0 collective-permute-done.1.refs_1_
  17.1 0.7 %shard_map.72 = (bf16[64,512]{1,0:T(8,128)(2,1)S(1)}, f32[64,512]{1,0:T(8,128)S(1)}) custom-call(s32[13]{0:T(128)S(4)} %get-tuple-element.31.meta_ref, bf16[6,512,512]{2,1,0:T(8,128)(2,1)S(1)} %get-tuple-element.32.tiles_ref, bf16[64,512]{1,0:T(8,128)(2,1)S(1)} %shard_map.69.refs_0_, bf16[64,512]{1,0:T(8,128)(2,1)S(1)} %collective-permute-done.1.refs_1_, ...), custom_call_target="tpu_custom_call" | custom-call | flops 100663296 | bytes 3145728 | tf_op jit(solution)/shard_map/pallas_call | solution.py:23
  17.8 0.1 collective-permute-start.6
  17.9 1.0 %collective-permute-done.7.refs_3_ = bf16[64,512]{1,0:T(8,128)(2,1)S(1)} collective-permute-done((bf16[64,512]{1,0:T(8,128)(2,1)S(1)}, bf16[64,512]{1,0:T(8,128)(2,1)S(1)}, u32[]{:S(2)}, u32[]{:S(2)}) %collective-permute-start.7) | collective-permute-done | bytes 65568 | tf_op jit(solution)/shard_map/ppermute | solution.py:19
  18.9 1.5 %collective-permute-done.8.refs_4_ = bf16[64,512]{1,0:T(8,128)(2,1)S(1)} collective-permute-done((bf16[64,512]{1,0:T(8,128)(2,1)S(1)}, bf16[64,512]{1,0:T(8,128)(2,1)S(1)}, u32[]{:S(2)}, u32[]{:S(2)}) %collective-permute-start.8) | collective-permute-done | bytes 65568 | tf_op jit(solution)/shard_map/ppermute | solution.py:19
  20.4 0.5 %collective-permute-done.9.refs_5_ = bf16[64,512]{1,0:T(8,128)(2,1)S(1)} collective-permute-done((bf16[64,512]{1,0:T(8,128)(2,1)S(1)}, bf16[64,512]{1,0:T(8,128)(2,1)S(1)}, u32[]{:S(2)}, u32[]{:S(2)}) %collective-permute-start.9) | collective-permute-done | bytes 65568 | tf_op jit(solution)/shard_map/ppermute | solution.py:19
  20.9 0.0 collective-permute-done.6.refs_1_
  20.9 0.1 shard_map.73
  21.0 2.1 %collective-permute-start.10 = (bf16[64,512]{1,0:T(8,128)(2,1)S(1)}, bf16[64,512]{1,0:T(8,128)(2,1)S(1)}, u32[]{:S(2)}, u32[]{:S(2)}) collective-permute-start(bf16[64,512]{1,0:T(8,128)(2,1)S(1)} %get-tuple-element.41), channel_id=1, source_target_pairs={{0,20},{1,21},{2,22},{3,23},{4,16},{5,17},{6,18},{7,19},{8,28},{9,... | collective-permute-start | bytes 196616 | tf_op jit(solution)/shard_map/ppermute | solution.py:230
  23.1 0.8 %collective-permute-start.11 = (bf16[64,512]{1,0:T(8,128)(2,1)S(1)}, bf16[64,512]{1,0:T(8,128)(2,1)S(1)}, u32[]{:S(2)}, u32[]{:S(2)}) collective-permute-start(bf16[64,512]{1,0:T(8,128)(2,1)S(1)} %get-tuple-element.42), channel_id=1, source_target_pairs={{0,4},{1,5},{2,6},{3,7},{4,0},{5,1},{6,2},{7,3},{8,12},{9,13},{10,... | collective-permute-start | bytes 196616 | tf_op jit(solution)/shard_map/ppermute | solution.py:19
  23.9 1.5 %collective-permute-start.12 = (bf16[64,512]{1,0:T(8,128)(2,1)S(1)}, bf16[64,512]{1,0:T(8,128)(2,1)S(1)}, u32[]{:S(2)}, u32[]{:S(2)}) collective-permute-start(bf16[64,512]{1,0:T(8,128)(2,1)S(1)} %get-tuple-element.43), channel_id=1, source_target_pairs={{0,16},{8,24},{16,0},{24,8},{1,17},{9,25},{17,1},{25,9},{2,18},{10... | collective-permute-start | bytes 196616 | tf_op jit(solution)/shard_map/ppermute | solution.py:19
  25.5 3.7 %collective-permute-done.10.diag_ref = bf16[64,512]{1,0:T(8,128)(2,1)S(1)} collective-permute-done((bf16[64,512]{1,0:T(8,128)(2,1)S(1)}, bf16[64,512]{1,0:T(8,128)(2,1)S(1)}, u32[]{:S(2)}, u32[]{:S(2)}) %collective-permute-start.10) | collective-permute-done | bytes 65568 | tf_op jit(solution)/shard_map/ppermute | solution.py:230
  29.1 0.0 collective-permute-done.11.z_ref
  29.1 0.0 collective-permute-done.12.y_ref
  29.1 0.1 shard_map.74
  29.2 0.1 collective-permute-start.16
  29.3 0.6 %collective-permute-start.15 = (bf16[64,512]{1,0:T(8,128)(2,1)S(1)}, bf16[64,512]{1,0:T(8,128)(2,1)S(1)}, u32[]{:S(2)}, u32[]{:S(2)}) collective-permute-start(bf16[64,512]{1,0:T(8,128)(2,1)S(1)} %get-tuple-element.46.refs_0_), channel_id=1, source_target_pairs={{0,3},{1,2},{2,1},{3,0},{4,7},{5,6},{6,5},{7,4},{8,11},{9,10},{10,... | collective-permute-start | bytes 196616 | tf_op jit(solution)/shard_map/ppermute | solution.py:19
  29.8 2.5 %collective-permute-start.14 = (bf16[64,512]{1,0:T(8,128)(2,1)S(1)}, bf16[64,512]{1,0:T(8,128)(2,1)S(1)}, u32[]{:S(2)}, u32[]{:S(2)}) collective-permute-start(bf16[64,512]{1,0:T(8,128)(2,1)S(1)} %get-tuple-element.46.refs_0_), channel_id=1, source_target_pairs={{0,2},{1,3},{2,0},{3,1},{4,6},{5,7},{6,4},{7,5},{8,10},{9,11},{10,... | collective-permute-start | bytes 196616 | tf_op jit(solution)/shard_map/ppermute | solution.py:19
  32.3 0.5 %collective-permute-start.13 = (bf16[64,512]{1,0:T(8,128)(2,1)S(1)}, bf16[64,512]{1,0:T(8,128)(2,1)S(1)}, u32[]{:S(2)}, u32[]{:S(2)}) collective-permute-start(bf16[64,512]{1,0:T(8,128)(2,1)S(1)} %get-tuple-element.46.refs_0_), channel_id=1, source_target_pairs={{0,1},{1,0},{2,3},{3,2},{4,5},{5,4},{6,7},{7,6},{8,9},{9,8},{10,11... | collective-permute-start | bytes 196616 | tf_op jit(solution)/shard_map/ppermute | solution.py:19
  32.8 0.0 collective-permute-done.16.refs_1_
  32.8 0.7 %shard_map.75 = (bf16[64,512]{1,0:T(8,128)(2,1)S(1)}, bf16[64,512]{1,0:T(8,128)(2,1)S(1)}, bf16[64,512]{1,0:T(8,128)(2,1)S(1)}, f32[64,512]{1,0:T(8,128)S(1)}) custom-call(s32[13]{0:T(128)S(4)} %get-tuple-element.31.meta_ref, bf16[6,512,512]{2,1,0:T(8,128)(2,1)S(1)} %get-tuple-element.34.tiles_ref, bf16[64,512]{1,0:T(8,128)(2,1)S(1)} %get-tuple-element.47.refs_0_.refs_4_, ...), custom_call_target="tpu_custom_call" | custom-call | flops 100663296 | bytes 3145728 | tf_op jit(solution)/shard_map/pallas_call | solution.py:23
  33.5 1.0 %collective-permute-start.19 = (bf16[64,512]{1,0:T(8,128)(2,1)S(1)}, bf16[64,512]{1,0:T(8,128)(2,1)S(1)}, u32[]{:S(2)}, u32[]{:S(2)}) collective-permute-start(bf16[64,512]{1,0:T(8,128)(2,1)S(1)} %get-tuple-element.53), channel_id=1, source_target_pairs={{0,3},{1,2},{2,1},{3,0},{4,7},{5,6},{6,5},{7,4},{8,11},{9,10},{10,... | collective-permute-start | bytes 196616 | tf_op jit(solution)/shard_map/ppermute | solution.py:19
  34.5 0.6 %collective-permute-start.20 = (bf16[64,512]{1,0:T(8,128)(2,1)S(1)}, bf16[64,512]{1,0:T(8,128)(2,1)S(1)}, u32[]{:S(2)}, u32[]{:S(2)}) collective-permute-start(bf16[64,512]{1,0:T(8,128)(2,1)S(1)} %get-tuple-element.54), channel_id=1, source_target_pairs={{0,1},{1,0},{2,3},{3,2},{4,5},{5,4},{6,7},{7,6},{8,9},{9,8},{10,11... | collective-permute-start | bytes 196616 | tf_op jit(solution)/shard_map/ppermute | solution.py:19
  35.2 0.0 collective-permute-done.15.refs_3_
  35.2 1.9 %collective-permute-start.21 = (bf16[64,512]{1,0:T(8,128)(2,1)S(1)}, bf16[64,512]{1,0:T(8,128)(2,1)S(1)}, u32[]{:S(2)}, u32[]{:S(2)}) collective-permute-start(bf16[64,512]{1,0:T(8,128)(2,1)S(1)} %get-tuple-element.55), channel_id=1, source_target_pairs={{0,2},{1,3},{2,0},{3,1},{4,6},{5,7},{6,4},{7,5},{8,10},{9,11},{10,... | collective-permute-start | bytes 196616 | tf_op jit(solution)/shard_map/ppermute | solution.py:19
  37.1 0.0 collective-permute-done.14.refs_2_
  37.1 0.0 collective-permute-done.13.refs_1_
  37.1 0.7 %shard_map.76 = (bf16[64,512]{1,0:T(8,128)(2,1)S(1)}, f32[64,512]{1,0:T(8,128)S(1)}) custom-call(s32[13]{0:T(128)S(4)} %get-tuple-element.31.meta_ref, bf16[6,512,512]{2,1,0:T(8,128)(2,1)S(1)} %get-tuple-element.32.tiles_ref, bf16[64,512]{1,0:T(8,128)(2,1)S(1)} %get-tuple-element.46.refs_0_, bf16[64,512]{1,0:T(8,128)(2,1)S(1)} %collective-permute-done.13.refs_1_, ...), custom_call_target="tpu_custom_call" | custom-call | flops 100663296 | bytes 3145728 | tf_op jit(solution)/shard_map/pallas_call | solution.py:23
  37.8 1.3 %collective-permute-start.17 = (bf16[64,512]{1,0:T(8,128)(2,1)S(1)}, bf16[64,512]{1,0:T(8,128)(2,1)S(1)}, u32[]{:S(2)}, u32[]{:S(2)}) collective-permute-start(bf16[64,512]{1,0:T(8,128)(2,1)S(1)} %get-tuple-element.50), channel_id=1, source_target_pairs={{0,16},{8,24},{16,0},{24,8},{1,17},{9,25},{17,1},{25,9},{2,18},{10... | collective-permute-start | bytes 196616 | tf_op jit(solution)/shard_map/ppermute | solution.py:19
  39.1 0.3 collective-permute-done.19.refs_0_
  39.4 0.1 collective-permute-done.20.refs_1_
  39.5 0.0 collective-permute-done.21.refs_2_
  39.6 2.6 %collective-permute-start.22 = (bf16[32,512]{1,0:T(8,128)(2,1)S(1)}, bf16[32,512]{1,0:T(8,128)(2,1)S(1)}, u32[]{:S(2)}, u32[]{:S(2)}) collective-permute-start(bf16[32,512]{1,0:T(8,128)(2,1)S(1)} %get-tuple-element.57), channel_id=1, source_target_pairs={{0,4},{1,5},{2,6},{3,7},{4,0},{5,1},{6,2},{7,3},{8,12},{9,13},{10,... | collective-permute-start | bytes 98312 | tf_op jit(solution)/shard_map/ppermute | solution.py:19
  42.2 0.0 collective-permute-done.17.refs_0_
  42.2 0.1 collective-permute-start.18
  42.3 2.1 %collective-permute-done.22.refs_3_ = bf16[32,512]{1,0:T(8,128)(2,1)S(1)} collective-permute-done((bf16[32,512]{1,0:T(8,128)(2,1)S(1)}, bf16[32,512]{1,0:T(8,128)(2,1)S(1)}, u32[]{:S(2)}, u32[]{:S(2)}) %collective-permute-start.22) | collective-permute-done | bytes 32800 | tf_op jit(solution)/shard_map/ppermute | solution.py:19
  44.4 0.0 collective-permute-done.18.refs_1_
  44.4 0.6 %shard_map.79 = (bf16[32,512]{1,0:T(8,128)(2,1)}, bf16[32,512]{1,0:T(8,128)(2,1)}) custom-call(f32[32,512]{1,0:T(8,128)S(1)} %get-tuple-element.51.refs_0_, bf16[32,512]{1,0:T(8,128)(2,1)S(1)} %collective-permute-done.18.refs_1_, f32[32,512]{1,0:T(8,128)S(1)} %get-tuple-element.56.refs_2_, bf16[32,512]{1,0:T(8,128)(2,1)S(1)} %collective-permute-done.22.refs_3_, ...), custom_call_target="tpu_custom_call" | custom-call | flops 1000 | bytes 100000 | tf_op jit(solution)/shard_map/pallas_call | solution.py:23
  (4 shorter events, 0.1 us)
Async XLA Ops:
  0.6 8.6 %collective-permute-start.4 = (bf16[32,512]{1,0:T(8,128)(2,1)}, bf16[32,512]{1,0:T(8,128)(2,1)S(1)}, u32[]{:S(2)}, u32[]{:S(2)}) collective-permute-start(bf16[32,512]{1,0:T(8,128)(2,1)} %bitcast.3), channel_id=1, source_target_pairs={{0,16},{8,24},{16,0},{24,8},{1,17},{9,25},{17,1},{25,9},{2,18},{10... | collective-permute-start | bytes 98312 | tf_op jit(solution)/shard_map/ppermute | solution.py:19
  3.7 5.6 %collective-permute-start = (bf16[32,512]{1,0:T(8,128)(2,1)}, bf16[32,512]{1,0:T(8,128)(2,1)S(1)}, u32[]{:S(2)}, u32[]{:S(2)}) collective-permute-start(bf16[32,512]{1,0:T(8,128)(2,1)} %bitcast.4), channel_id=1, source_target_pairs={{0,4},{1,5},{2,6},{3,7},{4,0},{5,1},{6,2},{7,3},{8,12},{9,13},{10,... | collective-permute-start | bytes 98312 | tf_op jit(solution)/shard_map/ppermute | solution.py:19
  9.2 3.7 %collective-permute-start.5 = (bf16[64,512]{1,0:T(8,128)(2,1)S(1)}, bf16[64,512]{1,0:T(8,128)(2,1)S(1)}, u32[]{:S(2)}, u32[]{:S(2)}) collective-permute-start(bf16[64,512]{1,0:T(8,128)(2,1)S(1)} %shard_map.70.refs_0_), channel_id=1, source_target_pairs={{0,8},{8,0},{16,24},{24,16},{1,9},{9,1},{17,25},{25,17},{2,10},{10... | collective-permute-start | bytes 196616 | tf_op jit(solution)/shard_map/ppermute | solution.py:19
  9.3 7.3 %collective-permute-start.3 = (bf16[64,512]{1,0:T(8,128)(2,1)S(1)}, bf16[64,512]{1,0:T(8,128)(2,1)S(1)}, u32[]{:S(2)}, u32[]{:S(2)}) collective-permute-start(bf16[64,512]{1,0:T(8,128)(2,1)S(1)} %shard_map.69.refs_0_), channel_id=1, source_target_pairs={{0,3},{1,2},{2,1},{3,0},{4,7},{5,6},{6,5},{7,4},{8,11},{9,10},{10,... | collective-permute-start | bytes 196616 | tf_op jit(solution)/shard_map/ppermute | solution.py:19
  11.9 5.2 %collective-permute-start.2 = (bf16[64,512]{1,0:T(8,128)(2,1)S(1)}, bf16[64,512]{1,0:T(8,128)(2,1)S(1)}, u32[]{:S(2)}, u32[]{:S(2)}) collective-permute-start(bf16[64,512]{1,0:T(8,128)(2,1)S(1)} %shard_map.69.refs_0_), channel_id=1, source_target_pairs={{0,2},{1,3},{2,0},{3,1},{4,6},{5,7},{6,4},{7,5},{8,10},{9,11},{10,... | collective-permute-start | bytes 196616 | tf_op jit(solution)/shard_map/ppermute | solution.py:19
  12.3 4.8 %collective-permute-start.1 = (bf16[64,512]{1,0:T(8,128)(2,1)S(1)}, bf16[64,512]{1,0:T(8,128)(2,1)S(1)}, u32[]{:S(2)}, u32[]{:S(2)}) collective-permute-start(bf16[64,512]{1,0:T(8,128)(2,1)S(1)} %shard_map.69.refs_0_), channel_id=1, source_target_pairs={{0,1},{1,0},{2,3},{3,2},{4,5},{5,4},{6,7},{7,6},{8,9},{9,8},{10,11... | collective-permute-start | bytes 196616 | tf_op jit(solution)/shard_map/ppermute | solution.py:19
  13.6 5.3 %collective-permute-start.7 = (bf16[64,512]{1,0:T(8,128)(2,1)S(1)}, bf16[64,512]{1,0:T(8,128)(2,1)S(1)}, u32[]{:S(2)}, u32[]{:S(2)}) collective-permute-start(bf16[64,512]{1,0:T(8,128)(2,1)S(1)} %get-tuple-element.38), channel_id=1, source_target_pairs={{0,3},{1,2},{2,1},{3,0},{4,7},{5,6},{6,5},{7,4},{8,11},{9,10},{10,... | collective-permute-start | bytes 196616 | tf_op jit(solution)/shard_map/ppermute | solution.py:19
  16.1 4.3 %collective-permute-start.8 = (bf16[64,512]{1,0:T(8,128)(2,1)S(1)}, bf16[64,512]{1,0:T(8,128)(2,1)S(1)}, u32[]{:S(2)}, u32[]{:S(2)}) collective-permute-start(bf16[64,512]{1,0:T(8,128)(2,1)S(1)} %get-tuple-element.39), channel_id=1, source_target_pairs={{0,1},{1,0},{2,3},{3,2},{4,5},{5,4},{6,7},{7,6},{8,9},{9,8},{10,11... | collective-permute-start | bytes 196616 | tf_op jit(solution)/shard_map/ppermute | solution.py:19
  16.7 4.3 %collective-permute-start.9 = (bf16[64,512]{1,0:T(8,128)(2,1)S(1)}, bf16[64,512]{1,0:T(8,128)(2,1)S(1)}, u32[]{:S(2)}, u32[]{:S(2)}) collective-permute-start(bf16[64,512]{1,0:T(8,128)(2,1)S(1)} %get-tuple-element.40), channel_id=1, source_target_pairs={{0,2},{1,3},{2,0},{3,1},{4,6},{5,7},{6,4},{7,5},{8,10},{9,11},{10,... | collective-permute-start | bytes 196616 | tf_op jit(solution)/shard_map/ppermute | solution.py:19
  17.8 3.1 %collective-permute-start.6 = (bf16[64,512]{1,0:T(8,128)(2,1)S(1)}, bf16[64,512]{1,0:T(8,128)(2,1)S(1)}, u32[]{:S(2)}, u32[]{:S(2)}) collective-permute-start(bf16[64,512]{1,0:T(8,128)(2,1)S(1)} %get-tuple-element.37), channel_id=1, source_target_pairs={{0,8},{8,0},{16,24},{24,16},{1,9},{9,1},{17,25},{25,17},{2,10},{10... | collective-permute-start | bytes 196616 | tf_op jit(solution)/shard_map/ppermute | solution.py:19
  21.0 8.1 %collective-permute-start.10 = (bf16[64,512]{1,0:T(8,128)(2,1)S(1)}, bf16[64,512]{1,0:T(8,128)(2,1)S(1)}, u32[]{:S(2)}, u32[]{:S(2)}) collective-permute-start(bf16[64,512]{1,0:T(8,128)(2,1)S(1)} %get-tuple-element.41), channel_id=1, source_target_pairs={{0,20},{1,21},{2,22},{3,23},{4,16},{5,17},{6,18},{7,19},{8,28},{9,... | collective-permute-start | bytes 196616 | tf_op jit(solution)/shard_map/ppermute | solution.py:230
  23.1 6.0 %collective-permute-start.11 = (bf16[64,512]{1,0:T(8,128)(2,1)S(1)}, bf16[64,512]{1,0:T(8,128)(2,1)S(1)}, u32[]{:S(2)}, u32[]{:S(2)}) collective-permute-start(bf16[64,512]{1,0:T(8,128)(2,1)S(1)} %get-tuple-element.42), channel_id=1, source_target_pairs={{0,4},{1,5},{2,6},{3,7},{4,0},{5,1},{6,2},{7,3},{8,12},{9,13},{10,... | collective-permute-start | bytes 196616 | tf_op jit(solution)/shard_map/ppermute | solution.py:19
  23.9 5.2 %collective-permute-start.12 = (bf16[64,512]{1,0:T(8,128)(2,1)S(1)}, bf16[64,512]{1,0:T(8,128)(2,1)S(1)}, u32[]{:S(2)}, u32[]{:S(2)}) collective-permute-start(bf16[64,512]{1,0:T(8,128)(2,1)S(1)} %get-tuple-element.43), channel_id=1, source_target_pairs={{0,16},{8,24},{16,0},{24,8},{1,17},{9,25},{17,1},{25,9},{2,18},{10... | collective-permute-start | bytes 196616 | tf_op jit(solution)/shard_map/ppermute | solution.py:19
  29.2 3.6 %collective-permute-start.16 = (bf16[64,512]{1,0:T(8,128)(2,1)S(1)}, bf16[64,512]{1,0:T(8,128)(2,1)S(1)}, u32[]{:S(2)}, u32[]{:S(2)}) collective-permute-start(bf16[64,512]{1,0:T(8,128)(2,1)S(1)} %get-tuple-element.47.refs_0_.refs_4_), channel_id=1, source_target_pairs={{0,8},{8,0},{16,24},{24,16},{1,9},{9,1},{17,25},{25,17},{2,10},{10... | collective-permute-start | bytes 196616 | tf_op jit(solution)/shard_map/ppermute | solution.py:19
  29.3 5.9 %collective-permute-start.15 = (bf16[64,512]{1,0:T(8,128)(2,1)S(1)}, bf16[64,512]{1,0:T(8,128)(2,1)S(1)}, u32[]{:S(2)}, u32[]{:S(2)}) collective-permute-start(bf16[64,512]{1,0:T(8,128)(2,1)S(1)} %get-tuple-element.46.refs_0_), channel_id=1, source_target_pairs={{0,3},{1,2},{2,1},{3,0},{4,7},{5,6},{6,5},{7,4},{8,11},{9,10},{10,... | collective-permute-start | bytes 196616 | tf_op jit(solution)/shard_map/ppermute | solution.py:19
  29.8 7.2 %collective-permute-start.14 = (bf16[64,512]{1,0:T(8,128)(2,1)S(1)}, bf16[64,512]{1,0:T(8,128)(2,1)S(1)}, u32[]{:S(2)}, u32[]{:S(2)}) collective-permute-start(bf16[64,512]{1,0:T(8,128)(2,1)S(1)} %get-tuple-element.46.refs_0_), channel_id=1, source_target_pairs={{0,2},{1,3},{2,0},{3,1},{4,6},{5,7},{6,4},{7,5},{8,10},{9,11},{10,... | collective-permute-start | bytes 196616 | tf_op jit(solution)/shard_map/ppermute | solution.py:19
  32.3 4.8 %collective-permute-start.13 = (bf16[64,512]{1,0:T(8,128)(2,1)S(1)}, bf16[64,512]{1,0:T(8,128)(2,1)S(1)}, u32[]{:S(2)}, u32[]{:S(2)}) collective-permute-start(bf16[64,512]{1,0:T(8,128)(2,1)S(1)} %get-tuple-element.46.refs_0_), channel_id=1, source_target_pairs={{0,1},{1,0},{2,3},{3,2},{4,5},{5,4},{6,7},{7,6},{8,9},{9,8},{10,11... | collective-permute-start | bytes 196616 | tf_op jit(solution)/shard_map/ppermute | solution.py:19
  33.5 5.9 %collective-permute-start.19 = (bf16[64,512]{1,0:T(8,128)(2,1)S(1)}, bf16[64,512]{1,0:T(8,128)(2,1)S(1)}, u32[]{:S(2)}, u32[]{:S(2)}) collective-permute-start(bf16[64,512]{1,0:T(8,128)(2,1)S(1)} %get-tuple-element.53), channel_id=1, source_target_pairs={{0,3},{1,2},{2,1},{3,0},{4,7},{5,6},{6,5},{7,4},{8,11},{9,10},{10,... | collective-permute-start | bytes 196616 | tf_op jit(solution)/shard_map/ppermute | solution.py:19
  34.5 5.0 %collective-permute-start.20 = (bf16[64,512]{1,0:T(8,128)(2,1)S(1)}, bf16[64,512]{1,0:T(8,128)(2,1)S(1)}, u32[]{:S(2)}, u32[]{:S(2)}) collective-permute-start(bf16[64,512]{1,0:T(8,128)(2,1)S(1)} %get-tuple-element.54), channel_id=1, source_target_pairs={{0,1},{1,0},{2,3},{3,2},{4,5},{5,4},{6,7},{7,6},{8,9},{9,8},{10,11... | collective-permute-start | bytes 196616 | tf_op jit(solution)/shard_map/ppermute | solution.py:19
  35.2 4.4 %collective-permute-start.21 = (bf16[64,512]{1,0:T(8,128)(2,1)S(1)}, bf16[64,512]{1,0:T(8,128)(2,1)S(1)}, u32[]{:S(2)}, u32[]{:S(2)}) collective-permute-start(bf16[64,512]{1,0:T(8,128)(2,1)S(1)} %get-tuple-element.55), channel_id=1, source_target_pairs={{0,2},{1,3},{2,0},{3,1},{4,6},{5,7},{6,4},{7,5},{8,10},{9,11},{10,... | collective-permute-start | bytes 196616 | tf_op jit(solution)/shard_map/ppermute | solution.py:19
  37.8 4.4 %collective-permute-start.17 = (bf16[64,512]{1,0:T(8,128)(2,1)S(1)}, bf16[64,512]{1,0:T(8,128)(2,1)S(1)}, u32[]{:S(2)}, u32[]{:S(2)}) collective-permute-start(bf16[64,512]{1,0:T(8,128)(2,1)S(1)} %get-tuple-element.50), channel_id=1, source_target_pairs={{0,16},{8,24},{16,0},{24,8},{1,17},{9,25},{17,1},{25,9},{2,18},{10... | collective-permute-start | bytes 196616 | tf_op jit(solution)/shard_map/ppermute | solution.py:19
  39.6 4.9 %collective-permute-start.22 = (bf16[32,512]{1,0:T(8,128)(2,1)S(1)}, bf16[32,512]{1,0:T(8,128)(2,1)S(1)}, u32[]{:S(2)}, u32[]{:S(2)}) collective-permute-start(bf16[32,512]{1,0:T(8,128)(2,1)S(1)} %get-tuple-element.57), channel_id=1, source_target_pairs={{0,4},{1,5},{2,6},{3,7},{4,0},{5,1},{6,2},{7,3},{8,12},{9,13},{10,... | collective-permute-start | bytes 98312 | tf_op jit(solution)/shard_map/ppermute | solution.py:19
  42.2 2.2 %collective-permute-start.18 = (bf16[32,512]{1,0:T(8,128)(2,1)S(1)}, bf16[32,512]{1,0:T(8,128)(2,1)S(1)}, u32[]{:S(2)}, u32[]{:S(2)}) collective-permute-start(bf16[32,512]{1,0:T(8,128)(2,1)S(1)} %get-tuple-element.52), channel_id=1, source_target_pairs={{0,8},{8,0},{16,24},{24,16},{1,9},{9,1},{17,25},{25,17},{2,10},{10... | collective-permute-start | bytes 98312 | tf_op jit(solution)/shard_map/ppermute | solution.py:19
